TPU v7x, 512 devices: a whole 4x4x16 slice. The times are simulated.
512 devices in a mesh: cuts: 16 (over z), sx: 8 (over x, core), sy: 4 (over y).
Axes of the slice: x: 4, y: 4, z: 16, core: 2. Of those that a mesh axis runs over, the one named last changes fastest.
Arguments:
- starts: float32 [16, 3, 512, 2048], P('cuts', None, 'sx', 'sy'), may hold values from -2 to 2
- viscosity: float32 [512, 2048], P('sx', 'sy'), may hold values from 0.02 to 0.15
- turbine_x: int32 [64], replicated, may hold values from 0 to 511
- turbine_y: int32 [64], replicated, may hold values from 0 to 2047
- yaw_index: int32 [16, 64], replicated, may hold values from 0 to 6
Outputs:
- new_starts: float32 [16, 3, 512, 2048], P('cuts', None, 'sx', 'sy')
All inputs are finite; a program needn't handle non-finite values.
Results may differ from a plain program's by a relative error of at most 0.0001.
Values sent between devices are 32-bit elements; how exact they have to be, the bound alone decides.
No kernel may reach another device: no remote copies, remote signals or barrier semaphores. Data moves between devices by JAX's collectives and lax.ppermute only.
A program may use at most 64 MiB of HBM per device.

v0:
```python
import math

import jax
import jax.numpy as jnp
from jax import lax
from jax.sharding import PartitionSpec as P

FINE = 4
COARSE = 2
YAWS = 7


rotor_reach = 3
fine_terms = (0.3, 0.5, 0.2, 0.5)
coarse_terms = (0.15, 0.25, 0.1, 1.0)


def with_halo(x, sides, width):
    for axis, dim in sides:
        count, length = (lax.axis_size(axis), x.shape[dim])
        up = [(i, (i + 1) % count) for i in range(count - 1)]
        down = [(j, i) for i, j in up]
        last = lax.slice_in_dim(x, length - width, length, axis=dim)
        leading = lax.slice_in_dim(x, 0, width, axis=dim)
        before = lax.ppermute(last, axis, up)
        after = lax.ppermute(leading, axis, down)
        x = jnp.concatenate([before, x, after], axis=dim)
    return x


def passed_along(x, axis, by):
    count = lax.axis_size(axis)
    pairs = [(i, i + by) for i in range(count) if 0 <= i + by < count]
    return lax.ppermute(x, axis, pairs)


def centre(field):
    return field[1:-1, 1:-1]


def east_of(field):
    return field[2:, 1:-1]


def west_of(field):
    return field[:-2, 1:-1]


def north_of(field):
    return field[1:-1, 2:]


def south_of(field):
    return field[1:-1, :-2]


def laplace(field):
    return east_of(field) + west_of(field) + north_of(field) + south_of(field) - 4.0 * centre(field)


def advance(padded, nu_here, push_x, push_y, terms):
    carry_rate, steep_rate, couple_rate, thrust_rate = terms
    speed_x = padded[0]
    speed_y = padded[1]
    pressure = padded[2]
    here_x = centre(speed_x)
    here_y = centre(speed_y)
    here_p = centre(pressure)
    slope_xx = 0.5 * (east_of(speed_x) - west_of(speed_x))
    slope_yy = 0.5 * (north_of(speed_y) - south_of(speed_y))
    slope_yx = 0.5 * (east_of(speed_y) - west_of(speed_y))
    lifted = 1.0 + here_x
    drag = thrust_rate * lifted * jnp.abs(lifted) / (1.0 + jnp.abs(lifted))
    new_x = (
        here_x
        + nu_here * laplace(speed_x)
        - carry_rate * (here_x - west_of(speed_x))
        - steep_rate * here_x * slope_xx
        - couple_rate * 0.5 * (east_of(pressure) - west_of(pressure))
        - push_x * drag
    )
    new_y = (
        here_y
        + nu_here * laplace(speed_y)
        - carry_rate * (here_y - west_of(speed_y))
        - steep_rate * here_x * slope_yx
        - couple_rate * 0.5 * (north_of(pressure) - south_of(pressure))
        - push_y * drag
    )
    new_p = here_p + nu_here * laplace(pressure) - couple_rate * (slope_xx + slope_yy)
    return jnp.stack([new_x, new_y, new_p])


def rotor_fields(rows_at, cols_at, turbine_x, turbine_y, yaw_row, block):
    angle = (yaw_row.astype(jnp.float32) - 0.5 * (YAWS - 1)) * (math.pi / 18.0)
    cosine = jnp.cos(angle)
    sine = jnp.sin(angle)
    if block == 1:
        row_hit = (rows_at[None, :] == turbine_x[:, None]).astype(jnp.float32)
        col_hit = (jnp.abs(cols_at[None, :] - turbine_y[:, None]) <= rotor_reach).astype(
            jnp.float32
        )
    else:
        row_hit = (rows_at[None, :] == (turbine_x // 4)[:, None]).astype(jnp.float32) * 0.25
        col_hit = jnp.zeros((turbine_y.shape[0], cols_at.shape[0]), jnp.float32)
        for offset in range(4):
            col_hit = col_hit + (
                jnp.abs(4 * cols_at[None, :] + offset - turbine_y[:, None]) <= rotor_reach
            ).astype(jnp.float32)
        col_hit = col_hit * 0.25
    weight_x = cosine * cosine * cosine
    weight_y = cosine * cosine * sine
    push_x = jnp.einsum(
        "kh,kw->hw", row_hit, col_hit * weight_x[:, None], precision=lax.Precision.HIGHEST
    )
    push_y = jnp.einsum(
        "kh,kw->hw", row_hit, col_hit * weight_y[:, None], precision=lax.Precision.HIGHEST
    )
    return (push_x, push_y)


def restrict(field):
    leading = field.shape[:-2]
    height = field.shape[-2]
    breadth = field.shape[-1]
    return field.reshape(leading + (height // 4, 4, breadth // 4, 4)).mean(axis=(-3, -1))


def prolong(field):
    return jnp.repeat(jnp.repeat(field, 4, axis=-2), 4, axis=-1)


def shrink(field, margin):
    return field[..., margin : field.shape[-2] - margin, margin : field.shape[-1] - margin]


def coarse_advance(state, coarse_nu, push_x, push_y, inside):
    stacked = jnp.concatenate([state, coarse_nu[None]], 0)
    padded = with_halo(stacked, (("sx", 1), ("sy", 2)), COARSE)
    current = padded[:3]
    nu_pad = padded[3]
    for step in range(COARSE):
        current = advance(
            current,
            shrink(nu_pad, step + 1),
            shrink(push_x, step + 1),
            shrink(push_y, step + 1),
            coarse_terms,
        ) * shrink(inside, step + 1)
    return current


def on_device(starts, viscosity, turbine_x, turbine_y, yaw_index):
    start = starts[0]
    rows = start.shape[1]
    cols = start.shape[2]
    total_rows = rows * lax.axis_size("sx")
    total_cols = cols * lax.axis_size("sy")
    slice_at = lax.axis_index("cuts")
    row_base = lax.axis_index("sx") * rows
    col_base = lax.axis_index("sy") * cols
    yaw_row = lax.dynamic_index_in_dim(yaw_index, slice_at, 0, keepdims=False)
    rows_at = row_base + lax.iota(jnp.int32, rows)
    cols_at = col_base + lax.iota(jnp.int32, cols)
    push_x, push_y = rotor_fields(rows_at, cols_at, turbine_x, turbine_y, yaw_row, 1)
    state = start
    for step in range(FINE):
        padded = with_halo(state, (("sx", 1), ("sy", 2)), 1)
        state = advance(padded, viscosity, push_x, push_y, fine_terms)
    coarse_rows = rows // 4
    coarse_cols = cols // 4
    crow_at = (
        lax.axis_index("sx") * coarse_rows - COARSE + lax.iota(jnp.int32, coarse_rows + 2 * COARSE)
    )
    ccol_at = (
        lax.axis_index("sy") * coarse_cols - COARSE + lax.iota(jnp.int32, coarse_cols + 2 * COARSE)
    )
    coarse_inside = (
        ((crow_at >= 0) & (crow_at < total_rows // 4))[:, None]
        & ((ccol_at >= 0) & (ccol_at < total_cols // 4))[None, :]
    ).astype(jnp.float32)
    coarse_nu = restrict(viscosity) * 0.5
    own_x, own_y = rotor_fields(crow_at, ccol_at, turbine_x, turbine_y, yaw_row, 4)
    rough = restrict(start)
    guess = coarse_advance(rough, coarse_nu, own_x, own_y, coarse_inside)
    fine_part = state - prolong(guess)
    defect = restrict(state) - guess
    count = lax.axis_size("cuts")
    empty = jnp.zeros_like(rough)

    def turn(level, carry):
        handed, moved = carry
        incoming = passed_along(handed, "cuts", 1)
        current = jnp.where(slice_at == 0, rough, incoming)
        moved = coarse_advance(current, coarse_nu, own_x, own_y, coarse_inside)
        return (moved + defect, moved)

    handed, moved = lax.fori_loop(0, count, turn, (empty, empty))
    return (fine_part + prolong(moved))[None]


def solution(mesh):
    in_specs = (P("cuts", None, "sx", "sy"), P("sx", "sy"), P(), P(), P())
    out_specs = P("cuts", None, "sx", "sy")
    return jax.shard_map(
        on_device, mesh=mesh, in_specs=in_specs, out_specs=out_specs, check_vma=False
    )
```

profile of v0, /device:TPU:412, one launch (start us, length us, event | category | flops | bytes accessed | tf_op | source)
XLA Modules:
  0.0 515.0 jit_solution(17062695688371885450)
XLA Ops:
  0.0 15.3 %reshape_squeeze.3 = f32[3,16,4,128,4]{4,3,2,1,0:T(8,128)} reshape(f32[1,3,64,512]{3,2,1,0:T(8,128)} %param.7) | data formatting | bytes 786432 | tf_op jit(solution)/shard_map/reshape;squeeze | solution.py:126
  15.3 5.5 %reduce_sum.27 = f32[3,16,128]{2,1,0:T(8,128)S(1)} reduce(f32[3,16,4,128,4]{4,3,2,1,0:T(8,128)} %reshape_squeeze.3, f32[]{:T(128)} %constant.142.clone.1), dimensions={2,4}, to_apply=%region_0.1 | reduce | flops 92160 | bytes 417796 | tf_op jit(solution)/shard_map/reduce_sum | solution.py:126
  20.8 5.7 %reshape.164 = f32[16,4,128,4]{3,2,1,0:T(8,128)} reshape(f32[64,512]{1,0:T(8,128)S(1)} %copy-done) | data formatting | bytes 262144 | tf_op jit(solution)/shard_map/reshape | solution.py:126
  43.9 4.5 collective-permute-start.24
  51.7 4.9 collective-permute-start.8
  68.3 5.0 collective-permute-start.12
  85.0 5.0 collective-permute-start.16
  102.5 5.2 %collective-permute-start.20 = (f32[3,66,1]{2,1,0:T(8,128)S(1)}, f32[3,66,1]{2,1,0:T(8,128)S(1)}, u32[]{:S(2)}, u32[]{:S(2)}) collective-permute-start(f32[3,66,1]{2,1,0:T(8,128)S(1)} %get-tuple-element.215), channel_id=1, source_target_pairs={{1,0},{2,1},{3,2},{5,4},{6,5},{7,6},{9,8},{10,9},{11,10},{13,12},{... | collective-permute-start | bytes 2384 | tf_op jit(solution)/shard_map/ppermute | solution.py:26
  111.0 5.7 %stack.144 = f32[1,16,4,128,4]{4,3,2,1,0:T(8,128)} reshape(f32[64,512]{1,0:T(8,128)S(1)} %fusion.25) | data formatting | bytes 262144 | tf_op jit(solution)/shard_map/stack | solution.py:91
  120.0 5.7 %stack.145 = f32[1,16,4,128,4]{4,3,2,1,0:T(8,128)} reshape(f32[64,512]{1,0:T(8,128)S(1)} %get-tuple-element.194) | data formatting | bytes 262144 | tf_op jit(solution)/shard_map/stack | solution.py:91
  128.6 5.7 %stack.146 = f32[1,16,4,128,4]{4,3,2,1,0:T(8,128)} reshape(f32[64,512]{1,0:T(8,128)S(1)} %get-tuple-element.195) | data formatting | bytes 262144 | tf_op jit(solution)/shard_map/stack | solution.py:91
  137.2 375.2 %while.15 = (s32[]{:T(128)}, f32[3,16,128]{2,1,0:T(8,128)S(1)}, f32[3,16,128]{2,1,0:T(8,128)}, pred[]{:T(512)}, f32[3,16,128]{2,1,0:T(8,128)S(1)}, /*index=5*/f3...) while((s32[]{:T(128)}, f32[3,16,128]{2,1,0:T(8,128)S(1)}, ...), condition=%wide.region_4.5_spmd.clone, body=%wide.region_3.4_spmd.clone.sunk | while | flops 415551 | bytes 1290984 | solution.py:198
  151.1 4.4 collective-permute-start.3
  157.2 4.3 collective-permute-done.4
  164.7 5.0 collective-permute-done
  182.3 4.3 collective-permute-done.4
  189.7 5.0 collective-permute-done
  207.1 4.3 collective-permute-done.4
  214.5 5.0 collective-permute-done
  230.1 4.3 collective-permute-done.4
  237.6 5.0 collective-permute-done
  260.6 5.0 collective-permute-done
  283.7 5.0 collective-permute-done
  306.7 5.0 collective-permute-done
  329.8 5.0 collective-permute-done
  352.8 5.0 collective-permute-done
  375.9 5.0 collective-permute-done
  399.0 5.0 collective-permute-done
  422.0 5.0 collective-permute-done
  445.1 5.0 collective-permute-done
  468.1 5.0 collective-permute-done
  491.2 5.0 collective-permute-done
  (509 shorter events, 347.9 us)
Async XLA Ops:
  29.1 13.3 %collective-permute-start.21 = (f32[4,2,128]{2,1,0:T(2,128)S(1)}, f32[4,2,128]{2,1,0:T(2,128)S(1)}, u32[]{:S(2)}, u32[]{:S(2)}) collective-permute-start(f32[4,2,128]{2,1,0:T(2,128)S(1)} %get-tuple-element.243), channel_id=1, source_target_pairs={{0,4},{4,8},{8,12},{12,16},{16,20},{20,24},{24,28},{1,5},{5,9},{9,... | collective-permute-start | bytes 12296 | tf_op jit(solution)/shard_map/ppermute | solution.py:25
  31.1 11.4 %collective-permute-start.22 = (f32[4,2,128]{2,1,0:T(2,128)S(1)}, f32[4,2,128]{2,1,0:T(2,128)S(1)}, u32[]{:S(2)}, u32[]{:S(2)}) collective-permute-start(f32[4,2,128]{2,1,0:T(2,128)S(1)} %get-tuple-element.244), channel_id=1, source_target_pairs={{4,0},{8,4},{12,8},{16,12},{20,16},{24,20},{28,24},{5,1},{9,5},{13... | collective-permute-start | bytes 12296 | tf_op jit(solution)/shard_map/ppermute | solution.py:26
  34.7 15.5 %collective-permute-start.5 = (f32[3,1,512]{2,1,0:T(1,128)S(1)}, f32[3,1,512]{2,1,0:T(1,128)S(1)}, u32[]{:S(2)}, u32[]{:S(2)}) collective-permute-start(f32[3,1,512]{2,1,0:T(1,128)S(1)} %get-tuple-element.228), channel_id=1, source_target_pairs={{0,4},{4,8},{8,12},{12,16},{16,20},{20,24},{24,28},{1,5},{5,9},{9,... | collective-permute-start | bytes 18440 | tf_op jit(solution)/shard_map/ppermute | solution.py:25
  36.7 13.6 %collective-permute-start.6 = (f32[3,1,512]{2,1,0:T(1,128)S(1)}, f32[3,1,512]{2,1,0:T(1,128)S(1)}, u32[]{:S(2)}, u32[]{:S(2)}) collective-permute-start(f32[3,1,512]{2,1,0:T(1,128)S(1)} %get-tuple-element.229), channel_id=1, source_target_pairs={{4,0},{8,4},{12,8},{16,12},{20,16},{24,20},{28,24},{5,1},{9,5},{13... | collective-permute-start | bytes 18440 | tf_op jit(solution)/shard_map/ppermute | solution.py:26
  42.6 6.1 %collective-permute-start.23 = (f32[4,20,2]{2,1,0:T(8,128)S(1)}, f32[4,20,2]{2,1,0:T(8,128)S(1)}, u32[]{:S(2)}, u32[]{:S(2)}) collective-permute-start(f32[4,20,2]{2,1,0:T(8,128)S(1)} %get-tuple-element.241), channel_id=1, source_target_pairs={{0,1},{1,2},{2,3},{4,5},{5,6},{6,7},{8,9},{9,10},{10,11},{12,13},{... | collective-permute-start | bytes 1928 | tf_op jit(solution)/shard_map/ppermute | solution.py:25
  43.9 6.3 %collective-permute-start.24 = (f32[4,20,2]{2,1,0:T(8,128)S(1)}, f32[4,20,2]{2,1,0:T(8,128)S(1)}, u32[]{:S(2)}, u32[]{:S(2)}) collective-permute-start(f32[4,20,2]{2,1,0:T(8,128)S(1)} %get-tuple-element.242), channel_id=1, source_target_pairs={{1,0},{2,1},{3,2},{5,4},{6,5},{7,6},{9,8},{10,9},{11,10},{13,12},{... | collective-permute-start | bytes 1928 | tf_op jit(solution)/shard_map/ppermute | solution.py:26
  50.4 7.0 %collective-permute-start.7 = (f32[3,66,1]{2,1,0:T(8,128)S(1)}, f32[3,66,1]{2,1,0:T(8,128)S(1)}, u32[]{:S(2)}, u32[]{:S(2)}) collective-permute-start(f32[3,66,1]{2,1,0:T(8,128)S(1)} %get-tuple-element.220), channel_id=1, source_target_pairs={{0,1},{1,2},{2,3},{4,5},{5,6},{6,7},{8,9},{9,10},{10,11},{12,13},{... | collective-permute-start | bytes 2384 | tf_op jit(solution)/shard_map/ppermute | solution.py:25
  51.7 7.2 %collective-permute-start.8 = (f32[3,66,1]{2,1,0:T(8,128)S(1)}, f32[3,66,1]{2,1,0:T(8,128)S(1)}, u32[]{:S(2)}, u32[]{:S(2)}) collective-permute-start(f32[3,66,1]{2,1,0:T(8,128)S(1)} %get-tuple-element.221), channel_id=1, source_target_pairs={{1,0},{2,1},{3,2},{5,4},{6,5},{7,6},{9,8},{10,9},{11,10},{13,12},{... | collective-permute-start | bytes 2384 | tf_op jit(solution)/shard_map/ppermute | solution.py:26
  67.0 7.0 %collective-permute-start.11 = (f32[3,66,1]{2,1,0:T(8,128)S(1)}, f32[3,66,1]{2,1,0:T(8,128)S(1)}, u32[]{:S(2)}, u32[]{:S(2)}) collective-permute-start(f32[3,66,1]{2,1,0:T(8,128)S(1)} %get-tuple-element.218), channel_id=1, source_target_pairs={{0,1},{1,2},{2,3},{4,5},{5,6},{6,7},{8,9},{9,10},{10,11},{12,13},{... | collective-permute-start | bytes 2384 | tf_op jit(solution)/shard_map/ppermute | solution.py:25
  68.3 7.3 %collective-permute-start.12 = (f32[3,66,1]{2,1,0:T(8,128)S(1)}, f32[3,66,1]{2,1,0:T(8,128)S(1)}, u32[]{:S(2)}, u32[]{:S(2)}) collective-permute-start(f32[3,66,1]{2,1,0:T(8,128)S(1)} %get-tuple-element.219), channel_id=1, source_target_pairs={{1,0},{2,1},{3,2},{5,4},{6,5},{7,6},{9,8},{10,9},{11,10},{13,12},{... | collective-permute-start | bytes 2384 | tf_op jit(solution)/shard_map/ppermute | solution.py:26
  83.7 7.7 %collective-permute-start.15 = (f32[3,66,1]{2,1,0:T(8,128)S(1)}, f32[3,66,1]{2,1,0:T(8,128)S(1)}, u32[]{:S(2)}, u32[]{:S(2)}) collective-permute-start(f32[3,66,1]{2,1,0:T(8,128)S(1)} %get-tuple-element.216), channel_id=1, source_target_pairs={{0,1},{1,2},{2,3},{4,5},{5,6},{6,7},{8,9},{9,10},{10,11},{12,13},{... | collective-permute-start | bytes 2384 | tf_op jit(solution)/shard_map/ppermute | solution.py:25
  85.0 8.1 %collective-permute-start.16 = (f32[3,66,1]{2,1,0:T(8,128)S(1)}, f32[3,66,1]{2,1,0:T(8,128)S(1)}, u32[]{:S(2)}, u32[]{:S(2)}) collective-permute-start(f32[3,66,1]{2,1,0:T(8,128)S(1)} %get-tuple-element.217), channel_id=1, source_target_pairs={{1,0},{2,1},{3,2},{5,4},{6,5},{7,6},{9,8},{10,9},{11,10},{13,12},{... | collective-permute-start | bytes 2384 | tf_op jit(solution)/shard_map/ppermute | solution.py:26
  101.2 8.0 %collective-permute-start.19 = (f32[3,66,1]{2,1,0:T(8,128)S(1)}, f32[3,66,1]{2,1,0:T(8,128)S(1)}, u32[]{:S(2)}, u32[]{:S(2)}) collective-permute-start(f32[3,66,1]{2,1,0:T(8,128)S(1)} %get-tuple-element.214), channel_id=1, source_target_pairs={{0,1},{1,2},{2,3},{4,5},{5,6},{6,7},{8,9},{9,10},{10,11},{12,13},{... | collective-permute-start | bytes 2384 | tf_op jit(solution)/shard_map/ppermute | solution.py:25
  102.5 7.9 %collective-permute-start.20 = (f32[3,66,1]{2,1,0:T(8,128)S(1)}, f32[3,66,1]{2,1,0:T(8,128)S(1)}, u32[]{:S(2)}, u32[]{:S(2)}) collective-permute-start(f32[3,66,1]{2,1,0:T(8,128)S(1)} %get-tuple-element.215), channel_id=1, source_target_pairs={{1,0},{2,1},{3,2},{5,4},{6,5},{7,6},{9,8},{10,9},{11,10},{13,12},{... | collective-permute-start | bytes 2384 | tf_op jit(solution)/shard_map/ppermute | solution.py:26
  137.2 6.9 %collective-permute-start = (f32[3,16,128]{2,1,0:T(8,128)S(1)}, f32[3,16,128]{2,1,0:T(8,128)S(1)}, u32[]{:S(2)}, u32[]{:S(2)}) collective-permute-start(f32[3,16,128]{2,1,0:T(8,128)S(1)} %broadcast_select_fusion.4), channel_id=1, source_target_pairs={{0,32},{32,64},{64,96},{96,128},{128,160},{160,192},{192,224},{224... | collective-permute-start | bytes 73736 | tf_op jit(solution)/shard_map/while/body/eval_jaxpr/ppermute | solution.py:34
  151.1 6.1 %collective-permute-start.3 = (f32[4,20,2]{2,1,0:T(8,128)S(1)}, f32[4,20,2]{2,1,0:T(8,128)S(1)}, u32[]{:S(2)}, u32[]{:S(2)}) collective-permute-start(f32[4,20,2]{2,1,0:T(8,128)S(1)} %get-tuple-element.331), channel_id=1, source_target_pairs={{1,0},{2,1},{3,2},{5,4},{6,5},{7,6},{9,8},{10,9},{11,10},{13,12},{... | collective-permute-start | bytes 1928 | tf_op jit(solution)/shard_map/while/body/eval_jaxpr/ppermute | solution.py:26
  155.5 6.0 %collective-permute-start.4 = (f32[4,20,2]{2,1,0:T(8,128)S(1)}, f32[4,20,2]{2,1,0:T(8,128)S(1)}, u32[]{:S(2)}, u32[]{:S(2)}) collective-permute-start(f32[4,20,2]{2,1,0:T(8,128)S(1)} %get-tuple-element.332), channel_id=1, source_target_pairs={{0,1},{1,2},{2,3},{4,5},{5,6},{6,7},{8,9},{9,10},{10,11},{12,13},{... | collective-permute-start | bytes 1928 | tf_op jit(solution)/shard_map/while/body/eval_jaxpr/ppermute | solution.py:25
  162.7 6.9 %collective-permute-start = (f32[3,16,128]{2,1,0:T(8,128)S(1)}, f32[3,16,128]{2,1,0:T(8,128)S(1)}, u32[]{:S(2)}, u32[]{:S(2)}) collective-permute-start(f32[3,16,128]{2,1,0:T(8,128)S(1)} %broadcast_select_fusion.4), channel_id=1, source_target_pairs={{0,32},{32,64},{64,96},{96,128},{128,160},{160,192},{192,224},{224... | collective-permute-start | bytes 73736 | tf_op jit(solution)/shard_map/while/body/eval_jaxpr/ppermute | solution.py:34
  187.8 6.9 %collective-permute-start = (f32[3,16,128]{2,1,0:T(8,128)S(1)}, f32[3,16,128]{2,1,0:T(8,128)S(1)}, u32[]{:S(2)}, u32[]{:S(2)}) collective-permute-start(f32[3,16,128]{2,1,0:T(8,128)S(1)} %broadcast_select_fusion.4), channel_id=1, source_target_pairs={{0,32},{32,64},{64,96},{96,128},{128,160},{160,192},{192,224},{224... | collective-permute-start | bytes 73736 | tf_op jit(solution)/shard_map/while/body/eval_jaxpr/ppermute | solution.py:34
  212.6 6.9 %collective-permute-start = (f32[3,16,128]{2,1,0:T(8,128)S(1)}, f32[3,16,128]{2,1,0:T(8,128)S(1)}, u32[]{:S(2)}, u32[]{:S(2)}) collective-permute-start(f32[3,16,128]{2,1,0:T(8,128)S(1)} %broadcast_select_fusion.4), channel_id=1, source_target_pairs={{0,32},{32,64},{64,96},{96,128},{128,160},{160,192},{192,224},{224... | collective-permute-start | bytes 73736 | tf_op jit(solution)/shard_map/while/body/eval_jaxpr/ppermute | solution.py:34
  235.6 6.9 %collective-permute-start = (f32[3,16,128]{2,1,0:T(8,128)S(1)}, f32[3,16,128]{2,1,0:T(8,128)S(1)}, u32[]{:S(2)}, u32[]{:S(2)}) collective-permute-start(f32[3,16,128]{2,1,0:T(8,128)S(1)} %broadcast_select_fusion.4), channel_id=1, source_target_pairs={{0,32},{32,64},{64,96},{96,128},{128,160},{160,192},{192,224},{224... | collective-permute-start | bytes 73736 | tf_op jit(solution)/shard_map/while/body/eval_jaxpr/ppermute | solution.py:34
  258.7 6.9 %collective-permute-start = (f32[3,16,128]{2,1,0:T(8,128)S(1)}, f32[3,16,128]{2,1,0:T(8,128)S(1)}, u32[]{:S(2)}, u32[]{:S(2)}) collective-permute-start(f32[3,16,128]{2,1,0:T(8,128)S(1)} %broadcast_select_fusion.4), channel_id=1, source_target_pairs={{0,32},{32,64},{64,96},{96,128},{128,160},{160,192},{192,224},{224... | collective-permute-start | bytes 73736 | tf_op jit(solution)/shard_map/while/body/eval_jaxpr/ppermute | solution.py:34
  281.8 6.9 %collective-permute-start = (f32[3,16,128]{2,1,0:T(8,128)S(1)}, f32[3,16,128]{2,1,0:T(8,128)S(1)}, u32[]{:S(2)}, u32[]{:S(2)}) collective-permute-start(f32[3,16,128]{2,1,0:T(8,128)S(1)} %broadcast_select_fusion.4), channel_id=1, source_target_pairs={{0,32},{32,64},{64,96},{96,128},{128,160},{160,192},{192,224},{224... | collective-permute-start | bytes 73736 | tf_op jit(solution)/shard_map/while/body/eval_jaxpr/ppermute | solution.py:34
  304.8 6.9 %collective-permute-start = (f32[3,16,128]{2,1,0:T(8,128)S(1)}, f32[3,16,128]{2,1,0:T(8,128)S(1)}, u32[]{:S(2)}, u32[]{:S(2)}) collective-permute-start(f32[3,16,128]{2,1,0:T(8,128)S(1)} %broadcast_select_fusion.4), channel_id=1, source_target_pairs={{0,32},{32,64},{64,96},{96,128},{128,160},{160,192},{192,224},{224... | collective-permute-start | bytes 73736 | tf_op jit(solution)/shard_map/while/body/eval_jaxpr/ppermute | solution.py:34
  327.9 6.9 %collective-permute-start = (f32[3,16,128]{2,1,0:T(8,128)S(1)}, f32[3,16,128]{2,1,0:T(8,128)S(1)}, u32[]{:S(2)}, u32[]{:S(2)}) collective-permute-start(f32[3,16,128]{2,1,0:T(8,128)S(1)} %broadcast_select_fusion.4), channel_id=1, source_target_pairs={{0,32},{32,64},{64,96},{96,128},{128,160},{160,192},{192,224},{224... | collective-permute-start | bytes 73736 | tf_op jit(solution)/shard_map/while/body/eval_jaxpr/ppermute | solution.py:34
  350.9 6.9 %collective-permute-start = (f32[3,16,128]{2,1,0:T(8,128)S(1)}, f32[3,16,128]{2,1,0:T(8,128)S(1)}, u32[]{:S(2)}, u32[]{:S(2)}) collective-permute-start(f32[3,16,128]{2,1,0:T(8,128)S(1)} %broadcast_select_fusion.4), channel_id=1, source_target_pairs={{0,32},{32,64},{64,96},{96,128},{128,160},{160,192},{192,224},{224... | collective-permute-start | bytes 73736 | tf_op jit(solution)/shard_map/while/body/eval_jaxpr/ppermute | solution.py:34
  374.0 6.9 %collective-permute-start = (f32[3,16,128]{2,1,0:T(8,128)S(1)}, f32[3,16,128]{2,1,0:T(8,128)S(1)}, u32[]{:S(2)}, u32[]{:S(2)}) collective-permute-start(f32[3,16,128]{2,1,0:T(8,128)S(1)} %broadcast_select_fusion.4), channel_id=1, source_target_pairs={{0,32},{32,64},{64,96},{96,128},{128,160},{160,192},{192,224},{224... | collective-permute-start | bytes 73736 | tf_op jit(solution)/shard_map/while/body/eval_jaxpr/ppermute | solution.py:34
  397.0 6.9 %collective-permute-start = (f32[3,16,128]{2,1,0:T(8,128)S(1)}, f32[3,16,128]{2,1,0:T(8,128)S(1)}, u32[]{:S(2)}, u32[]{:S(2)}) collective-permute-start(f32[3,16,128]{2,1,0:T(8,128)S(1)} %broadcast_select_fusion.4), channel_id=1, source_target_pairs={{0,32},{32,64},{64,96},{96,128},{128,160},{160,192},{192,224},{224... | collective-permute-start | bytes 73736 | tf_op jit(solution)/shard_map/while/body/eval_jaxpr/ppermute | solution.py:34
  420.1 6.9 %collective-permute-start = (f32[3,16,128]{2,1,0:T(8,128)S(1)}, f32[3,16,128]{2,1,0:T(8,128)S(1)}, u32[]{:S(2)}, u32[]{:S(2)}) collective-permute-start(f32[3,16,128]{2,1,0:T(8,128)S(1)} %broadcast_select_fusion.4), channel_id=1, source_target_pairs={{0,32},{32,64},{64,96},{96,128},{128,160},{160,192},{192,224},{224... | collective-permute-start | bytes 73736 | tf_op jit(solution)/shard_map/while/body/eval_jaxpr/ppermute | solution.py:34
  443.2 6.9 %collective-permute-start = (f32[3,16,128]{2,1,0:T(8,128)S(1)}, f32[3,16,128]{2,1,0:T(8,128)S(1)}, u32[]{:S(2)}, u32[]{:S(2)}) collective-permute-start(f32[3,16,128]{2,1,0:T(8,128)S(1)} %broadcast_select_fusion.4), channel_id=1, source_target_pairs={{0,32},{32,64},{64,96},{96,128},{128,160},{160,192},{192,224},{224... | collective-permute-start | bytes 73736 | tf_op jit(solution)/shard_map/while/body/eval_jaxpr/ppermute | solution.py:34
  466.2 6.9 %collective-permute-start = (f32[3,16,128]{2,1,0:T(8,128)S(1)}, f32[3,16,128]{2,1,0:T(8,128)S(1)}, u32[]{:S(2)}, u32[]{:S(2)}) collective-permute-start(f32[3,16,128]{2,1,0:T(8,128)S(1)} %broadcast_select_fusion.4), channel_id=1, source_target_pairs={{0,32},{32,64},{64,96},{96,128},{128,160},{160,192},{192,224},{224... | collective-permute-start | bytes 73736 | tf_op jit(solution)/shard_map/while/body/eval_jaxpr/ppermute | solution.py:34
  489.3 6.9 %collective-permute-start = (f32[3,16,128]{2,1,0:T(8,128)S(1)}, f32[3,16,128]{2,1,0:T(8,128)S(1)}, u32[]{:S(2)}, u32[]{:S(2)}) collective-permute-start(f32[3,16,128]{2,1,0:T(8,128)S(1)} %broadcast_select_fusion.4), channel_id=1, source_target_pairs={{0,32},{32,64},{64,96},{96,128},{128,160},{160,192},{192,224},{224... | collective-permute-start | bytes 73736 | tf_op jit(solution)/shard_map/while/body/eval_jaxpr/ppermute | solution.py:34
  (72 other events, 386.2 us)
where the time goes:
time: 520 us; the launch traced here: 515 us
  starting transfers between devices  216 us (42%)
  waiting for transfers between devices  208 us (40%)
  local copies, waits for them, and re-layouts  52.7 us (10%)
  other arithmetic  34.5 us (7%)
    ppermute x42, waiting for transfers between devices, with_halo(): before = lax.ppermute(last, axis, up)  115 us
    ppermute x42, starting transfers between devices, with_halo(): after = lax.ppermute(leading, axis, down)  108 us
    ppermute x16, waiting for transfers between devices, passed_along(): return lax.ppermute(x, axis, pairs)  79 us
    ppermute x42, starting transfers between devices, with_halo(): before = lax.ppermute(last, axis, up)  76.1 us
    ppermute x16, starting transfers between devices, passed_along(): return lax.ppermute(x, axis, pairs)  31.6 us
    another operation x6, local copies, waits for them, and re-layouts, advance(): return jnp.stack([new_x, new_y, new_p])  25.6 us
    another operation x1, local copies, waits for them, and re-layouts, restrict(): field.reshape(leading + (height // 4, 4, breadth // 4, 4))  15.3 us
    ppermute x42, waiting for transfers between devices, with_halo(): after = lax.ppermute(leading, axis, down)  14.5 us
  transfers between devices with their start and end apart: 100, of which 76 were waited for; matrix products, arithmetic and copies ran while one was open for 1% of the time, Pallas kernels for 0%

commit v1 on v0

v1 whole, which is shorter than its diff:
```python
import math

import jax
import jax.numpy as jnp
import numpy as np
from jax import lax
from jax.experimental import pallas as pl
from jax.experimental.pallas import tpu as pltpu
from jax.sharding import PartitionSpec as P

YAWS = 7
CUTS = 16
REACH = 3
FINE_TERMS = (0.3, 0.5, 0.2)
FINE_THRUST = 0.5
COARSE_TERMS = (0.15, 0.25, 0.1)
COARSE_THRUST = 1.0
EXACT = lax.Precision.HIGHEST
F32 = jnp.float32

ROWS, COLS = 64, 512
CROWS, CCOLS = 16, 128
REACHED = 2 * (CUTS - 1)
EXT = 80
PLANES = 46
ANGLES = [(k - 0.5 * (YAWS - 1)) * (math.pi / 18.0) for k in range(YAWS)]
WEIGHT_X = [float(np.float32(math.cos(t) ** 3)) for t in ANGLES]
WEIGHT_Y = [float(np.float32(math.cos(t) ** 2 * math.sin(t))) for t in ANGLES]

_CLASS = [
    (0, 80, 32, list(range(9)) + [45]),
    (8, 64, 32, list(range(9, 21))),
    (16, 48, 16, list(range(21, 33))),
    (24, 32, 8, list(range(33, 45))),
]
GROUPS = []
_at = 0
for _first, _count, _width, _members in _CLASS:
    _per = 128 // _width
    for _i in range(0, len(_members), _per):
        GROUPS.append((_at, _first, _count, _width, _members[_i : _i + _per]))
        _at += _count
YROWS = _at
S1_ROWS = 11 * 48 + 12 * 8 + 16
S2_ROWS = 9 * 16 + 12 * 8 + 16


def lanes(shape):
    return lax.broadcasted_iota(jnp.int32, shape, len(shape) - 1)


def sublanes(shape):
    return lax.broadcasted_iota(jnp.int32, shape, len(shape) - 2)


def advance(src, dst, nu, fx, fy, mask, row, count, tiles, wanted, terms, post=None):
    carry, steep, couple = terms
    lane = lanes((count, 128))
    low, high = lane == 0, lane == 127
    here = pl.ds(row, count)
    east = pl.ds(row + 1, count)
    west = pl.ds(row - 1, count)
    mid = [[src[f, c, here, :] for c in range(tiles)] for f in range(3)]
    up = [[pltpu.roll(mid[f][c], 127, 1) for c in range(tiles)] for f in range(3)]
    down = [[pltpu.roll(mid[f][c], 1, 1) for c in range(tiles)] for f in range(3)]
    for c in wanted:
        after, before = (c + 1) % tiles, (c - 1) % tiles
        u, v, p = mid[0][c], mid[1][c], mid[2][c]
        un, vn, pn = [jnp.where(high, up[f][after], up[f][c]) for f in range(3)]
        us, vs, ps = [jnp.where(low, down[f][before], down[f][c]) for f in range(3)]
        ue, ve, pe = [src[f, c, east, :] for f in range(3)]
        uw, vw, pw = [src[f, c, west, :] for f in range(3)]
        nu_here = nu(c, here)
        du = ue - uw
        steeper = (0.5 * steep) * u
        lifted = 1.0 + u
        size = jnp.abs(lifted)
        drag = lifted * size / (1.0 + size)
        new_u = (
            u
            + nu_here * ((ue + uw) + (un + us) - 4.0 * u)
            - carry * (u - uw)
            - steeper * du
            - (0.5 * couple) * (pe - pw)
            - fx(c, here) * drag
        )
        new_v = (
            v
            + nu_here * ((ve + vw) + (vn + vs) - 4.0 * v)
            - carry * (v - vw)
            - steeper * (ve - vw)
            - (0.5 * couple) * (pn - ps)
            - fy(c, here) * drag
        )
        new_p = p + nu_here * ((pe + pw) + (pn + ps) - 4.0 * p) - (0.5 * couple) * (du + (vn - vs))
        new = [new_u, new_v, new_p]
        if mask is not None:
            inside = mask(c, here)
            new = [f * inside for f in new]
        for f in range(3):
            if post is None:
                dst[f, c, here, :] = new[f]
            else:
                post(f, c, here, new[f])


def yaw_weights(yaw):
    wx = jnp.zeros(yaw.shape, F32)
    wy = jnp.zeros(yaw.shape, F32)
    for k in range(YAWS):
        hit = yaw == k
        wx = jnp.where(hit, WEIGHT_X[k], wx)
        wy = jnp.where(hit, WEIGHT_Y[k], wy)
    return wx, wy


def edge_kernel(at, start, visc, send_a, send_b):
    even = lax.rem(at[1], 2) == 0
    for f in range(4):
        first = start[f, 0:8, :] if f < 3 else visc[0:8, :]
        last = start[f, 56:64, :] if f < 3 else visc[56:64, :]
        send_a[f] = jnp.where(even, last, first)
        send_b[f] = jnp.where(even, first, last)


def side_kernel(at, start, visc, got_a, got_b, send_a, send_b):
    even_x = lax.rem(at[1], 2) == 0
    even_y = lax.rem(at[2], 2) == 0
    for r0, count in ((0, 8), (8, 64), (72, 8)):
        lane = lanes((count, 128))
        left = jnp.zeros((count, 128), F32)
        right = jnp.zeros((count, 128), F32)
        for f in range(4):
            own = start.at[f] if f < 3 else visc
            if r0 == 8:
                a, b = own[:, 0:128], own[:, COLS - 128 : COLS]
            else:
                top = jnp.logical_xor(even_x, r0 == 0)
                a = jnp.where(top, got_a[f, :, 0:128], got_b[f, :, 0:128])
                b = jnp.where(top, got_a[f, :, COLS - 128 : COLS], got_b[f, :, COLS - 128 : COLS])
            mine = (lane >= 8 * f) & (lane < 8 * f + 8)
            left = jnp.where(mine, pltpu.roll(a, 8 * f, 1) if f else a, left)
            right = jnp.where(mine, pltpu.roll(b, 8 * f + 8, 1), right)
        send_a[r0 : r0 + count, :] = jnp.where(even_y, right, left)
        send_b[r0 : r0 + count, :] = jnp.where(even_y, left, right)


def push_kernel(at, tx, ty, yaw, fine_push, own_push):
    mine = lanes(yaw.shape) == at[0]
    own_yaw = jnp.sum(jnp.where(mine, yaw[...], 0), axis=1, keepdims=True)
    wx, wy = yaw_weights(own_yaw)
    row = at[1] * ROWS - 16 + sublanes((96, 64))
    row_hit = (row == tx[...]).astype(F32) * FINE_THRUST
    for c in range(5):
        lane = lanes((64, 128))
        if c < 4:
            col = at[2] * COLS + 128 * c + lane
        else:
            col = at[2] * COLS + jnp.where(lane < 64, COLS + lane, lane - 128)
        col_hit = (jnp.abs(col - ty[...]) <= REACH).astype(F32)
        fine_push[0, c] = jnp.dot(row_hit, col_hit * wx, precision=EXACT, preferred_element_type=F32)
        fine_push[1, c] = jnp.dot(row_hit, col_hit * wy, precision=EXACT, preferred_element_type=F32)
    row = at[1] * CROWS - 10 + sublanes((40, 64))
    row_hit = (row == tx[...] // 4).astype(F32) * (0.25 * COARSE_THRUST)
    for c in range(2):
        col_hit = coarse_cols(at[2], c, ty[...])
        own_push[0, c] = jnp.dot(row_hit, col_hit * wx, precision=EXACT, preferred_element_type=F32)
        own_push[1, c] = jnp.dot(row_hit, col_hit * wy, precision=EXACT, preferred_element_type=F32)


def coarse_cols(sy, c, ty):
    lane = lanes((64, 128))
    col = sy * CCOLS + (lane if c == 0 else jnp.where(lane < 64, CCOLS + lane, lane - 128))
    hit = jnp.zeros((64, 128), F32)
    for offset in range(4):
        hit = hit + (jnp.abs(4 * col + offset - ty) <= REACH).astype(F32)
    return hit * 0.25


def chain_push_kernel(at, tx, ty, yaw, push):
    row = at[1] * CROWS - 32 + sublanes((EXT, 64))
    row_hit = (row == tx[...] // 4).astype(F32) * (0.25 * COARSE_THRUST)
    cols = [coarse_cols(at[2], c, ty[...]) for c in range(2)]
    for n in range(1, CUTS):
        weights = yaw_weights(yaw[:, n : n + 1])
        for d in range(2):
            for c in range(2):
                push[n, d, c] = jnp.dot(row_hit, cols[c] * weights[d], precision=EXACT, preferred_element_type=F32)


def fine_kernel(at, start, visc, rows_a, rows_b, cols_a, cols_b, push, own_push, fine, guess, sent, coarse_nu,
                one, two, nu, mask, rough, rough_two, rough_mask):
    even_x = lax.rem(at[1], 2) == 0
    even_y = lax.rem(at[2], 2) == 0
    for f in range(4):
        own = start.at[f] if f < 3 else visc
        for c in range(4):
            dst = one.at[f, c] if f < 3 else nu.at[c]
            cut = slice(128 * c, 128 * c + 128)
            dst[16:80, :] = own[:, cut]
            dst[8:16, :] = jnp.where(even_x, rows_b[f, :, cut], rows_a[f, :, cut])
            dst[80:88, :] = jnp.where(even_x, rows_a[f, :, cut], rows_b[f, :, cut])
        after = jnp.where(even_y, cols_a[...], cols_b[...])
        before = jnp.where(even_y, cols_b[...], cols_a[...])
        lane = lanes((EXT, 128))
        after = pltpu.roll(after, (128 - 8 * f) % 128, 1) if f else after
        before = pltpu.roll(before, 120 - 8 * f, 1)
        dst = one.at[f, 4] if f < 3 else nu.at[4]
        dst[8:88, :] = jnp.where(lane < 8, after, jnp.where(lane >= 120, before, 0.0))
    lane, line = lanes((96, 128)), sublanes((96, 128))
    last_x, last_y = at[3] - 1, at[4] - 1
    in_rows = ((line >= 16) | (at[1] > 0)) & ((line < 80) | (at[1] < last_x))
    in_cols = ((lane >= 64) | (at[2] < last_y)) & ((lane < 64) | (at[2] > 0))
    for c in range(4):
        mask[c] = in_rows.astype(F32)
    mask[4] = (in_rows & in_cols).astype(F32)

    i, j = sublanes((COLS, 128)), lanes((COLS, 128))
    gather = (i // 4 == j).astype(F32) * 0.0625
    i, j = sublanes((128, 128)), lanes((128, 128))
    gather_side = (((i < 8) & (i // 4 == j)) | ((i >= 120) & ((i - 120) // 4 == j - 126))).astype(F32) * 0.0625

    def row_sum(ref, first, count):
        parts = [ref[pl.ds(first + k, count, stride=4), :] for k in range(4)]
        return (parts[0] + parts[1]) + (parts[2] + parts[3])

    body = [jnp.concatenate([row_sum(one.at[f, c] if f < 3 else nu.at[c], 0, 24) for c in range(4)], axis=1) for f in range(4)]
    side = [row_sum(one.at[f, 4] if f < 3 else nu.at[4], 0, 24) for f in range(4)]
    body = jnp.dot(jnp.concatenate(body, axis=0), gather, precision=EXACT, preferred_element_type=F32)
    side = jnp.dot(jnp.concatenate(side, axis=0), gather_side, precision=EXACT, preferred_element_type=F32)
    rough[...] = jnp.zeros(rough.shape, F32)
    rough_two[...] = jnp.zeros(rough_two.shape, F32)
    for f in range(4):
        scale = 0.5 if f == 3 else 1.0
        rough[f, 0, 6:30, :] = body[24 * f : 24 * f + 24, :] * scale
        rough[f, 1, 6:30, :] = side[24 * f : 24 * f + 24, :] * scale
    coarse_nu[...] = rough[3, 0, 10:26, :]
    lane, line = lanes((40, 128)), sublanes((40, 128))
    in_rows = ((line >= 10) | (at[1] > 0)) & ((line < 26) | (at[1] < last_x))
    in_cols = ((lane >= 64) | (at[2] < last_y)) & ((lane < 64) | (at[2] > 0))
    rough_mask[0] = in_rows.astype(F32)
    rough_mask[1] = (in_rows & in_cols).astype(F32)
    coarse = (
        lambda c, r: rough[3, c, r, :],
        lambda c, r: own_push[0, c, r, :],
        lambda c, r: own_push[1, c, r, :],
        lambda c, r: rough_mask[c, r, :],
    )
    for k in range(3):
        advance(rough, rough_two, *coarse, 9 + 8 * k, 8, 2, (0, 1), COARSE_TERMS)

    def keep_guess(f, c, r, value):
        guess[pl.ds(16 * f + r.start - 10, 8), :] = value

    for k in range(2):
        advance(rough_two, None, *coarse, 10 + 8 * k, 8, 2, (0,), COARSE_TERMS, post=keep_guess)

    finest = (
        lambda c, r: nu[c, r, :],
        lambda c, r: push[0, c, r, :],
        lambda c, r: push[1, c, r, :],
        lambda c, r: mask[c, r, :],
    )
    for src, dst, first, count, wanted in (
        (one, two, 12, 9, range(5)),
        (two, one, 12, 9, range(5)),
        (one, two, 12, 9, range(5)),
        (two, one, 16, 8, range(4)),
    ):
        for k in range(count):
            advance(src, dst, *finest, first + 8 * k, 8, 5, wanted, FINE_TERMS)
    for f in range(3):
        for c in range(4):
            fine[f, :, 128 * c : 128 * c + 128] = one[f, c, 16:80, :]
    ends = [jnp.concatenate([row_sum(one.at[f, c], 16, 16) for c in range(4)], axis=1) for f in range(3)]
    ends = jnp.dot(jnp.concatenate(ends, axis=0), gather, precision=EXACT, preferred_element_type=F32)
    defect = ends - jnp.where(at[0] == 0, 0.0, guess[...])
    for m in range(CUTS):
        sent[m] = defect


def rows_kernel(at, held, nu, send_a, send_b, send_c, send_d):
    odd = lax.rem(at[1], 2)
    odd_pair = lax.rem(at[1], 4) // 2
    for ref, lower in ((send_a, odd == 0), (send_b, odd == 1)):
        for m in range(11):
            ref[48 * m : 48 * m + 48, :] = held[m]
        for q in range(12):
            m, f = 11 + q // 3, q % 3
            ref[528 + 8 * q : 536 + 8 * q, :] = jnp.where(
                lower, held[m, 16 * f + 8 : 16 * f + 16, :], held[m, 16 * f : 16 * f + 8, :])
        ref[624:640, :] = nu[...]
    for ref, lower in ((send_c, odd_pair == 0), (send_d, odd_pair == 1)):
        for m in range(3):
            ref[48 * m : 48 * m + 48, :] = held[m]
        for q in range(12):
            m, f = 3 + q // 3, q % 3
            ref[144 + 8 * q : 152 + 8 * q, :] = jnp.where(
                lower, held[m, 16 * f + 8 : 16 * f + 16, :], held[m, 16 * f : 16 * f + 8, :])
        ref[240:256, :] = nu[...]


def cols_kernel(at, held, nu, got_a, got_b, got_c, got_d, whole, send_a, send_b):
    even = lax.rem(at[1], 2) == 0
    even_pair = lax.rem(at[1], 4) < 2
    even_y = lax.rem(at[2], 2) == 0

    def near(first, count):
        a, b = got_a[first : first + count, :], got_b[first : first + count, :]
        return jnp.where(even, b, a), jnp.where(even, a, b)

    def far(first, count):
        a, b = got_c[first : first + count, :], got_d[first : first + count, :]
        return jnp.where(even_pair, b, a), jnp.where(even_pair, a, b)

    for q in range(PLANES):
        m, f = q // 3, q % 3
        is_nu = q == 45
        whole[q, 32:48, :] = nu[...] if is_nu else held[m, 16 * f : 16 * f + 16, :]
        if is_nu or m < 11:
            before, after = near(624 if is_nu else 16 * q, 16)
            whole[q, 16:32, :] = before
            whole[q, 48:64, :] = after
        else:
            before, after = near(528 + 8 * (q - 33), 8)
            whole[q, 24:32, :] = before
            whole[q, 48:56, :] = after
        if is_nu or m < 3:
            before, after = far(240 if is_nu else 16 * q, 16)
            whole[q, 0:16, :] = before
            whole[q, 64:80, :] = after
        elif m < 7:
            before, after = far(144 + 8 * (q - 9), 8)
            whole[q, 8:16, :] = before
            whole[q, 64:72, :] = after
    for at_row, first, count, width, members in GROUPS:
        lane = lanes((count, 128))
        left = jnp.zeros((count, 128), F32)
        right = jnp.zeros((count, 128), F32)
        for slot, q in enumerate(members):
            offset = slot * width
            value = whole[q, first : first + count, :]
            mine = (lane >= offset) & (lane < offset + width)
            left = jnp.where(mine, pltpu.roll(value, offset, 1) if offset else value, left)
            shift = (offset + width) % 128
            right = jnp.where(mine, pltpu.roll(value, shift, 1) if shift else value, right)
        send_a[at_row : at_row + count, :] = jnp.where(even_y, right, left)
        send_b[at_row : at_row + count, :] = jnp.where(even_y, left, right)


def chain_kernel(at, whole, got_a, got_b, push, fine, guess, out, side, one, two, kept, mask, moved):
    even_y = lax.rem(at[2], 2) == 0
    for at_row, first, count, width, members in GROUPS:
        lane = lanes((count, 128))
        a, b = got_a[at_row : at_row + count, :], got_b[at_row : at_row + count, :]
        after, before = jnp.where(even_y, a, b), jnp.where(even_y, b, a)
        for slot, q in enumerate(members):
            offset = slot * width
            hi = pltpu.roll(after, (128 - offset) % 128, 1) if offset else after
            shift = (128 - width - offset) % 128
            lo = pltpu.roll(before, shift, 1) if shift else before
            side[q, first : first + count, :] = jnp.where(lane < width, hi, jnp.where(lane >= 128 - width, lo, 0.0))
    lane, line = lanes((EXT, 128)), sublanes((EXT, 128))
    row = at[1] * CROWS - 32 + line
    in_rows = (row >= 0) & (row < at[3] * CROWS)
    in_cols = ((lane >= 64) | (at[2] < at[4] - 1)) & ((lane < 64) | (at[2] > 0))
    mask[0] = in_rows.astype(F32)
    mask[1] = (in_rows & in_cols).astype(F32)
    for f in range(3):
        one[f, 0, 8:88, :] = whole[f]
        one[f, 1, 8:88, :] = side[f]

    def shifted(r):
        return pl.ds(r.start - 8, r.size)

    for n in range(1, CUTS):
        fields = (
            lambda c, r: (whole if c == 0 else side)[45, shifted(r), :],
            lambda c, r, n=n: push[n, 0, c, shifted(r), :],
            lambda c, r, n=n: push[n, 1, c, shifted(r), :],
            lambda c, r: mask[c, shifted(r), :],
        )
        for half in range(2):
            halo = 2 * (CUTS - 1 - n) + 1 - half
            count = 2 + -(-halo // 4)
            first = min(8 + 32 - halo, 88 - 8 * count)
            src, dst = (one, two) if half == 0 else (two, one)
            wanted = (0, 1) if halo else (0,)
            post = None
            if half == 1:
                def post(f, c, r, value, n=n):
                    if n < CUTS - 1:
                        one[f, c, r, :] = value + (whole if c == 0 else side)[3 * n + f, shifted(r), :]
                    else:
                        one[f, c, r, :] = value
                    if c == 0:
                        kept[f, r, :] = value
            for k in range(count):
                advance(src, dst, *fields, first + 8 * k, 8, 2, wanted, COARSE_TERMS, post=post)
        for f in range(3):
            moved[n, 16 * f : 16 * f + 16, :] = kept[f, 40:56, :]

    change = jnp.where(at[0] == 0, 0.0, moved[at[0]] - guess[...])
    i, j = sublanes((3 * ROWS, 48)), lanes((3 * ROWS, 48))
    repeat_rows = (i // 4 == j).astype(F32)
    i, j = sublanes((128, COLS)), lanes((128, COLS))
    repeat_cols = (i == j // 4).astype(F32)
    change = jnp.dot(repeat_rows, change, precision=EXACT, preferred_element_type=F32)
    change = jnp.dot(change, repeat_cols, precision=EXACT, preferred_element_type=F32)
    for f in range(3):
        out[f] = fine[f] + change[ROWS * f : ROWS * f + ROWS, :]


def call(kernel, args, outs, scratch=()):
    smem = pl.BlockSpec(memory_space=pltpu.SMEM)
    vmem = pl.BlockSpec(memory_space=pltpu.VMEM)
    shapes = [jax.ShapeDtypeStruct(s, F32) for s in outs]
    return pl.pallas_call(
        kernel,
        out_shape=shapes,
        in_specs=[smem] + [vmem] * (len(args) - 1),
        out_specs=[vmem] * len(shapes),
        scratch_shapes=[pltpu.VMEM(s, F32) for s in scratch],
        compiler_params=pltpu.CompilerParams(vmem_limit_bytes=48 * 1024 * 1024),
    )(*args)


def swap(x, axis, pairs):
    return lax.ppermute(x, axis, [(a, b) for a, b in pairs] + [(b, a) for a, b in pairs])


def on_device(starts, viscosity, turbine_x, turbine_y, yaw_index):
    count_x, count_y = lax.axis_size("sx"), lax.axis_size("sy")
    at = jnp.stack([
        lax.axis_index("cuts"), lax.axis_index("sx"), lax.axis_index("sy"),
        jnp.int32(count_x), jnp.int32(count_y),
    ]).astype(jnp.int32)
    start = starts[0]
    tx, ty, yaw = turbine_x[None, :], turbine_y[:, None], yaw_index.T
    x_a = [(i, i + 1) for i in range(0, count_x - 1, 2)]
    x_b = [(i, i + 1) for i in range(1, count_x - 1, 2)]
    x_c = [(i, i + 2) for i in range(count_x - 2) if i % 4 < 2]
    x_d = [(i, i + 2) for i in range(count_x - 2) if i % 4 >= 2]
    y_a = [(i, i + 1) for i in range(0, count_y - 1, 2)]
    y_b = [(i, i + 1) for i in range(1, count_y - 1, 2)]

    edge = (4, 8, COLS)
    send_a, send_b = call(edge_kernel, (at, start, viscosity), [edge, edge])
    rows_b = swap(send_b, "sx", x_b)
    rows_a = swap(send_a, "sx", x_a)
    push, own_push = call(push_kernel, (at, tx, ty, yaw), [(2, 5, 96, 128), (2, 2, 40, 128)])
    (chain_push,) = call(chain_push_kernel, (at, tx, ty, yaw), [(CUTS, 2, 2, EXT, 128)])
    send_a, send_b = call(side_kernel, (at, start, viscosity, rows_a, rows_b), [(EXT, 128)] * 2)
    cols_a = swap(send_a, "sy", y_a)
    cols_b = swap(send_b, "sy", y_b)
    fine, guess, sent, coarse_nu = call(
        fine_kernel,
        (at, start, viscosity, rows_a, rows_b, cols_a, cols_b, push, own_push),
        [(3, ROWS, COLS), (48, 128), (CUTS, 48, 128), (CROWS, 128)],
        [(3, 5, 96, 128), (3, 5, 96, 128), (5, 96, 128), (5, 96, 128), (4, 2, 40, 128), (3, 2, 40, 128), (2, 40, 128)],
    )
    held = lax.all_to_all(sent, "cuts", 0, 0)
    send_a, send_b, send_c, send_d = call(
        rows_kernel, (at, held, coarse_nu), [(S1_ROWS, 128)] * 2 + [(S2_ROWS, 128)] * 2)
    got_b = swap(send_b, "sx", x_b)
    got_c = swap(send_c, "sx", x_c)
    got_d = swap(send_d, "sx", x_d)
    got_a = swap(send_a, "sx", x_a)
    whole, send_a, send_b = call(
        cols_kernel, (at, held, coarse_nu, got_a, got_b, got_c, got_d), [(PLANES, EXT, 128)] + [(YROWS, 128)] * 2)
    got_a = swap(send_a, "sy", y_a)
    got_b = swap(send_b, "sy", y_b)
    (out,) = call(
        chain_kernel,
        (at, whole, got_a, got_b, chain_push, fine, guess),
        [(3, ROWS, COLS)],
        [(PLANES, EXT, 128), (3, 2, 96, 128), (3, 2, 96, 128), (3, 96, 128), (2, EXT, 128), (CUTS, 48, 128)],
    )
    return out[None]


def solution(mesh):
    in_specs = (P("cuts", None, "sx", "sy"), P("sx", "sy"), P(), P(), P())
    out_specs = P("cuts", None, "sx", "sy")
    return jax.shard_map(
        on_device, mesh=mesh, in_specs=in_specs, out_specs=out_specs, check_vma=False
    )
```

time: 520 us -> 102 us (0.20)
  the two profiles are of different devices: /device:TPU:412 before, /device:TPU:10 now
where the time goes in v1:
time: 102 us; the launch traced here: 101 us
  blocking collectives  36.7 us (36%)
  starting transfers between devices  28.5 us (28%)
  Pallas kernels  18.1 us (18%)
  waiting for transfers between devices  11.9 us (12%)
  local copies, waits for them, and re-layouts  6.06 us (6%)
    all_to_all x1, blocking collectives, on_device(): held = lax.all_to_all(sent, 'cuts', 0, 0)  36.7 us
    ppermute x10, starting transfers between devices, swap(): lax.ppermute(x, axis, [(a, b) for a, b in pairs] + [(b, a) for a, b in pa...  28.5 us
    pallas_call x8, Pallas kernels, call(): pl.pallas_call(kernel, out_shape=shapes, in_specs=[smem] + [vmem] * (len(...  18.1 us
    ppermute x10, waiting for transfers between devices, swap(): lax.ppermute(x, axis, [(a, b) for a, b in pairs] + [(b, a) for a, b in pa...  11.9 us
    unnamed x11, local copies, waits for them, and re-layouts  5.23 us
  transfers between devices with their start and end apart: 10, of which 6 were waited for; matrix products, arithmetic and copies ran while one was open for 2% of the time, Pallas kernels for 4%

profile of v1, /device:TPU:10, one launch (start us, length us, event | category | flops | bytes accessed | tf_op | source)
XLA Modules:
  0.0 101.3 jit_solution(11674451601310871521)
XLA Ops:
  0.1 1.0 copy-done
  1.1 0.9 copy-done.2
  2.0 0.6 shard_map.55
  2.6 1.9 %collective-permute-start = (f32[4,8,512]{2,1,0:T(8,128)S(1)}, f32[4,8,512]{2,1,0:T(8,128)S(1)}, u32[]{:S(2)}, u32[]{:S(2)}) collective-permute-start(f32[4,8,512]{2,1,0:T(8,128)S(1)} %get-tuple-element.22), channel_id=1, source_target_pairs={{0,4},{8,12},{16,20},{24,28},{4,0},{12,8},{20,16},{28,24},{1,5},{9... | collective-permute-start | bytes 196616 | tf_op jit(solution)/shard_map/ppermute | solution.py:429
  4.5 2.5 %collective-permute-start.1 = (f32[4,8,512]{2,1,0:T(8,128)S(1)}, f32[4,8,512]{2,1,0:T(8,128)S(1)}, u32[]{:S(2)}, u32[]{:S(2)}) collective-permute-start(f32[4,8,512]{2,1,0:T(8,128)S(1)} %get-tuple-element.23), channel_id=1, source_target_pairs={{4,8},{12,16},{20,24},{8,4},{16,12},{24,20},{5,9},{13,17},{21,25},... | collective-permute-start | bytes 196616 | tf_op jit(solution)/shard_map/ppermute | solution.py:429
  7.0 3.0 %collective-permute-done.1.got_b.rows_b = f32[4,8,512]{2,1,0:T(8,128)S(1)} collective-permute-done((f32[4,8,512]{2,1,0:T(8,128)S(1)}, f32[4,8,512]{2,1,0:T(8,128)S(1)}, u32[]{:S(2)}, u32[]{:S(2)}) %collective-permute-start.1) | collective-permute-done | bytes 65568 | tf_op jit(solution)/shard_map/ppermute | solution.py:429
  10.1 0.7 shard_map.56
  10.8 6.6 %collective-permute-start.2 = (f32[80,128]{1,0:T(8,128)S(1)}, f32[80,128]{1,0:T(8,128)S(1)}, u32[]{:S(2)}, u32[]{:S(2)}) collective-permute-start(f32[80,128]{1,0:T(8,128)S(1)} %get-tuple-element.24), channel_id=1, source_target_pairs={{0,1},{2,3},{1,0},{3,2},{4,5},{6,7},{5,4},{7,6},{8,9},{10,11},{9,8... | collective-permute-start | bytes 122888 | tf_op jit(solution)/shard_map/ppermute | solution.py:429
  17.4 1.9 %collective-permute-start.3 = (f32[80,128]{1,0:T(8,128)S(1)}, f32[80,128]{1,0:T(8,128)S(1)}, u32[]{:S(2)}, u32[]{:S(2)}) collective-permute-start(f32[80,128]{1,0:T(8,128)S(1)} %get-tuple-element.25), channel_id=1, source_target_pairs={{1,2},{2,1},{5,6},{6,5},{9,10},{10,9},{13,14},{14,13},{17,18},{18,... | collective-permute-start | bytes 122888 | tf_op jit(solution)/shard_map/ppermute | solution.py:429
  19.3 0.7 copy.7.ty
  20.1 0.8 copy.6
  20.9 0.7 copy-done.4
  21.5 1.4 %shard_map.57 = (f32[2,5,96,128]{3,2,1,0:T(8,128)S(1)}, f32[2,2,40,128]{3,2,1,0:T(8,128)S(1)}) custom-call(s32[5]{0:T(128)S(1)} %stack.15.at, s32[1,64]{1,0:T(1,128)S(1)} %bitcast.13, s32[64,1]{1,0:T(8,128)S(1)} %copy.7.ty, s32[64,16]{1,0:T(8,128)S(1)} %bitcast.11), custom_call_target="tpu_custom_call" | custom-call | tf_op jit(solution)/shard_map/pallas_call | solution.py:418
  22.9 0.4 collective-permute-done.3.cols_b
  23.3 1.0 copy-done.1
  24.3 0.9 copy-done.3
  25.2 3.3 %shard_map.58 = (f32[3,64,512]{2,1,0:T(8,128)S(1)}, f32[48,128]{1,0:T(8,128)S(1)}, f32[16,48,128]{2,1,0:T(8,128)S(1)}, f32[16,128]{1,0:T(8,128)S(1)}) custom-call(s32[5]{0:T(128)S(1)} %stack.15.at, f32[3,64,512]{2,1,0:T(8,128)S(1)} %bitcast.10, f32[64,512]{1,0:T(8,128)S(1)} %copy-done.3, f32[4,8,512]{2,1,0:T(8,128)S(1)} %collective-permute-done.got_a.rows_a, ...), custom_call_target="tpu_custom_call" | custom-call | tf_op jit(solution)/shard_map/pallas_call | solution.py:418
  28.5 36.7 %all_to_all.5.held = f32[16,48,128]{2,1,0:T(8,128)S(1)} all-to-all(f32[16,48,128]{2,1,0:T(8,128)S(1)} %get-tuple-element.28), channel_id=1, replica_groups=mesh['cuts'=16,'sx'=8,'sy'=4] {'cuts'}, dimensions={0} | all-to-all | bytes 786432 | tf_op jit(solution)/shard_map/all_to_all | solution.py:462
  65.2 0.6 shard_map.59
  65.8 1.9 %collective-permute-start.4 = (f32[640,128]{1,0:T(8,128)S(1)}, f32[640,128]{1,0:T(8,128)S(1)}, u32[]{:S(2)}, u32[]{:S(2)}) collective-permute-start(f32[640,128]{1,0:T(8,128)S(1)} %get-tuple-element.30), channel_id=1, source_target_pairs={{0,4},{8,12},{16,20},{24,28},{4,0},{12,8},{20,16},{28,24},{1,5},{9... | collective-permute-start | bytes 983048 | tf_op jit(solution)/shard_map/ppermute | solution.py:429
  67.8 1.9 %collective-permute-start.5 = (f32[640,128]{1,0:T(8,128)S(1)}, f32[640,128]{1,0:T(8,128)S(1)}, u32[]{:S(2)}, u32[]{:S(2)}) collective-permute-start(f32[640,128]{1,0:T(8,128)S(1)} %get-tuple-element.31), channel_id=1, source_target_pairs={{4,8},{12,16},{20,24},{8,4},{16,12},{24,20},{5,9},{13,17},{21,25},... | collective-permute-start | bytes 983048 | tf_op jit(solution)/shard_map/ppermute | solution.py:429
  69.7 1.9 %collective-permute-start.6 = (f32[256,128]{1,0:T(8,128)S(1)}, f32[256,128]{1,0:T(8,128)S(1)}, u32[]{:S(2)}, u32[]{:S(2)}) collective-permute-start(f32[256,128]{1,0:T(8,128)S(1)} %get-tuple-element.32), channel_id=1, source_target_pairs={{0,8},{4,12},{16,24},{20,28},{8,0},{12,4},{24,16},{28,20},{1,9},{5... | collective-permute-start | bytes 393224 | tf_op jit(solution)/shard_map/ppermute | solution.py:429
  71.6 5.5 %collective-permute-start.7 = (f32[256,128]{1,0:T(8,128)S(1)}, f32[256,128]{1,0:T(8,128)S(1)}, u32[]{:S(2)}, u32[]{:S(2)}) collective-permute-start(f32[256,128]{1,0:T(8,128)S(1)} %get-tuple-element.33), channel_id=1, source_target_pairs={{8,16},{12,20},{16,8},{20,12},{9,17},{13,21},{17,9},{21,13},{10,18... | collective-permute-start | bytes 393224 | tf_op jit(solution)/shard_map/ppermute | solution.py:429
  77.1 0.9 collective-permute-done.6.got_c
  78.0 2.7 %collective-permute-done.7.got_d = f32[256,128]{1,0:T(8,128)S(1)} collective-permute-done((f32[256,128]{1,0:T(8,128)S(1)}, f32[256,128]{1,0:T(8,128)S(1)}, u32[]{:S(2)}, u32[]{:S(2)}) %collective-permute-start.7) | collective-permute-done | bytes 131104 | tf_op jit(solution)/shard_map/ppermute | solution.py:429
  80.8 1.2 %shard_map.60 = (f32[46,80,128]{2,1,0:T(8,128)S(1)}, f32[560,128]{1,0:T(8,128)S(1)}, f32[560,128]{1,0:T(8,128)S(1)}) custom-call(s32[5]{0:T(128)S(1)} %stack.15.at, f32[16,48,128]{2,1,0:T(8,128)S(1)} %all_to_all.5.held, f32[16,128]{1,0:T(8,128)S(1)} %get-tuple-element.29.nu, f32[640,128]{1,0:T(8,128)S(1)} %collective-permute-done.4.got_a, ...), custom_call_target="tpu_custom_call" | custom-call | tf_op jit(solution)/shard_map/pallas_call | solution.py:418
  81.9 1.9 %collective-permute-start.8 = (f32[560,128]{1,0:T(8,128)S(1)}, f32[560,128]{1,0:T(8,128)S(1)}, u32[]{:S(2)}, u32[]{:S(2)}) collective-permute-start(f32[560,128]{1,0:T(8,128)S(1)} %get-tuple-element.35), channel_id=1, source_target_pairs={{0,1},{2,3},{1,0},{3,2},{4,5},{6,7},{5,4},{7,6},{8,9},{10,11},{9,8... | collective-permute-start | bytes 860168 | tf_op jit(solution)/shard_map/ppermute | solution.py:429
  83.9 2.3 %collective-permute-start.9 = (f32[560,128]{1,0:T(8,128)S(1)}, f32[560,128]{1,0:T(8,128)S(1)}, u32[]{:S(2)}, u32[]{:S(2)}) collective-permute-start(f32[560,128]{1,0:T(8,128)S(1)} %get-tuple-element.36), channel_id=1, source_target_pairs={{1,2},{2,1},{5,6},{6,5},{9,10},{10,9},{13,14},{14,13},{17,18},{18,... | collective-permute-start | bytes 860168 | tf_op jit(solution)/shard_map/ppermute | solution.py:429
  86.1 3.0 %shard_map.61.push = f32[16,2,2,80,128]{4,3,2,1,0:T(8,128)S(1)} custom-call(s32[5]{0:T(128)S(1)} %stack.15.at, s32[1,64]{1,0:T(1,128)S(1)} %bitcast.14, s32[64,1]{1,0:T(8,128)S(1)} %copy.7.ty, s32[64,16]{1,0:T(8,128)S(1)} %bitcast.12), custom_call_target="tpu_custom_call" | custom-call | tf_op jit(solution)/shard_map/pallas_call | solution.py:418
  89.1 2.9 %collective-permute-done.8.got_a = f32[560,128]{1,0:T(8,128)S(1)} collective-permute-done((f32[560,128]{1,0:T(8,128)S(1)}, f32[560,128]{1,0:T(8,128)S(1)}, u32[]{:S(2)}, u32[]{:S(2)}) %collective-permute-start.8) | collective-permute-done | bytes 286752 | tf_op jit(solution)/shard_map/ppermute | solution.py:429
  92.0 1.9 %collective-permute-done.9.got_b = f32[560,128]{1,0:T(8,128)S(1)} collective-permute-done((f32[560,128]{1,0:T(8,128)S(1)}, f32[560,128]{1,0:T(8,128)S(1)}, u32[]{:S(2)}, u32[]{:S(2)}) %collective-permute-start.9) | collective-permute-done | bytes 286752 | tf_op jit(solution)/shard_map/ppermute | solution.py:429
  94.0 7.4 %shard_map.62 = f32[3,64,512]{2,1,0:T(8,128)} custom-call(s32[5]{0:T(128)S(1)} %stack.15.at, f32[46,80,128]{2,1,0:T(8,128)S(1)} %get-tuple-element.34.whole, f32[560,128]{1,0:T(8,128)S(1)} %collective-permute-done.8.got_a, f32[560,128]{1,0:T(8,128)S(1)} %collective-permute-done.9.got_b, f32[16,2,2,80,128]{4,3,2,1,0:T(8,128)S(1)} %shard_map.61.push, ...), custom_call_target="tpu_custom_call" | custom-call | tf_op jit(solution)/shard_map/pallas_call | solution.py:418
  (10 shorter events, 0.1 us)
Async XLA Ops:
  0.1 1.0 copy-start
  1.1 0.9 copy-start.2
  2.6 4.5 %collective-permute-start = (f32[4,8,512]{2,1,0:T(8,128)S(1)}, f32[4,8,512]{2,1,0:T(8,128)S(1)}, u32[]{:S(2)}, u32[]{:S(2)}) collective-permute-start(f32[4,8,512]{2,1,0:T(8,128)S(1)} %get-tuple-element.22), channel_id=1, source_target_pairs={{0,4},{8,12},{16,20},{24,28},{4,0},{12,8},{20,16},{28,24},{1,5},{9... | collective-permute-start | bytes 196616 | tf_op jit(solution)/shard_map/ppermute | solution.py:429
  4.5 5.6 %collective-permute-start.1 = (f32[4,8,512]{2,1,0:T(8,128)S(1)}, f32[4,8,512]{2,1,0:T(8,128)S(1)}, u32[]{:S(2)}, u32[]{:S(2)}) collective-permute-start(f32[4,8,512]{2,1,0:T(8,128)S(1)} %get-tuple-element.23), channel_id=1, source_target_pairs={{4,8},{12,16},{20,24},{8,4},{16,12},{24,20},{5,9},{13,17},{21,25},... | collective-permute-start | bytes 196616 | tf_op jit(solution)/shard_map/ppermute | solution.py:429
  10.8 12.1 %collective-permute-start.2 = (f32[80,128]{1,0:T(8,128)S(1)}, f32[80,128]{1,0:T(8,128)S(1)}, u32[]{:S(2)}, u32[]{:S(2)}) collective-permute-start(f32[80,128]{1,0:T(8,128)S(1)} %get-tuple-element.24), channel_id=1, source_target_pairs={{0,1},{2,3},{1,0},{3,2},{4,5},{6,7},{5,4},{7,6},{8,9},{10,11},{9,8... | collective-permute-start | bytes 122888 | tf_op jit(solution)/shard_map/ppermute | solution.py:429
  17.4 5.9 %collective-permute-start.3 = (f32[80,128]{1,0:T(8,128)S(1)}, f32[80,128]{1,0:T(8,128)S(1)}, u32[]{:S(2)}, u32[]{:S(2)}) collective-permute-start(f32[80,128]{1,0:T(8,128)S(1)} %get-tuple-element.25), channel_id=1, source_target_pairs={{1,2},{2,1},{5,6},{6,5},{9,10},{10,9},{13,14},{14,13},{17,18},{18,... | collective-permute-start | bytes 122888 | tf_op jit(solution)/shard_map/ppermute | solution.py:429
  20.9 0.7 copy-start.4
  23.3 1.0 copy-start.1
  24.3 0.9 copy-start.3
  65.8 14.9 %collective-permute-start.4 = (f32[640,128]{1,0:T(8,128)S(1)}, f32[640,128]{1,0:T(8,128)S(1)}, u32[]{:S(2)}, u32[]{:S(2)}) collective-permute-start(f32[640,128]{1,0:T(8,128)S(1)} %get-tuple-element.30), channel_id=1, source_target_pairs={{0,4},{8,12},{16,20},{24,28},{4,0},{12,8},{20,16},{28,24},{1,5},{9... | collective-permute-start | bytes 983048 | tf_op jit(solution)/shard_map/ppermute | solution.py:429
  67.8 13.0 %collective-permute-start.5 = (f32[640,128]{1,0:T(8,128)S(1)}, f32[640,128]{1,0:T(8,128)S(1)}, u32[]{:S(2)}, u32[]{:S(2)}) collective-permute-start(f32[640,128]{1,0:T(8,128)S(1)} %get-tuple-element.31), channel_id=1, source_target_pairs={{4,8},{12,16},{20,24},{8,4},{16,12},{24,20},{5,9},{13,17},{21,25},... | collective-permute-start | bytes 983048 | tf_op jit(solution)/shard_map/ppermute | solution.py:429
  69.7 8.3 %collective-permute-start.6 = (f32[256,128]{1,0:T(8,128)S(1)}, f32[256,128]{1,0:T(8,128)S(1)}, u32[]{:S(2)}, u32[]{:S(2)}) collective-permute-start(f32[256,128]{1,0:T(8,128)S(1)} %get-tuple-element.32), channel_id=1, source_target_pairs={{0,8},{4,12},{16,24},{20,28},{8,0},{12,4},{24,16},{28,20},{1,9},{5... | collective-permute-start | bytes 393224 | tf_op jit(solution)/shard_map/ppermute | solution.py:429
  71.6 9.1 %collective-permute-start.7 = (f32[256,128]{1,0:T(8,128)S(1)}, f32[256,128]{1,0:T(8,128)S(1)}, u32[]{:S(2)}, u32[]{:S(2)}) collective-permute-start(f32[256,128]{1,0:T(8,128)S(1)} %get-tuple-element.33), channel_id=1, source_target_pairs={{8,16},{12,20},{16,8},{20,12},{9,17},{13,21},{17,9},{21,13},{10,18... | collective-permute-start | bytes 393224 | tf_op jit(solution)/shard_map/ppermute | solution.py:429
  81.9 10.1 %collective-permute-start.8 = (f32[560,128]{1,0:T(8,128)S(1)}, f32[560,128]{1,0:T(8,128)S(1)}, u32[]{:S(2)}, u32[]{:S(2)}) collective-permute-start(f32[560,128]{1,0:T(8,128)S(1)} %get-tuple-element.35), channel_id=1, source_target_pairs={{0,1},{2,3},{1,0},{3,2},{4,5},{6,7},{5,4},{7,6},{8,9},{10,11},{9,8... | collective-permute-start | bytes 860168 | tf_op jit(solution)/shard_map/ppermute | solution.py:429
  83.9 10.1 %collective-permute-start.9 = (f32[560,128]{1,0:T(8,128)S(1)}, f32[560,128]{1,0:T(8,128)S(1)}, u32[]{:S(2)}, u32[]{:S(2)}) collective-permute-start(f32[560,128]{1,0:T(8,128)S(1)} %get-tuple-element.36), channel_id=1, source_target_pairs={{1,2},{2,1},{5,6},{6,5},{9,10},{10,9},{13,14},{14,13},{17,18},{18,... | collective-permute-start | bytes 860168 | tf_op jit(solution)/shard_map/ppermute | solution.py:429

commit v2 on v0

v2 whole, which is shorter than its diff:
```python
import math

import jax
import jax.numpy as jnp
import numpy as np
from jax import lax
from jax.experimental import pallas as pl
from jax.experimental.pallas import tpu as pltpu
from jax.sharding import PartitionSpec as P

YAWS = 7
CUTS = 16
REACH = 3
F32 = jnp.float32
BF16 = jnp.bfloat16

FINE = (0.3, 0.25, 0.01)
FINE_THRUST = 0.5
FINE_SCALE = (0.25, 0.25, 0.025)
COARSE = (0.15, 0.125, 0.0025)
COARSE_THRUST = 1.0
COARSE_SCALE = (0.125, 0.125, 0.00625)
FINE_TO_COARSE = (0.5, 0.5, 0.25)

ROWS, COLS = 64, 512
CROWS, CCOLS = 16, 128
HALF = CUTS // 2
EXT = 48
NU = 45
ANGLES = [(k - 0.5 * (YAWS - 1)) * (math.pi / 18.0) for k in range(YAWS)]
WEIGHT_X = [float(np.float32(math.cos(t) ** 3)) for t in ANGLES]
WEIGHT_Y = [float(np.float32(math.cos(t) ** 2 * math.sin(t))) for t in ANGLES]

GROUPS = []
for _width, _members in (
    (32, list(range(21)) + [NU]),
    (16, list(range(21, 33))),
    (8, list(range(33, 45))),
):
    _per = 128 // _width
    GROUPS += [(_width, _members[_i : _i + _per]) for _i in range(0, len(_members), _per)]
STRIPS = 16 * len(GROUPS)
PARTS = (
    [(q, 16) for q in range(0, 9)] + [(q, 8) for q in range(9, 21)]
    + [(q, 16) for q in range(24, 33)] + [(q, 8) for q in range(33, 45)] + [(NU, 16)]
)
PART_AT = {}
_at = 0
for _q, _rows in PARTS:
    PART_AT[_q] = (_at, _rows)
    _at += _rows
STRIP_AT = _at
MESSAGE = STRIP_AT + 2 * STRIPS


def lanes(shape):
    return lax.broadcasted_iota(jnp.int32, shape, len(shape) - 1)


def sublanes(shape):
    return lax.broadcasted_iota(jnp.int32, shape, len(shape) - 2)


def rolled(x, by):
    return pltpu.roll(x, by % 128, 1) if by % 128 else x


def split3(x):
    high = x.astype(BF16)
    rest = x - high.astype(F32)
    middle = rest.astype(BF16)
    return high, middle, (rest - middle.astype(F32)).astype(BF16)


def exact_dot(x, y, dims=(((1,), (0,)), ((), ()))):
    y = y.astype(BF16)
    a, b, c = [lax.dot_general(part, y, dims, preferred_element_type=F32) for part in split3(x)]
    return a + (b + c)


def dot_exact(y, x):
    y = y.astype(BF16)
    a, b, c = [jnp.dot(y, part, preferred_element_type=F32) for part in split3(x)]
    return a + (b + c)


def advance(src, dst, coef, push, shift, row, count, tiles, wanted, terms, side_mask, post=None):
    _, lift, gain = terms
    lane = lanes((count, 128))
    low, high = lane == 0, lane == 127
    here, east, west = pl.ds(row, count), pl.ds(row + 1, count), pl.ds(row - 1, count)
    there = pl.ds(row - shift, count)
    mid = [[src[f, c, here, :] for c in range(tiles)] for f in range(3)]
    up = [[pltpu.roll(mid[f][c], 127, 1) for c in range(tiles)] for f in range(3)]
    down = [[pltpu.roll(mid[f][c], 1, 1) for c in range(tiles)] for f in range(3)]
    for c in wanted:
        after, before = (c + 1) % tiles, (c - 1) % tiles
        u, v, p = mid[0][c], mid[1][c], mid[2][c]
        un, vn, pn = [jnp.where(high, up[f][after], up[f][c]) for f in range(3)]
        us, vs, ps = [jnp.where(low, down[f][before], down[f][c]) for f in range(3)]
        ue, ve, pe = [src[f, c, east, :] for f in range(3)]
        uw, vw, pw = [src[f, c, west, :] for f in range(3)]
        nu, nu_carry, keep, keep_p = [coef[k, c, there, :] for k in range(4)]
        to_east, to_west = nu - u, nu_carry + u
        lifted = u + lift
        size = jnp.abs(lifted)
        drag = lifted * size / (size + lift)
        new_u = ue * to_east + uw * to_west + nu * (un + us) + keep * u - (pe - pw) - push(0, c, there) * drag
        new_v = ve * to_east + vw * to_west + nu * (vn + vs) + keep * v - (pn - ps) - push(1, c, there) * drag
        new_p = nu * ((pe + pw) + (pn + ps)) + keep_p * p - gain * ((ue - uw) + (vn - vs))
        new = [new_u, new_v, new_p]
        if c == tiles - 1:
            new = [f * side_mask for f in new]
        for f in range(3):
            if post is not None:
                new[f] = post(f, c, here, new[f])
            dst[f, c, here, :] = new[f]


def clear_rows(ref, tiles, before, after, outside):
    for row, factor in ((before, outside[0]), (after, outside[1])):
        for f in range(3):
            for c in range(tiles):
                ref[f, c, pl.ds(row, 1), :] = ref[f, c, pl.ds(row, 1), :] * factor


def edges(at):
    lane = lanes((8, 128))
    outside = [jnp.where(at[1] > 0, 1.0, 0.0), jnp.where(at[1] < at[3] - 1, 1.0, 0.0)]
    side = jnp.where(lane < 64, jnp.where(at[2] < at[4] - 1, 1.0, 0.0), jnp.where(at[2] > 0, 1.0, 0.0))
    return outside, side


def coefficients(coef, c, rows, nu, carry):
    coef[0, c, rows, :] = nu
    coef[1, c, rows, :] = nu + carry
    coef[2, c, rows, :] = (1.0 - carry) - 4.0 * nu
    coef[3, c, rows, :] = 1.0 - 4.0 * nu


def yaw_weights(yaw):
    wx = jnp.zeros(yaw.shape, F32)
    wy = jnp.zeros(yaw.shape, F32)
    for k in range(YAWS):
        hit = yaw == k
        wx = jnp.where(hit, WEIGHT_X[k], wx)
        wy = jnp.where(hit, WEIGHT_Y[k], wy)
    return wx, wy


def fetch(pairs, sems):
    copies = [pltpu.make_async_copy(a, b, sems.at[i]) for i, (a, b) in enumerate(pairs)]
    for copy in copies:
        copy.start()
    for copy in copies:
        copy.wait()


def edge_kernel(at, start, visc, send_a, send_b, sems):
    last = pl.multiple_of(56 * (1 - lax.rem(at[1], 2)), 8)
    first = pl.multiple_of(56 * lax.rem(at[1], 2), 8)
    fetch([
        (start.at[:, pl.ds(last, 8), :], send_a.at[0:3]),
        (visc.at[pl.ds(last, 8), :], send_a.at[3]),
        (start.at[:, pl.ds(first, 8), :], send_b.at[0:3]),
        (visc.at[pl.ds(first, 8), :], send_b.at[3]),
    ], sems)


def load_kernel(at, after, start, visc, out, sems):
    fetch(
        [(start.at[:, :, 128 * c : 128 * c + 128], out.at[0:3, c]) for c in range(4)]
        + [(visc.at[:, 128 * c : 128 * c + 128], out.at[3, c]) for c in range(4)],
        sems,
    )


def side_kernel(at, own, got_a, got_b, send_a, send_b):
    even_x = lax.rem(at[1], 2) == 0
    even_y = lax.rem(at[2], 2) == 0
    for r0, count in ((0, 8), (8, 64), (72, 8)):
        lane = lanes((count, 128))
        left = jnp.zeros((count, 128), F32)
        right = jnp.zeros((count, 128), F32)
        for f in range(4):
            if r0 == 8:
                a, b = own[f, 0], own[f, 3]
            else:
                from_a = jnp.logical_xor(even_x, r0 == 0)
                a = jnp.where(from_a, got_a[f, :, 0:128], got_b[f, :, 0:128])
                b = jnp.where(from_a, got_a[f, :, COLS - 128 : COLS], got_b[f, :, COLS - 128 : COLS])
            mine = (lane >= 8 * f) & (lane < 8 * f + 8)
            left = jnp.where(mine, rolled(a, 8 * f), left)
            right = jnp.where(mine, rolled(b, 8 * f + 8), right)
        send_a[r0 : r0 + count, :] = jnp.where(even_y, right, left)
        send_b[r0 : r0 + count, :] = jnp.where(even_y, left, right)


def fine_cols(sy, c, shape):
    i = sublanes(shape)
    return sy * COLS + (128 * c + i if c < 4 else jnp.where(i < 64, COLS + i, i - 128))


def coarse_cols(sy, c, ty):
    i = sublanes((128, 64))
    col = sy * CCOLS + (i if c == 0 else jnp.where(i < 64, CCOLS + i, i - 128))
    hit = jnp.zeros((128, 64), F32)
    for offset in range(4):
        hit = hit + jnp.where(jnp.abs(4 * col + offset - ty) <= REACH, 0.25, 0.0)
    return hit


LAST_DIMS = (((1,), (1,)), ((), ()))


def push_kernel(at, after, tx_in, ty_in, yaw_in, fine_push, own_push, tx_ref, ty_ref, yaw_ref, sems):
    fetch([(tx_in, tx_ref), (ty_in, ty_ref), (yaw_in, yaw_ref)], sems)
    tx, ty = tx_ref[...], ty_ref[...]
    mine = sublanes((CUTS, 64)) == at[0]
    wx, wy = yaw_weights(jnp.sum(jnp.where(mine, yaw_ref[...], 0), axis=0, keepdims=True))
    row = at[1] * ROWS - 16 + sublanes((96, 64))
    hit = jnp.where(row == tx, FINE_THRUST, 0.0)
    both = jnp.concatenate([hit * wx, hit * wy], axis=0)
    for c in range(5):
        cols = jnp.where(jnp.abs(fine_cols(at[2], c, (128, 64)) - ty) <= REACH, 1.0, 0.0)
        push = exact_dot(both, cols, LAST_DIMS)
        fine_push[0, c] = push[0:96]
        fine_push[1, c] = push[96:192]
    row = at[1] * CROWS - 10 + sublanes((40, 64))
    hit = jnp.where(row == tx // 4, 0.25 * COARSE_THRUST, 0.0)
    both = jnp.concatenate([hit * wx, hit * wy], axis=0)
    for c in range(2):
        push = exact_dot(both, coarse_cols(at[2], c, ty), LAST_DIMS)
        own_push[0, c] = push[0:40]
        own_push[1, c] = push[40:80]


def chain_push_kernel(at, after, tx_in, ty_in, yaw_in, push, tx_ref, ty_ref, yaw_ref, sems):
    fetch([(tx_in, tx_ref), (ty_in, ty_ref), (yaw_in, yaw_ref)], sems)
    tx, ty = tx_ref[...], ty_ref[...]
    row = at[1] * CROWS - 16 + sublanes((EXT, 64))
    hit = jnp.where(row == tx // 4, 0.25 * COARSE_THRUST, 0.0)
    wx, wy = yaw_weights(yaw_ref[...])
    cols = [coarse_cols(at[2], c, ty) for c in range(2)]
    for n in range(1, CUTS):
        both = jnp.concatenate([hit * wx[n : n + 1, :], hit * wy[n : n + 1, :]], axis=0)
        for c in range(2):
            value = exact_dot(both, cols[c], LAST_DIMS)
            push[n, 0, c] = value[0:EXT]
            push[n, 1, c] = value[EXT : 2 * EXT]


def fine_kernel(at, own, rows_a, rows_b, cols_a, cols_b, push, own_push, fine, guess, sent, coarse_nu,
                one, two, coef, rough, rough_two, rough_coef):
    even_x = lax.rem(at[1], 2) == 0
    even_y = lax.rem(at[2], 2) == 0
    outside, side_mask = edges(at)
    after_all = jnp.where(even_y, cols_a[...], cols_b[...])
    before_all = jnp.where(even_y, cols_b[...], cols_a[...])
    lane = lanes((80, 128))
    for f in range(4):
        for c in range(5):
            if c < 4:
                cut = slice(128 * c, 128 * c + 128)
                a, b = rows_a[f, :, cut], rows_b[f, :, cut]
                pieces = [(8, 8, jnp.where(even_x, b, a)), (16, 64, own[f, c]), (80, 8, jnp.where(even_x, a, b))]
            else:
                after, before = rolled(after_all, -8 * f), rolled(before_all, 120 - 8 * f)
                pieces = [(8, 80, jnp.where(lane < 8, after, jnp.where(lane >= 120, before, 0.0)))]
            for r, count, value in pieces:
                if f < 3:
                    one[f, c, r : r + count, :] = value * FINE_SCALE[f]
                else:
                    coefficients(coef, c, pl.ds(r, count), value, FINE[0])

    i, j = sublanes((COLS, 128)), lanes((COLS, 128))
    gather = jnp.where(i // 4 == j, 0.0625, 0.0)
    i, j = sublanes((128, 128)), lanes((128, 128))
    gather_side = jnp.where(((i < 8) & (i // 4 == j)) | ((i >= 120) & ((i - 120) // 4 == j - 126)), 0.0625, 0.0)

    def row_sum(ref, first, count):
        parts = [ref[pl.ds(first + k, count, stride=4), :] for k in range(4)]
        return (parts[0] + parts[1]) + (parts[2] + parts[3])

    def pick(f, c):
        return one.at[f, c] if f < 3 else coef.at[0, c]

    body = [jnp.concatenate([row_sum(pick(f, c), 0, 24) for c in range(4)], axis=1) for f in range(4)]
    side = [row_sum(pick(f, 4), 0, 24) for f in range(4)]
    body = exact_dot(jnp.concatenate(body, axis=0), gather)
    side = exact_dot(jnp.concatenate(side, axis=0), gather_side)
    rough[...] = jnp.zeros(rough.shape, F32)
    rough_two[...] = jnp.zeros(rough_two.shape, F32)
    rough_coef[...] = jnp.zeros(rough_coef.shape, F32)
    for c, value in enumerate((body, side)):
        for f in range(3):
            rough[f, c, 6:30, :] = value[24 * f : 24 * f + 24, :] * FINE_TO_COARSE[f]
        coefficients(rough_coef, c, pl.ds(6, 24), value[72:96, :] * 0.5, COARSE[0])
    coarse_nu[...] = rough_coef[0, 0, 10:26, :]

    def coarse_push(d, c, r):
        return own_push[d, c, r, :]

    for k in range(3):
        advance(rough, rough_two, rough_coef, coarse_push, 0, 9 + 8 * k, 8, 2, (0, 1), COARSE, side_mask)
    clear_rows(rough_two, 2, 9, 26, outside)
    for k in range(2):
        advance(rough_two, rough, rough_coef, coarse_push, 0, 10 + 8 * k, 8, 2, (0,), COARSE, side_mask)
    for f in range(3):
        guess[16 * f : 16 * f + 16, :] = rough[f, 0, 10:26, :]

    def fine_push(d, c, r):
        return push[d, c, r, :]

    for src, dst, first, count, wanted in (
        (one, two, 12, 9, range(5)),
        (two, one, 12, 9, range(5)),
        (one, two, 12, 9, range(5)),
        (two, one, 16, 8, range(4)),
    ):
        for k in range(count):
            advance(src, dst, coef, fine_push, 0, first + 8 * k, 8, 5, wanted, FINE, side_mask)
        if count == 9:
            clear_rows(dst, 5, 15, 80, outside)
    for f in range(3):
        for c in range(4):
            fine[f, :, 128 * c : 128 * c + 128] = one[f, c, 16:80, :] * (1.0 / FINE_SCALE[f])
    ends = [jnp.concatenate([row_sum(one.at[f, c], 16, 16) for c in range(4)], axis=1) for f in range(3)]
    ends = exact_dot(jnp.concatenate(ends, axis=0), gather)
    first_slice = at[0] == 0
    for f in range(3):
        cut = slice(16 * f, 16 * f + 16)
        defect = ends[cut] * FINE_TO_COARSE[f] - jnp.where(first_slice, 0.0, guess[cut, :])
        for m in range(CUTS):
            sent[m, cut, :] = defect


def plane_of(held, nu, q):
    return nu[...] if q == NU else held[q // 3, 16 * (q % 3) : 16 * (q % 3) + 16, :]


def cols_kernel(at, held, nu, send_a, send_b):
    even_y = lax.rem(at[2], 2) == 0
    lane = lanes((16, 128))
    for g, (width, members) in enumerate(GROUPS):
        left = jnp.zeros((16, 128), F32)
        right = jnp.zeros((16, 128), F32)
        for slot, q in enumerate(members):
            offset = slot * width
            value = plane_of(held, nu, q)
            mine = (lane >= offset) & (lane < offset + width)
            left = jnp.where(mine, rolled(value, offset), left)
            right = jnp.where(mine, rolled(value, offset + width), right)
        send_a[16 * g : 16 * g + 16, :] = jnp.where(even_y, right, left)
        send_b[16 * g : 16 * g + 16, :] = jnp.where(even_y, left, right)


def rows_kernel(at, held, nu, cols_a, cols_b, send_a, send_b):
    even = lax.rem(at[1], 2) == 0
    for q, rows in PARTS:
        place, _ = PART_AT[q]
        value = plane_of(held, nu, q)
        if rows == 16:
            send_a[place : place + 16, :] = value
            send_b[place : place + 16, :] = value
        else:
            send_a[place : place + 8, :] = jnp.where(even, value[8:16], value[0:8])
            send_b[place : place + 8, :] = jnp.where(even, value[0:8], value[8:16])
    for ref in (send_a, send_b):
        ref[STRIP_AT : STRIP_AT + STRIPS, :] = cols_a[...]
        ref[STRIP_AT + STRIPS : MESSAGE, :] = cols_b[...]


def assemble(at, planes, held, nu, cols_a, cols_b, rows_a, rows_b, put):
    even_x = lax.rem(at[1], 2) == 0
    even_y = lax.rem(at[2], 2) == 0
    for q in planes:
        put(q, 0, 16, plane_of(held, nu, q))
        if q in PART_AT:
            place, rows = PART_AT[q]
            a, b = rows_a[place : place + rows, :], rows_b[place : place + rows, :]
            put(q, 0, 16 - rows, jnp.where(even_x, b, a))
            put(q, 0, 32, jnp.where(even_x, a, b))
    lane = lanes((16, 128))
    for g, (width, members) in enumerate(GROUPS):
        if not any(q in planes for q in members):
            continue
        cut = slice(16 * g, 16 * g + 16)
        cut_a = slice(STRIP_AT + 16 * g, STRIP_AT + 16 * g + 16)
        cut_b = slice(STRIP_AT + STRIPS + 16 * g, STRIP_AT + STRIPS + 16 * g + 16)
        for first, a, b in (
            (16, cols_a[cut, :], cols_b[cut, :]),
            (0, jnp.where(even_x, rows_b[cut_a, :], rows_a[cut_a, :]), jnp.where(even_x, rows_b[cut_b, :], rows_a[cut_b, :])),
            (32, jnp.where(even_x, rows_a[cut_a, :], rows_b[cut_a, :]), jnp.where(even_x, rows_a[cut_b, :], rows_b[cut_b, :])),
        ):
            after, before = jnp.where(even_y, a, b), jnp.where(even_y, b, a)
            for slot, q in enumerate(members):
                if q in planes and (first == 16 or q in PART_AT):
                    hi, lo = rolled(after, -slot * width), rolled(before, 128 - width - slot * width)
                    put(q, 1, first, jnp.where(lane < width, hi, jnp.where(lane >= 128 - width, lo, 0.0)))


def chain(first_n, last_n, one, two, coef, push, added, at, save):
    outside, side_mask = edges(at)
    for n in range(first_n, last_n + 1):
        def pushed(d, c, r, n=n):
            return push[n, d, c, r, :]

        for half in range(2):
            halo = 2 * (last_n - n) + 1 - half
            count = 2 + -(-halo // 4)
            first = min(8 + 16 - halo, 8 + EXT - 8 * count)
            src, dst = (one, two) if half == 0 else (two, one)
            post = None
            if half == 1:
                def post(f, c, r, value, n=n):
                    return save(n, f, c, r, value, added)

            for k in range(count):
                advance(src, dst, coef, pushed, 8, first + 8 * k, 8, 2, (0, 1), COARSE, side_mask, post=post)
            if halo:
                clear_rows(dst, 2, 8 + 15, 8 + 32, outside)


def with_defect(kept, extra, first_plane, last):
    def save(n, f, c, r, value, added):
        if c == 0:
            kept[n % HALF, f, r, :] = value
        if n == last:
            return value
        return value + extra[3 * n + f - first_plane, c, pl.ds(r.start - 8, r.size), :]

    return save


def lower_kernel(at, held, nu, cols_a, cols_b, rows_a, rows_b, push, state, moved, coef, one, two, extra, kept):
    planes = list(range(3 * HALF)) + [NU]

    def put(q, c, row, value):
        rows = pl.ds(row, value.shape[0])
        if q == NU:
            coefficients(coef, c, rows, value, COARSE[0])
        elif q < 3:
            one[q, c, pl.ds(row + 8, value.shape[0]), :] = value
        else:
            extra[q - 3, c, rows, :] = value

    assemble(at, planes, held, nu, cols_a, cols_b, rows_a, rows_b, put)
    chain(1, HALF - 1, one, two, coef, push, extra, at, with_defect(kept, extra, 3, None))
    for f in range(3):
        for c in range(2):
            state[2 * f + c] = one[f, c, 24:40, :]
    mine = jnp.clip(at[0], 1, HALF - 1)
    for f in range(3):
        moved[16 * f : 16 * f + 16, :] = kept[mine, f, 24:40, :]


def upper_fields_kernel(at, held, nu, cols_a, cols_b, rows_a, rows_b, extra):
    planes = list(range(3 * HALF, NU))

    def put(q, c, row, value):
        extra[q - 3 * HALF, c, pl.ds(row, value.shape[0]), :] = value

    assemble(at, planes, held, nu, cols_a, cols_b, rows_a, rows_b, put)


def upper_kernel(at, state, state_a, state_b, extra, coef, push, fine, guess, moved, out, one, two, kept):
    even_x = lax.rem(at[1], 2) == 0
    for f in range(3):
        for c in range(2):
            a, b = state_a[2 * f + c], state_b[2 * f + c]
            one[f, c, 8:24, :] = jnp.where(even_x, b, a)
            one[f, c, 24:40, :] = state[2 * f + c]
            one[f, c, 40:56, :] = jnp.where(even_x, a, b)
    chain(HALF, CUTS - 1, one, two, coef, push, extra, at, with_defect(kept, extra, 3 * HALF, CUTS - 1))
    mine = jnp.maximum(at[0] - HALF, 0)
    parts = []
    for f in range(3):
        cut = slice(16 * f, 16 * f + 16)
        value = jnp.where(at[0] < HALF, moved[cut, :], kept[mine, f, 24:40, :]) - guess[cut, :]
        parts.append(jnp.where(at[0] == 0, 0.0, value * (1.0 / COARSE_SCALE[f])))
    change = jnp.concatenate(parts, axis=0)
    i, j = sublanes((3 * ROWS, 48)), lanes((3 * ROWS, 48))
    repeat_rows = jnp.where(i // 4 == j, 1.0, 0.0)
    i, j = sublanes((128, COLS)), lanes((128, COLS))
    repeat_cols = jnp.where(i == j // 4, 1.0, 0.0)
    change = exact_dot(dot_exact(repeat_rows, change), repeat_cols)
    for f in range(3):
        out[f] = fine[f] + change[ROWS * f : ROWS * f + ROWS, :]


SMEM = pl.BlockSpec(memory_space=pltpu.SMEM)
VMEM = pl.BlockSpec(memory_space=pltpu.VMEM)
ANY = pl.BlockSpec(memory_space=pl.ANY)


def call(kernel, args, outs, scratch=(), far=0, sems=0):
    shapes = [jax.ShapeDtypeStruct(s, F32) for s in outs]
    near = len(args) - 1 - far
    memory = [s if not isinstance(s, tuple) else pltpu.VMEM(s, F32) for s in scratch]
    if sems:
        memory.append(pltpu.SemaphoreType.DMA((sems,)))
    return pl.pallas_call(
        kernel,
        out_shape=shapes,
        in_specs=[SMEM] + [VMEM] * near + [ANY] * far,
        out_specs=[VMEM] * len(shapes),
        scratch_shapes=memory,
        compiler_params=pltpu.CompilerParams(vmem_limit_bytes=48 * 1024 * 1024),
    )(*args)


def swap(x, axis, pairs):
    return lax.ppermute(x, axis, [(a, b) for a, b in pairs] + [(b, a) for a, b in pairs])


def on_device(starts, viscosity, turbine_x, turbine_y, yaw_index):
    count_x, count_y = lax.axis_size("sx"), lax.axis_size("sy")
    at = jnp.stack([
        lax.axis_index("cuts"), lax.axis_index("sx"), lax.axis_index("sy"),
        jnp.int32(count_x), jnp.int32(count_y),
    ]).astype(jnp.int32)
    start = starts[0]
    x_a = [(i, i + 1) for i in range(0, count_x - 1, 2)]
    x_b = [(i, i + 1) for i in range(1, count_x - 1, 2)]
    y_a = [(i, i + 1) for i in range(0, count_y - 1, 2)]
    y_b = [(i, i + 1) for i in range(1, count_y - 1, 2)]
    turbines = (turbine_x[None, :], turbine_y[None, :], yaw_index)
    turbine_scratch = [pltpu.VMEM((1, 64), jnp.int32), pltpu.VMEM((1, 64), jnp.int32), pltpu.VMEM((CUTS, 64), jnp.int32)]

    edge = (4, 8, COLS)
    send_a, send_b = call(edge_kernel, (at, start, viscosity), [edge, edge], far=2, sems=4)
    rows_a = swap(send_a, "sx", x_a)
    rows_b = swap(send_b, "sx", x_b)
    (own,) = call(load_kernel, (at, send_b, start, viscosity), [(4, 4, ROWS, 128)], far=3, sems=8)
    send_a, send_b = call(side_kernel, (at, own, rows_a, rows_b), [(80, 128)] * 2)
    cols_a = swap(send_a, "sy", y_a)
    cols_b = swap(send_b, "sy", y_b)
    push, own_push = call(
        push_kernel, (at, send_b) + turbines, [(2, 5, 96, 128), (2, 2, 40, 128)], turbine_scratch, far=4, sems=3)
    fine, guess, sent, coarse_nu = call(
        fine_kernel,
        (at, own, rows_a, rows_b, cols_a, cols_b, push, own_push),
        [(3, ROWS, COLS), (48, 128), (CUTS, 48, 128), (CROWS, 128)],
        [(3, 5, 96, 128), (3, 5, 96, 128), (4, 5, 96, 128), (3, 2, 40, 128), (3, 2, 40, 128), (4, 2, 40, 128)],
    )
    held = lax.all_to_all(sent, "cuts", 0, 0)
    send_a, send_b = call(cols_kernel, (at, held, coarse_nu), [(STRIPS, 128)] * 2)
    cols_a = swap(send_a, "sy", y_a)
    cols_b = swap(send_b, "sy", y_b)
    (chain_push,) = call(
        chain_push_kernel, (at, send_b) + turbines, [(CUTS, 2, 2, EXT, 128)], turbine_scratch, far=4, sems=3)
    send_a, send_b = call(rows_kernel, (at, held, coarse_nu, cols_a, cols_b), [(MESSAGE, 128)] * 2)
    rows_a = swap(send_a, "sx", x_a)
    rows_b = swap(send_b, "sx", x_b)
    blocks = (at, held, coarse_nu, cols_a, cols_b, rows_a, rows_b)
    planes = 3 * HALF - 3
    field = (3, 2, 64, 128)
    state, moved, coef = call(
        lower_kernel, blocks + (chain_push,),
        [(6, CROWS, 128), (48, 128), (4, 2, EXT, 128)],
        [field, field, (planes, 2, EXT, 128), (HALF, 3, 64, 128)],
    )
    state_a = swap(state, "sx", x_a)
    state_b = swap(state, "sx", x_b)
    (extra,) = call(upper_fields_kernel, blocks, [(planes, 2, EXT, 128)])
    (out,) = call(
        upper_kernel,
        (at, state, state_a, state_b, extra, coef, chain_push, fine, guess, moved),
        [(3, ROWS, COLS)],
        [field, field, (HALF, 3, 64, 128)],
    )
    return out[None]


def solution(mesh):
    in_specs = (P("cuts", None, "sx", "sy"), P("sx", "sy"), P(), P(), P())
    out_specs = P("cuts", None, "sx", "sy")
    return jax.shard_map(
        on_device, mesh=mesh, in_specs=in_specs, out_specs=out_specs, check_vma=False
    )
```

time: 520 us -> 95 us (0.18)
  the two profiles are of different devices: /device:TPU:412 before, /device:TPU:17 now
where the time goes in v2:
time: 95 us; the launch traced here: 94.6 us
  starting transfers between devices  33.6 us (35%)
  blocking collectives  32.7 us (34%)
  Pallas kernels  17.9 us (19%)
  waiting for transfers between devices  8.27 us (9%)
  local copies, waits for them, and re-layouts  2 us (2%)
    ppermute x10, starting transfers between devices, swap(): lax.ppermute(x, axis, [(a, b) for a, b in pairs] + [(b, a) for a, b in pa...  33.6 us
    all_to_all x1, blocking collectives, on_device(): held = lax.all_to_all(sent, 'cuts', 0, 0)  32.7 us
    pallas_call x11, Pallas kernels, call(): pl.pallas_call(kernel, out_shape=shapes, in_specs=[SMEM] + [VMEM] * near...  17.9 us
    ppermute x10, waiting for transfers between devices, swap(): lax.ppermute(x, axis, [(a, b) for a, b in pairs] + [(b, a) for a, b in pa...  8.27 us
    unnamed x10, local copies, waits for them, and re-layouts  1.91 us
  transfers between devices with their start and end apart: 10, of which 6 were waited for; matrix products, arithmetic and copies ran while one was open for 0% of the time, Pallas kernels for 6%

profile of v2, /device:TPU:17, one launch (start us, length us, event | category | flops | bytes accessed | tf_op | source)
XLA Modules:
  0.0 94.6 jit_solution(8218647143311474083)
XLA Ops:
  0.0 0.1 stack.15.at
  0.1 1.0 %copy-done = f32[1,3,64,512]{3,2,1,0:T(8,128)S(1)} copy-done((f32[1,3,64,512]{3,2,1,0:T(8,128)S(1)}, f32[1,3,64,512]{3,2,1,0:T(8,128)}, u32[]{:S(2)}) %copy-start) | copy-done | bytes 393240
  1.1 0.9 copy-done.1
  2.0 0.7 shard_map.55
  2.7 2.6 %collective-permute-start = (f32[4,8,512]{2,1,0:T(8,128)S(1)}, f32[4,8,512]{2,1,0:T(8,128)S(1)}, u32[]{:S(2)}, u32[]{:S(2)}) collective-permute-start(f32[4,8,512]{2,1,0:T(8,128)S(1)} %get-tuple-element.23), channel_id=1, source_target_pairs={{0,4},{8,12},{16,20},{24,28},{4,0},{12,8},{20,16},{28,24},{1,5},{9... | collective-permute-start | bytes 196616 | tf_op jit(solution)/shard_map/ppermute | solution.py:514
  5.3 3.0 %collective-permute-start.1 = (f32[4,8,512]{2,1,0:T(8,128)S(1)}, f32[4,8,512]{2,1,0:T(8,128)S(1)}, u32[]{:S(2)}, u32[]{:S(2)}) collective-permute-start(f32[4,8,512]{2,1,0:T(8,128)S(1)} %get-tuple-element.22.after), channel_id=1, source_target_pairs={{4,8},{12,16},{20,24},{8,4},{16,12},{24,20},{5,9},{13,17},{21,25},... | collective-permute-start | bytes 196616 | tf_op jit(solution)/shard_map/ppermute | solution.py:514
  8.3 0.7 shard_map.56.own
  9.0 0.0 collective-permute-done.got_a.rows_a
  9.0 1.8 %collective-permute-done.1.got_b.rows_b = f32[4,8,512]{2,1,0:T(8,128)S(1)} collective-permute-done((f32[4,8,512]{2,1,0:T(8,128)S(1)}, f32[4,8,512]{2,1,0:T(8,128)S(1)}, u32[]{:S(2)}, u32[]{:S(2)}) %collective-permute-start.1) | collective-permute-done | bytes 65568 | tf_op jit(solution)/shard_map/ppermute | solution.py:514
  10.9 0.7 shard_map.57
  11.6 2.9 %collective-permute-start.2 = (f32[80,128]{1,0:T(8,128)S(1)}, f32[80,128]{1,0:T(8,128)S(1)}, u32[]{:S(2)}, u32[]{:S(2)}) collective-permute-start(f32[80,128]{1,0:T(8,128)S(1)} %get-tuple-element.24), channel_id=1, source_target_pairs={{0,1},{2,3},{1,0},{3,2},{4,5},{6,7},{5,4},{7,6},{8,9},{10,11},{9,8... | collective-permute-start | bytes 122888 | tf_op jit(solution)/shard_map/ppermute | solution.py:514
  14.5 6.6 %collective-permute-start.3 = (f32[80,128]{1,0:T(8,128)S(1)}, f32[80,128]{1,0:T(8,128)S(1)}, u32[]{:S(2)}, u32[]{:S(2)}) collective-permute-start(f32[80,128]{1,0:T(8,128)S(1)} %get-tuple-element.25.after), channel_id=1, source_target_pairs={{1,2},{2,1},{5,6},{6,5},{9,10},{10,9},{13,14},{14,13},{17,18},{18,... | collective-permute-start | bytes 122888 | tf_op jit(solution)/shard_map/ppermute | solution.py:514
  21.1 1.2 %shard_map.58 = (f32[2,5,96,128]{3,2,1,0:T(8,128)S(1)}, f32[2,2,40,128]{3,2,1,0:T(8,128)S(1)}) custom-call(s32[5]{0:T(128)S(1)} %stack.15.at, f32[80,128]{1,0:T(8,128)S(1)} %get-tuple-element.25.after, s32[1,64]{1,0:T(1,128)S(1)} %bitcast.9, s32[1,64]{1,0:T(1,128)S(1)} %bitcast.11, s32[16,64]{1,0:T(8,128)S(1)} %copy-done.2), custom_call_target="tpu_custom_call" | custom-call | tf_op jit(solution)/shard_map/pallas_call | solution.py:503
  22.3 0.2 collective-permute-done.3.cols_b
  22.5 3.0 %shard_map.59 = (f32[3,64,512]{2,1,0:T(8,128)S(1)}, f32[48,128]{1,0:T(8,128)S(1)}, f32[16,48,128]{2,1,0:T(8,128)S(1)}, f32[16,128]{1,0:T(8,128)S(1)}) custom-call(s32[5]{0:T(128)S(1)} %stack.15.at, f32[4,4,64,128]{3,2,1,0:T(8,128)S(1)} %shard_map.56.own, f32[4,8,512]{2,1,0:T(8,128)S(1)} %collective-permute-done.got_a.rows_a, ...), custom_call_target="tpu_custom_call" | custom-call | tf_op jit(solution)/shard_map/pallas_call | solution.py:503
  25.5 32.7 %all_to_all.5.held = f32[16,48,128]{2,1,0:T(8,128)S(1)} all-to-all(f32[16,48,128]{2,1,0:T(8,128)S(1)} %get-tuple-element.28), channel_id=1, replica_groups=mesh['cuts'=16,'sx'=8,'sy'=4] {'cuts'}, dimensions={0} | all-to-all | bytes 786432 | tf_op jit(solution)/shard_map/all_to_all | solution.py:547
  58.2 0.8 shard_map.60
  58.9 1.9 %collective-permute-start.4 = (f32[144,128]{1,0:T(8,128)S(1)}, f32[144,128]{1,0:T(8,128)S(1)}, u32[]{:S(2)}, u32[]{:S(2)}) collective-permute-start(f32[144,128]{1,0:T(8,128)S(1)} %get-tuple-element.30), channel_id=1, source_target_pairs={{0,1},{2,3},{1,0},{3,2},{4,5},{6,7},{5,4},{7,6},{8,9},{10,11},{9,8... | collective-permute-start | bytes 221192 | tf_op jit(solution)/shard_map/ppermute | solution.py:514
  60.8 1.9 %collective-permute-start.5 = (f32[144,128]{1,0:T(8,128)S(1)}, f32[144,128]{1,0:T(8,128)S(1)}, u32[]{:S(2)}, u32[]{:S(2)}) collective-permute-start(f32[144,128]{1,0:T(8,128)S(1)} %get-tuple-element.31.after), channel_id=1, source_target_pairs={{1,2},{2,1},{5,6},{6,5},{9,10},{10,9},{13,14},{14,13},{17,18},{18,... | collective-permute-start | bytes 221192 | tf_op jit(solution)/shard_map/ppermute | solution.py:514
  62.8 1.2 %collective-permute-done.4.cols_a = f32[144,128]{1,0:T(8,128)S(1)} collective-permute-done((f32[144,128]{1,0:T(8,128)S(1)}, f32[144,128]{1,0:T(8,128)S(1)}, u32[]{:S(2)}, u32[]{:S(2)}) %collective-permute-start.4) | collective-permute-done | bytes 73760 | tf_op jit(solution)/shard_map/ppermute | solution.py:514
  64.0 1.9 %collective-permute-done.5.cols_b = f32[144,128]{1,0:T(8,128)S(1)} collective-permute-done((f32[144,128]{1,0:T(8,128)S(1)}, f32[144,128]{1,0:T(8,128)S(1)}, u32[]{:S(2)}, u32[]{:S(2)}) %collective-permute-start.5) | collective-permute-done | bytes 73760 | tf_op jit(solution)/shard_map/ppermute | solution.py:514
  65.9 0.6 shard_map.61
  66.5 1.9 %collective-permute-start.6 = (f32[784,128]{1,0:T(8,128)S(1)}, f32[784,128]{1,0:T(8,128)S(1)}, u32[]{:S(2)}, u32[]{:S(2)}) collective-permute-start(f32[784,128]{1,0:T(8,128)S(1)} %get-tuple-element.32), channel_id=1, source_target_pairs={{0,4},{8,12},{16,20},{24,28},{4,0},{12,8},{20,16},{28,24},{1,5},{9... | collective-permute-start | bytes 1204232 | tf_op jit(solution)/shard_map/ppermute | solution.py:514
  68.5 7.2 %collective-permute-start.7 = (f32[784,128]{1,0:T(8,128)S(1)}, f32[784,128]{1,0:T(8,128)S(1)}, u32[]{:S(2)}, u32[]{:S(2)}) collective-permute-start(f32[784,128]{1,0:T(8,128)S(1)} %get-tuple-element.33), channel_id=1, source_target_pairs={{4,8},{12,16},{20,24},{8,4},{16,12},{24,20},{5,9},{13,17},{21,25},... | collective-permute-start | bytes 1204232 | tf_op jit(solution)/shard_map/ppermute | solution.py:514
  75.6 2.7 %shard_map.62.push = f32[16,2,2,48,128]{4,3,2,1,0:T(8,128)S(1)} custom-call(s32[5]{0:T(128)S(1)} %stack.15.at, f32[144,128]{1,0:T(8,128)S(1)} %get-tuple-element.31.after, s32[1,64]{1,0:T(1,128)S(1)} %bitcast.10, s32[1,64]{1,0:T(1,128)S(1)} %bitcast.12, s32[16,64]{1,0:T(8,128)S(1)} %copy-done.2), custom_call_target="tpu_custom_call" | custom-call | tf_op jit(solution)/shard_map/pallas_call | solution.py:503
  78.4 2.8 %collective-permute-done.7.rows_b = f32[784,128]{1,0:T(8,128)S(1)} collective-permute-done((f32[784,128]{1,0:T(8,128)S(1)}, f32[784,128]{1,0:T(8,128)S(1)}, u32[]{:S(2)}, u32[]{:S(2)}) %collective-permute-start.7) | collective-permute-done | bytes 401440 | tf_op jit(solution)/shard_map/ppermute | solution.py:514
  81.2 2.6 %shard_map.63 = (f32[6,16,128]{2,1,0:T(8,128)S(1)}, f32[48,128]{1,0:T(8,128)S(1)}, f32[4,2,48,128]{3,2,1,0:T(8,128)S(1)}) custom-call(s32[5]{0:T(128)S(1)} %stack.15.at, f32[16,48,128]{2,1,0:T(8,128)S(1)} %all_to_all.5.held, f32[16,128]{1,0:T(8,128)S(1)} %get-tuple-element.29.nu, f32[144,128]{1,0:T(8,128)S(1)} %collective-permute-done.4.cols_a, ...), custom_call_target="tpu_custom_call" | custom-call | tf_op jit(solution)/shard_map/pallas_call | solution.py:503
  83.8 3.6 %collective-permute-start.9 = (f32[6,16,128]{2,1,0:T(8,128)S(1)}, f32[6,16,128]{2,1,0:T(8,128)S(1)}, u32[]{:S(2)}, u32[]{:S(2)}) collective-permute-start(f32[6,16,128]{2,1,0:T(8,128)S(1)} %get-tuple-element.34.state), channel_id=1, source_target_pairs={{4,8},{12,16},{20,24},{8,4},{16,12},{24,20},{5,9},{13,17},{21,25},... | collective-permute-start | bytes 147464 | tf_op jit(solution)/shard_map/ppermute | solution.py:514
  87.5 1.9 %collective-permute-start.8 = (f32[6,16,128]{2,1,0:T(8,128)S(1)}, f32[6,16,128]{2,1,0:T(8,128)S(1)}, u32[]{:S(2)}, u32[]{:S(2)}) collective-permute-start(f32[6,16,128]{2,1,0:T(8,128)S(1)} %get-tuple-element.34.state), channel_id=1, source_target_pairs={{0,4},{8,12},{16,20},{24,28},{4,0},{12,8},{20,16},{28,24},{1,5},{9... | collective-permute-start | bytes 147464 | tf_op jit(solution)/shard_map/ppermute | solution.py:514
  89.4 0.9 shard_map.64.extra
  90.3 0.3 collective-permute-done.8.state_a
  90.6 4.1 %shard_map.65 = f32[3,64,512]{2,1,0:T(8,128)} custom-call(s32[5]{0:T(128)S(1)} %stack.15.at, f32[6,16,128]{2,1,0:T(8,128)S(1)} %get-tuple-element.34.state, f32[6,16,128]{2,1,0:T(8,128)S(1)} %collective-permute-done.8.state_a, f32[6,16,128]{2,1,0:T(8,128)S(1)} %collective-permute-done.9.state_b, f32[21,2,48,128]{3,2,1,0:T(8,128)S(1)} %shard_map.64.extra, ...), custom_call_target="tpu_custom_call" | custom-call | tf_op jit(solution)/shard_map/pallas_call | solution.py:503
  (11 shorter events, 0.0 us)
Async XLA Ops:
  0.0 21.1 %copy-start.2 = (s32[16,64]{1,0:T(8,128)S(1)}, s32[16,64]{1,0:T(8,128)}, u32[]{:S(2)}) copy-start(s32[16,64]{1,0:T(8,128)} %yaw_in.3) | copy-start | bytes 12292
  0.0 21.1 %copy-start.4 = (s32[64]{0:T(128)S(1)}, s32[64]{0:T(128)}, u32[]{:S(2)}) copy-start(s32[64]{0:T(128)} %param.8) | copy-start | bytes 772
  0.0 21.1 %copy-start.3 = (s32[64]{0:T(128)S(1)}, s32[64]{0:T(128)}, u32[]{:S(2)}) copy-start(s32[64]{0:T(128)} %param.7) | copy-start | bytes 772
  0.1 1.0 %copy-start = (f32[1,3,64,512]{3,2,1,0:T(8,128)S(1)}, f32[1,3,64,512]{3,2,1,0:T(8,128)}, u32[]{:S(2)}) copy-start(f32[1,3,64,512]{3,2,1,0:T(8,128)} %param.5) | copy-start | bytes 1179652
  1.1 0.9 copy-start.1
  2.7 6.3 %collective-permute-start = (f32[4,8,512]{2,1,0:T(8,128)S(1)}, f32[4,8,512]{2,1,0:T(8,128)S(1)}, u32[]{:S(2)}, u32[]{:S(2)}) collective-permute-start(f32[4,8,512]{2,1,0:T(8,128)S(1)} %get-tuple-element.23), channel_id=1, source_target_pairs={{0,4},{8,12},{16,20},{24,28},{4,0},{12,8},{20,16},{28,24},{1,5},{9... | collective-permute-start | bytes 196616 | tf_op jit(solution)/shard_map/ppermute | solution.py:514
  5.3 5.6 %collective-permute-start.1 = (f32[4,8,512]{2,1,0:T(8,128)S(1)}, f32[4,8,512]{2,1,0:T(8,128)S(1)}, u32[]{:S(2)}, u32[]{:S(2)}) collective-permute-start(f32[4,8,512]{2,1,0:T(8,128)S(1)} %get-tuple-element.22.after), channel_id=1, source_target_pairs={{4,8},{12,16},{20,24},{8,4},{16,12},{24,20},{5,9},{13,17},{21,25},... | collective-permute-start | bytes 196616 | tf_op jit(solution)/shard_map/ppermute | solution.py:514
  11.6 10.8 %collective-permute-start.2 = (f32[80,128]{1,0:T(8,128)S(1)}, f32[80,128]{1,0:T(8,128)S(1)}, u32[]{:S(2)}, u32[]{:S(2)}) collective-permute-start(f32[80,128]{1,0:T(8,128)S(1)} %get-tuple-element.24), channel_id=1, source_target_pairs={{0,1},{2,3},{1,0},{3,2},{4,5},{6,7},{5,4},{7,6},{8,9},{10,11},{9,8... | collective-permute-start | bytes 122888 | tf_op jit(solution)/shard_map/ppermute | solution.py:514
  14.5 8.0 %collective-permute-start.3 = (f32[80,128]{1,0:T(8,128)S(1)}, f32[80,128]{1,0:T(8,128)S(1)}, u32[]{:S(2)}, u32[]{:S(2)}) collective-permute-start(f32[80,128]{1,0:T(8,128)S(1)} %get-tuple-element.25.after), channel_id=1, source_target_pairs={{1,2},{2,1},{5,6},{6,5},{9,10},{10,9},{13,14},{14,13},{17,18},{18,... | collective-permute-start | bytes 122888 | tf_op jit(solution)/shard_map/ppermute | solution.py:514
  58.9 5.1 %collective-permute-start.4 = (f32[144,128]{1,0:T(8,128)S(1)}, f32[144,128]{1,0:T(8,128)S(1)}, u32[]{:S(2)}, u32[]{:S(2)}) collective-permute-start(f32[144,128]{1,0:T(8,128)S(1)} %get-tuple-element.30), channel_id=1, source_target_pairs={{0,1},{2,3},{1,0},{3,2},{4,5},{6,7},{5,4},{7,6},{8,9},{10,11},{9,8... | collective-permute-start | bytes 221192 | tf_op jit(solution)/shard_map/ppermute | solution.py:514
  60.8 5.1 %collective-permute-start.5 = (f32[144,128]{1,0:T(8,128)S(1)}, f32[144,128]{1,0:T(8,128)S(1)}, u32[]{:S(2)}, u32[]{:S(2)}) collective-permute-start(f32[144,128]{1,0:T(8,128)S(1)} %get-tuple-element.31.after), channel_id=1, source_target_pairs={{1,2},{2,1},{5,6},{6,5},{9,10},{10,9},{13,14},{14,13},{17,18},{18,... | collective-permute-start | bytes 221192 | tf_op jit(solution)/shard_map/ppermute | solution.py:514
  66.5 11.8 %collective-permute-start.6 = (f32[784,128]{1,0:T(8,128)S(1)}, f32[784,128]{1,0:T(8,128)S(1)}, u32[]{:S(2)}, u32[]{:S(2)}) collective-permute-start(f32[784,128]{1,0:T(8,128)S(1)} %get-tuple-element.32), channel_id=1, source_target_pairs={{0,4},{8,12},{16,20},{24,28},{4,0},{12,8},{20,16},{28,24},{1,5},{9... | collective-permute-start | bytes 1204232 | tf_op jit(solution)/shard_map/ppermute | solution.py:514
  68.5 12.7 %collective-permute-start.7 = (f32[784,128]{1,0:T(8,128)S(1)}, f32[784,128]{1,0:T(8,128)S(1)}, u32[]{:S(2)}, u32[]{:S(2)}) collective-permute-start(f32[784,128]{1,0:T(8,128)S(1)} %get-tuple-element.33), channel_id=1, source_target_pairs={{4,8},{12,16},{20,24},{8,4},{16,12},{24,20},{5,9},{13,17},{21,25},... | collective-permute-start | bytes 1204232 | tf_op jit(solution)/shard_map/ppermute | solution.py:514
  83.8 6.5 %collective-permute-start.9 = (f32[6,16,128]{2,1,0:T(8,128)S(1)}, f32[6,16,128]{2,1,0:T(8,128)S(1)}, u32[]{:S(2)}, u32[]{:S(2)}) collective-permute-start(f32[6,16,128]{2,1,0:T(8,128)S(1)} %get-tuple-element.34.state), channel_id=1, source_target_pairs={{4,8},{12,16},{20,24},{8,4},{16,12},{24,20},{5,9},{13,17},{21,25},... | collective-permute-start | bytes 147464 | tf_op jit(solution)/shard_map/ppermute | solution.py:514
  87.5 3.1 %collective-permute-start.8 = (f32[6,16,128]{2,1,0:T(8,128)S(1)}, f32[6,16,128]{2,1,0:T(8,128)S(1)}, u32[]{:S(2)}, u32[]{:S(2)}) collective-permute-start(f32[6,16,128]{2,1,0:T(8,128)S(1)} %get-tuple-element.34.state), channel_id=1, source_target_pairs={{0,4},{8,12},{16,20},{24,28},{4,0},{12,8},{20,16},{28,24},{1,5},{9... | collective-permute-start | bytes 147464 | tf_op jit(solution)/shard_map/ppermute | solution.py:514

commit v3 on v2

--- a/solution.py
+++ b/solution.py
@@ -26,31 +26,24 @@
 CROWS, CCOLS = 16, 128
 HALF = CUTS // 2
 EXT = 48
-NU = 45
+NU = 24
 ANGLES = [(k - 0.5 * (YAWS - 1)) * (math.pi / 18.0) for k in range(YAWS)]
 WEIGHT_X = [float(np.float32(math.cos(t) ** 3)) for t in ANGLES]
 WEIGHT_Y = [float(np.float32(math.cos(t) ** 2 * math.sin(t))) for t in ANGLES]
 
-GROUPS = []
-for _width, _members in (
-    (32, list(range(21)) + [NU]),
-    (16, list(range(21, 33))),
-    (8, list(range(33, 45))),
-):
-    _per = 128 // _width
-    GROUPS += [(_width, _members[_i : _i + _per]) for _i in range(0, len(_members), _per)]
+WIDTH = 32
+_ORDER = list(range(21)) + [NU, 21, 22, 23]
+GROUPS = [_ORDER[_i : _i + 4] for _i in range(0, len(_ORDER), 4)]
 STRIPS = 16 * len(GROUPS)
-PARTS = (
-    [(q, 16) for q in range(0, 9)] + [(q, 8) for q in range(9, 21)]
-    + [(q, 16) for q in range(24, 33)] + [(q, 8) for q in range(33, 45)] + [(NU, 16)]
-)
+ROW_STRIPS = 16 * 6
+PARTS = [(q, 16) for q in range(0, 9)] + [(q, 8) for q in range(9, 21)] + [(NU, 16)]
 PART_AT = {}
 _at = 0
 for _q, _rows in PARTS:
     PART_AT[_q] = (_at, _rows)
     _at += _rows
 STRIP_AT = _at
-MESSAGE = STRIP_AT + 2 * STRIPS
+MESSAGE = STRIP_AT + 2 * ROW_STRIPS
 
 
 def lanes(shape):
@@ -240,14 +233,14 @@
     tx, ty = tx_ref[...], ty_ref[...]
     row = at[1] * CROWS - 16 + sublanes((EXT, 64))
     hit = jnp.where(row == tx // 4, 0.25 * COARSE_THRUST, 0.0)
-    wx, wy = yaw_weights(yaw_ref[...])
+    wx, wy = yaw_weights(yaw_ref[pl.ds(pl.multiple_of(at[0] // HALF * HALF, HALF), HALF), :])
     cols = [coarse_cols(at[2], c, ty) for c in range(2)]
-    for n in range(1, CUTS):
-        both = jnp.concatenate([hit * wx[n : n + 1, :], hit * wy[n : n + 1, :]], axis=0)
+    for k in range(HALF):
+        both = jnp.concatenate([hit * wx[k : k + 1, :], hit * wy[k : k + 1, :]], axis=0)
         for c in range(2):
             value = exact_dot(both, cols[c], LAST_DIMS)
-            push[n, 0, c] = value[0:EXT]
-            push[n, 1, c] = value[EXT : 2 * EXT]
+            push[k, 0, c] = value[0:EXT]
+            push[k, 1, c] = value[EXT : 2 * EXT]
 
 
 def fine_kernel(at, own, rows_a, rows_b, cols_a, cols_b, push, own_push, fine, guess, sent, coarse_nu,
@@ -331,7 +324,7 @@
     for f in range(3):
         cut = slice(16 * f, 16 * f + 16)
         defect = ends[cut] * FINE_TO_COARSE[f] - jnp.where(first_slice, 0.0, guess[cut, :])
-        for m in range(CUTS):
+        for m in range(HALF):
             sent[m, cut, :] = defect
 
 
@@ -342,15 +335,15 @@
 def cols_kernel(at, held, nu, send_a, send_b):
     even_y = lax.rem(at[2], 2) == 0
     lane = lanes((16, 128))
-    for g, (width, members) in enumerate(GROUPS):
+    for g, members in enumerate(GROUPS):
         left = jnp.zeros((16, 128), F32)
         right = jnp.zeros((16, 128), F32)
         for slot, q in enumerate(members):
-            offset = slot * width
+            offset = slot * WIDTH
             value = plane_of(held, nu, q)
-            mine = (lane >= offset) & (lane < offset + width)
+            mine = (lane >= offset) & (lane < offset + WIDTH)
             left = jnp.where(mine, rolled(value, offset), left)
-            right = jnp.where(mine, rolled(value, offset + width), right)
+            right = jnp.where(mine, rolled(value, offset + WIDTH), right)
         send_a[16 * g : 16 * g + 16, :] = jnp.where(even_y, right, left)
         send_b[16 * g : 16 * g + 16, :] = jnp.where(even_y, left, right)
 
@@ -367,14 +360,14 @@
             send_a[place : place + 8, :] = jnp.where(even, value[8:16], value[0:8])
             send_b[place : place + 8, :] = jnp.where(even, value[0:8], value[8:16])
     for ref in (send_a, send_b):
-        ref[STRIP_AT : STRIP_AT + STRIPS, :] = cols_a[...]
-        ref[STRIP_AT + STRIPS : MESSAGE, :] = cols_b[...]
-
-
-def assemble(at, planes, held, nu, cols_a, cols_b, rows_a, rows_b, put):
+        ref[STRIP_AT : STRIP_AT + ROW_STRIPS, :] = cols_a[0:ROW_STRIPS, :]
+        ref[STRIP_AT + ROW_STRIPS : MESSAGE, :] = cols_b[0:ROW_STRIPS, :]
+
+
+def assemble(at, held, nu, cols_a, cols_b, rows_a, rows_b, put):
     even_x = lax.rem(at[1], 2) == 0
     even_y = lax.rem(at[2], 2) == 0
-    for q in planes:
+    for q in range(NU + 1):
         put(q, 0, 16, plane_of(held, nu, q))
         if q in PART_AT:
             place, rows = PART_AT[q]
@@ -382,103 +375,92 @@
             put(q, 0, 16 - rows, jnp.where(even_x, b, a))
             put(q, 0, 32, jnp.where(even_x, a, b))
     lane = lanes((16, 128))
-    for g, (width, members) in enumerate(GROUPS):
-        if not any(q in planes for q in members):
-            continue
+    for g, members in enumerate(GROUPS):
         cut = slice(16 * g, 16 * g + 16)
-        cut_a = slice(STRIP_AT + 16 * g, STRIP_AT + 16 * g + 16)
-        cut_b = slice(STRIP_AT + STRIPS + 16 * g, STRIP_AT + STRIPS + 16 * g + 16)
-        for first, a, b in (
-            (16, cols_a[cut, :], cols_b[cut, :]),
-            (0, jnp.where(even_x, rows_b[cut_a, :], rows_a[cut_a, :]), jnp.where(even_x, rows_b[cut_b, :], rows_a[cut_b, :])),
-            (32, jnp.where(even_x, rows_a[cut_a, :], rows_b[cut_a, :]), jnp.where(even_x, rows_a[cut_b, :], rows_b[cut_b, :])),
-        ):
+        blocks = [(16, cols_a[cut, :], cols_b[cut, :])]
+        if 16 * g < ROW_STRIPS:
+            cut_a = slice(STRIP_AT + 16 * g, STRIP_AT + 16 * g + 16)
+            cut_b = slice(STRIP_AT + ROW_STRIPS + 16 * g, STRIP_AT + ROW_STRIPS + 16 * g + 16)
+            aa, ab, ba, bb = rows_a[cut_a, :], rows_a[cut_b, :], rows_b[cut_a, :], rows_b[cut_b, :]
+            blocks.append((0, jnp.where(even_x, ba, aa), jnp.where(even_x, bb, ab)))
+            blocks.append((32, jnp.where(even_x, aa, ba), jnp.where(even_x, ab, bb)))
+        for first, a, b in blocks:
             after, before = jnp.where(even_y, a, b), jnp.where(even_y, b, a)
             for slot, q in enumerate(members):
-                if q in planes and (first == 16 or q in PART_AT):
-                    hi, lo = rolled(after, -slot * width), rolled(before, 128 - width - slot * width)
-                    put(q, 1, first, jnp.where(lane < width, hi, jnp.where(lane >= 128 - width, lo, 0.0)))
-
-
-def chain(first_n, last_n, one, two, coef, push, added, at, save):
+                if first == 16 or q in PART_AT:
+                    hi, lo = rolled(after, -slot * WIDTH), rolled(before, 128 - WIDTH - slot * WIDTH)
+                    put(q, 1, first, jnp.where(lane < WIDTH, hi, jnp.where(lane >= 128 - WIDTH, lo, 0.0)))
+
+
+def chain(first_k, one, two, coef, push, extra, kept, at):
     outside, side_mask = edges(at)
-    for n in range(first_n, last_n + 1):
-        def pushed(d, c, r, n=n):
-            return push[n, d, c, r, :]
+
+    for k in range(first_k, HALF):
+        def pushed(d, c, r, k=k):
+            return push[k, d, c, r, :]
+
+        def keep_and_add(f, c, r, value, k=k):
+            if c == 0:
+                kept[k, f, r, :] = value
+            return value + extra[3 * k + f, c, pl.ds(r.start - 8, r.size), :]
 
         for half in range(2):
-            halo = 2 * (last_n - n) + 1 - half
+            halo = 2 * (HALF - 1 - k) + 1 - half
             count = 2 + -(-halo // 4)
             first = min(8 + 16 - halo, 8 + EXT - 8 * count)
             src, dst = (one, two) if half == 0 else (two, one)
-            post = None
-            if half == 1:
-                def post(f, c, r, value, n=n):
-                    return save(n, f, c, r, value, added)
-
-            for k in range(count):
-                advance(src, dst, coef, pushed, 8, first + 8 * k, 8, 2, (0, 1), COARSE, side_mask, post=post)
+            post = keep_and_add if half else None
+            for i in range(count):
+                advance(src, dst, coef, pushed, 8, first + 8 * i, 8, 2, (0, 1), COARSE, side_mask, post=post)
             if halo:
                 clear_rows(dst, 2, 8 + 15, 8 + 32, outside)
 
 
-def with_defect(kept, extra, first_plane, last):
-    def save(n, f, c, r, value, added):
-        if c == 0:
-            kept[n % HALF, f, r, :] = value
-        if n == last:
-            return value
-        return value + extra[3 * n + f - first_plane, c, pl.ds(r.start - 8, r.size), :]
-
-    return save
-
-
-def lower_kernel(at, held, nu, cols_a, cols_b, rows_a, rows_b, push, state, moved, coef, one, two, extra, kept):
-    planes = list(range(3 * HALF)) + [NU]
-
+def low_kernel(at, held, nu, cols_a, cols_b, rows_a, rows_b, push, state, moved, extra, coef, one, two, kept):
     def put(q, c, row, value):
         rows = pl.ds(row, value.shape[0])
         if q == NU:
             coefficients(coef, c, rows, value, COARSE[0])
-        elif q < 3:
-            one[q, c, pl.ds(row + 8, value.shape[0]), :] = value
         else:
-            extra[q - 3, c, rows, :] = value
-
-    assemble(at, planes, held, nu, cols_a, cols_b, rows_a, rows_b, put)
-    chain(1, HALF - 1, one, two, coef, push, extra, at, with_defect(kept, extra, 3, None))
-    for f in range(3):
-        for c in range(2):
-            state[2 * f + c] = one[f, c, 24:40, :]
-    mine = jnp.clip(at[0], 1, HALF - 1)
-    for f in range(3):
-        moved[16 * f : 16 * f + 16, :] = kept[mine, f, 24:40, :]
-
-
-def upper_fields_kernel(at, held, nu, cols_a, cols_b, rows_a, rows_b, extra):
-    planes = list(range(3 * HALF, NU))
-
-    def put(q, c, row, value):
-        extra[q - 3 * HALF, c, pl.ds(row, value.shape[0]), :] = value
-
-    assemble(at, planes, held, nu, cols_a, cols_b, rows_a, rows_b, put)
-
-
-def upper_kernel(at, state, state_a, state_b, extra, coef, push, fine, guess, moved, out, one, two, kept):
+            extra[q, c, rows, :] = value
+
+    assemble(at, held, nu, cols_a, cols_b, rows_a, rows_b, put)
+
+    @pl.when(at[0] < HALF)
+    def _():
+        for f in range(3):
+            for c in range(2):
+                one[f, c, 8:56, :] = extra[f, c]
+        chain(1, one, two, coef, push, extra, kept, at)
+        for f in range(3):
+            for c in range(2):
+                state[2 * f + c] = one[f, c, 24:40, :]
+            moved[16 * f : 16 * f + 16, :] = kept[jnp.maximum(at[0], 1), f, 24:40, :]
+
+
+def high_kernel(at, state, state_a, state_b, extra, coef, push, fine, guess, moved_low, out, one, two, kept, moved):
     even_x = lax.rem(at[1], 2) == 0
-    for f in range(3):
-        for c in range(2):
-            a, b = state_a[2 * f + c], state_b[2 * f + c]
-            one[f, c, 8:24, :] = jnp.where(even_x, b, a)
-            one[f, c, 24:40, :] = state[2 * f + c]
-            one[f, c, 40:56, :] = jnp.where(even_x, a, b)
-    chain(HALF, CUTS - 1, one, two, coef, push, extra, at, with_defect(kept, extra, 3 * HALF, CUTS - 1))
-    mine = jnp.maximum(at[0] - HALF, 0)
+
+    @pl.when(at[0] < HALF)
+    def _():
+        moved[...] = moved_low[...]
+
+    @pl.when(at[0] >= HALF)
+    def _():
+        for f in range(3):
+            for c in range(2):
+                a, b = state_a[2 * f + c], state_b[2 * f + c]
+                one[f, c, 8:24, :] = jnp.where(even_x, b, a)
+                one[f, c, 24:40, :] = state[2 * f + c]
+                one[f, c, 40:56, :] = jnp.where(even_x, a, b)
+        chain(0, one, two, coef, push, extra, kept, at)
+        for f in range(3):
+            moved[16 * f : 16 * f + 16, :] = kept[at[0] - HALF, f, 24:40, :]
+
     parts = []
     for f in range(3):
         cut = slice(16 * f, 16 * f + 16)
-        value = jnp.where(at[0] < HALF, moved[cut, :], kept[mine, f, 24:40, :]) - guess[cut, :]
-        parts.append(jnp.where(at[0] == 0, 0.0, value * (1.0 / COARSE_SCALE[f])))
+        parts.append(jnp.where(at[0] == 0, 0.0, (moved[cut, :] - guess[cut, :]) * (1.0 / COARSE_SCALE[f])))
     change = jnp.concatenate(parts, axis=0)
     i, j = sublanes((3 * ROWS, 48)), lanes((3 * ROWS, 48))
     repeat_rows = jnp.where(i // 4 == j, 1.0, 0.0)
@@ -494,7 +476,7 @@
 ANY = pl.BlockSpec(memory_space=pl.ANY)
 
 
-def call(kernel, args, outs, scratch=(), far=0, sems=0):
+def call(kernel, args, outs, scratch=(), far=0, sems=0, grant=48):
     shapes = [jax.ShapeDtypeStruct(s, F32) for s in outs]
     near = len(args) - 1 - far
     memory = [s if not isinstance(s, tuple) else pltpu.VMEM(s, F32) for s in scratch]
@@ -506,12 +488,17 @@
         in_specs=[SMEM] + [VMEM] * near + [ANY] * far,
         out_specs=[VMEM] * len(shapes),
         scratch_shapes=memory,
-        compiler_params=pltpu.CompilerParams(vmem_limit_bytes=48 * 1024 * 1024),
+        compiler_params=pltpu.CompilerParams(vmem_limit_bytes=grant * 1024 * 1024) if grant else None,
     )(*args)
 
 
 def swap(x, axis, pairs):
     return lax.ppermute(x, axis, [(a, b) for a, b in pairs] + [(b, a) for a, b in pairs])
+
+
+def swap_high(x, count, pairs):
+    both = [(a, b) for a, b in pairs] + [(b, a) for a, b in pairs]
+    return lax.ppermute(x, ("cuts", "sx"), [(n * count + a, n * count + b) for n in range(HALF, CUTS) for a, b in both])
 
 
 def on_device(starts, viscosity, turbine_x, turbine_y, yaw_index):
@@ -529,10 +516,10 @@
     turbine_scratch = [pltpu.VMEM((1, 64), jnp.int32), pltpu.VMEM((1, 64), jnp.int32), pltpu.VMEM((CUTS, 64), jnp.int32)]
 
     edge = (4, 8, COLS)
-    send_a, send_b = call(edge_kernel, (at, start, viscosity), [edge, edge], far=2, sems=4)
+    send_a, send_b = call(edge_kernel, (at, start, viscosity), [edge, edge], far=2, sems=4, grant=0)
     rows_a = swap(send_a, "sx", x_a)
     rows_b = swap(send_b, "sx", x_b)
-    (own,) = call(load_kernel, (at, send_b, start, viscosity), [(4, 4, ROWS, 128)], far=3, sems=8)
+    (own,) = call(load_kernel, (at, send_b, start, viscosity), [(4, 4, ROWS, 128)], far=3, sems=8, grant=0)
     send_a, send_b = call(side_kernel, (at, own, rows_a, rows_b), [(80, 128)] * 2)
     cols_a = swap(send_a, "sy", y_a)
     cols_b = swap(send_b, "sy", y_b)
@@ -541,34 +528,34 @@
     fine, guess, sent, coarse_nu = call(
         fine_kernel,
         (at, own, rows_a, rows_b, cols_a, cols_b, push, own_push),
-        [(3, ROWS, COLS), (48, 128), (CUTS, 48, 128), (CROWS, 128)],
+        [(3, ROWS, COLS), (48, 128), (HALF, 48, 128), (CROWS, 128)],
         [(3, 5, 96, 128), (3, 5, 96, 128), (4, 5, 96, 128), (3, 2, 40, 128), (3, 2, 40, 128), (4, 2, 40, 128)],
     )
-    held = lax.all_to_all(sent, "cuts", 0, 0)
+    halves = [list(range(HALF)), list(range(HALF, CUTS))]
+    held = lax.all_to_all(sent, "cuts", 0, 0, axis_index_groups=halves)
     send_a, send_b = call(cols_kernel, (at, held, coarse_nu), [(STRIPS, 128)] * 2)
     cols_a = swap(send_a, "sy", y_a)
     cols_b = swap(send_b, "sy", y_b)
     (chain_push,) = call(
-        chain_push_kernel, (at, send_b) + turbines, [(CUTS, 2, 2, EXT, 128)], turbine_scratch, far=4, sems=3)
+        chain_push_kernel, (at, send_b) + turbines, [(HALF, 2, 2, EXT, 128)], turbine_scratch, far=4, sems=3)
     send_a, send_b = call(rows_kernel, (at, held, coarse_nu, cols_a, cols_b), [(MESSAGE, 128)] * 2)
     rows_a = swap(send_a, "sx", x_a)
     rows_b = swap(send_b, "sx", x_b)
     blocks = (at, held, coarse_nu, cols_a, cols_b, rows_a, rows_b)
-    planes = 3 * HALF - 3
     field = (3, 2, 64, 128)
-    state, moved, coef = call(
-        lower_kernel, blocks + (chain_push,),
-        [(6, CROWS, 128), (48, 128), (4, 2, EXT, 128)],
-        [field, field, (planes, 2, EXT, 128), (HALF, 3, 64, 128)],
+    state, moved, extra, coef = call(
+        low_kernel, blocks + (chain_push,),
+        [(6, CROWS, 128), (48, 128), (3 * HALF, 2, EXT, 128), (4, 2, EXT, 128)],
+        [field, field, (HALF, 3, 64, 128)],
     )
-    state_a = swap(state, "sx", x_a)
-    state_b = swap(state, "sx", x_b)
-    (extra,) = call(upper_fields_kernel, blocks, [(planes, 2, EXT, 128)])
+    state = lax.ppermute(state, "cuts", [(m, CUTS - 1 - m) for m in range(HALF)])
+    state_a = swap_high(state, count_x, x_a)
+    state_b = swap_high(state, count_x, x_b)
     (out,) = call(
-        upper_kernel,
+        high_kernel,
         (at, state, state_a, state_b, extra, coef, chain_push, fine, guess, moved),
         [(3, ROWS, COLS)],
-        [field, field, (HALF, 3, 64, 128)],
+        [field, field, (HALF, 3, 64, 128), (48, 128)],
     )
     return out[None]
 

time: 95 us -> 86.5 us (0.911)
  the two profiles are of different devices: /device:TPU:17 before, /device:TPU:371 now
where the time goes in v3:
time: 86.5 us; the launch traced here: 85.9 us
  starting transfers between devices  31.9 us (37%)
  waiting for transfers between devices  18.8 us (22%)
  Pallas kernels  17.7 us (20%)
  blocking collectives  14.5 us (17%)
  local copies, waits for them, and re-layouts  2.76 us (3%)
    ppermute x8, starting transfers between devices, swap(): lax.ppermute(x, axis, [(a, b) for a, b in pairs] + [(b, a) for a, b in pa...  24.7 us
    pallas_call x10, Pallas kernels, call(): pl.pallas_call(kernel, out_shape=shapes, in_specs=[SMEM] + [VMEM] * near...  17.7 us
    all_to_all x1, blocking collectives, on_device(): held = lax.all_to_all(sent, 'cuts', 0, 0, axis_index_groups=halves)  14.5 us
    ppermute x1, waiting for transfers between devices, on_device(): lax.ppermute(state, 'cuts', [(m, CUTS - 1 - m) for m in range(HALF)])  10.6 us
    ppermute x8, waiting for transfers between devices, swap(): lax.ppermute(x, axis, [(a, b) for a, b in pairs] + [(b, a) for a, b in pa...  7 us
    ppermute x2, starting transfers between devices, swap_high(): lax.ppermute(x, ('cuts', 'sx'), [(n * count + a, n * count + b) for n in...  5.91 us
    unnamed x12, local copies, waits for them, and re-layouts  2.1 us
  transfers between devices with their start and end apart: 11, of which 8 were waited for; matrix products, arithmetic and copies ran while one was open for 0% of the time, Pallas kernels for 7%

profile of v3, /device:TPU:371, one launch (start us, length us, event | category | flops | bytes accessed | tf_op | source)
XLA Modules:
  0.0 85.9 jit_solution(15786932189813976160)
XLA Ops:
  0.0 0.7 stack.15.at
  0.7 2.3 %shard_map.55 = (f32[4,8,512]{2,1,0:T(8,128)}, f32[4,8,512]{2,1,0:T(8,128)}) custom-call(s32[5]{0:T(128)} %stack.15.at, f32[3,64,512]{2,1,0:T(8,128)} %bitcast.11, f32[64,512]{1,0:T(8,128)} %visc.3), custom_call_target="tpu_custom_call" | custom-call | tf_op jit(solution)/shard_map/pallas_call | solution.py:485
  3.0 2.6 %collective-permute-start = (f32[4,8,512]{2,1,0:T(8,128)}, f32[4,8,512]{2,1,0:T(8,128)S(1)}, u32[]{:S(2)}, u32[]{:S(2)}) collective-permute-start(f32[4,8,512]{2,1,0:T(8,128)} %get-tuple-element.24), channel_id=1, source_target_pairs={{0,4},{8,12},{16,20},{24,28},{4,0},{12,8},{20,16},{28,24},{1,5},{9... | collective-permute-start | bytes 196616 | tf_op jit(solution)/shard_map/ppermute | solution.py:496
  5.6 3.0 %collective-permute-start.1 = (f32[4,8,512]{2,1,0:T(8,128)}, f32[4,8,512]{2,1,0:T(8,128)S(1)}, u32[]{:S(2)}, u32[]{:S(2)}) collective-permute-start(f32[4,8,512]{2,1,0:T(8,128)} %get-tuple-element.23.after), channel_id=1, source_target_pairs={{4,8},{12,16},{20,24},{8,4},{16,12},{24,20},{5,9},{13,17},{21,25},... | collective-permute-start | bytes 196616 | tf_op jit(solution)/shard_map/ppermute | solution.py:496
  8.6 2.6 %shard_map.56.own = f32[4,4,64,128]{3,2,1,0:T(8,128)} custom-call(s32[5]{0:T(128)} %stack.15.at, f32[4,8,512]{2,1,0:T(8,128)} %get-tuple-element.23.after, f32[3,64,512]{2,1,0:T(8,128)} %bitcast.12, f32[64,512]{1,0:T(8,128)} %visc.3), custom_call_target="tpu_custom_call" | custom-call | tf_op jit(solution)/shard_map/pallas_call | solution.py:485
  11.2 0.2 collective-permute-done.1.got_b.rows_b
  11.4 1.0 %copy-done = f32[4,4,64,128]{3,2,1,0:T(8,128)S(1)} copy-done((f32[4,4,64,128]{3,2,1,0:T(8,128)S(1)}, f32[4,4,64,128]{3,2,1,0:T(8,128)}, u32[]{:S(2)}) %copy-start) | copy-done | bytes 524312
  12.4 0.7 shard_map.57
  13.1 2.9 %collective-permute-start.2 = (f32[80,128]{1,0:T(8,128)S(1)}, f32[80,128]{1,0:T(8,128)S(1)}, u32[]{:S(2)}, u32[]{:S(2)}) collective-permute-start(f32[80,128]{1,0:T(8,128)S(1)} %get-tuple-element.25), channel_id=1, source_target_pairs={{0,1},{2,3},{1,0},{3,2},{4,5},{6,7},{5,4},{7,6},{8,9},{10,11},{9,8... | collective-permute-start | bytes 122888 | tf_op jit(solution)/shard_map/ppermute | solution.py:496
  16.1 1.9 %collective-permute-start.3 = (f32[80,128]{1,0:T(8,128)S(1)}, f32[80,128]{1,0:T(8,128)S(1)}, u32[]{:S(2)}, u32[]{:S(2)}) collective-permute-start(f32[80,128]{1,0:T(8,128)S(1)} %get-tuple-element.26.after), channel_id=1, source_target_pairs={{1,2},{2,1},{5,6},{6,5},{9,10},{10,9},{13,14},{14,13},{17,18},{18,... | collective-permute-start | bytes 122888 | tf_op jit(solution)/shard_map/ppermute | solution.py:496
  18.0 1.2 %shard_map.58 = (f32[2,5,96,128]{3,2,1,0:T(8,128)S(1)}, f32[2,2,40,128]{3,2,1,0:T(8,128)S(1)}) custom-call(s32[5]{0:T(128)S(1)} %copy-done.2, f32[80,128]{1,0:T(8,128)S(1)} %get-tuple-element.26.after, s32[1,64]{1,0:T(1,128)S(1)} %bitcast.7, s32[1,64]{1,0:T(1,128)S(1)} %bitcast.9, s32[16,64]{1,0:T(8,128)S(1)} %copy-done.3), custom_call_target="tpu_custom_call" | custom-call | tf_op jit(solution)/shard_map/pallas_call | solution.py:485
  19.2 1.6 %collective-permute-done.3.cols_b = f32[80,128]{1,0:T(8,128)S(1)} collective-permute-done((f32[80,128]{1,0:T(8,128)S(1)}, f32[80,128]{1,0:T(8,128)S(1)}, u32[]{:S(2)}, u32[]{:S(2)}) %collective-permute-start.3) | collective-permute-done | bytes 40992 | tf_op jit(solution)/shard_map/ppermute | solution.py:496
  20.8 1.0 %copy-done.1 = f32[4,4,64,128]{3,2,1,0:T(8,128)S(1)} copy-done((f32[4,4,64,128]{3,2,1,0:T(8,128)S(1)}, f32[4,4,64,128]{3,2,1,0:T(8,128)}, u32[]{:S(2)}) %copy-start.1) | copy-done | bytes 524312
  21.8 3.0 %shard_map.59 = (f32[3,64,512]{2,1,0:T(8,128)S(1)}, f32[48,128]{1,0:T(8,128)S(1)}, f32[8,48,128]{2,1,0:T(8,128)S(1)}, f32[16,128]{1,0:T(8,128)S(1)}) custom-call(s32[5]{0:T(128)S(1)} %copy-done.2, f32[4,4,64,128]{3,2,1,0:T(8,128)S(1)} %copy-done.1, f32[4,8,512]{2,1,0:T(8,128)S(1)} %collective-permute-done.got_a.rows_a, ...), custom_call_target="tpu_custom_call" | custom-call | tf_op jit(solution)/shard_map/pallas_call | solution.py:485
  24.9 14.5 %all_to_all.5.held = f32[8,48,128]{2,1,0:T(8,128)S(1)} all-to-all(f32[8,48,128]{2,1,0:T(8,128)S(1)} %get-tuple-element.29), channel_id=1, replica_groups={{0,32,64,96,128,160,192,224},{256,288,320,352,384,416,448,480},{1,33,65..., dimensions={0} | all-to-all | bytes 393216 | tf_op jit(solution)/shard_map/all_to_all | solution.py:535
  39.3 0.7 shard_map.60
  40.0 1.9 %collective-permute-start.4 = (f32[112,128]{1,0:T(8,128)S(1)}, f32[112,128]{1,0:T(8,128)S(1)}, u32[]{:S(2)}, u32[]{:S(2)}) collective-permute-start(f32[112,128]{1,0:T(8,128)S(1)} %get-tuple-element.31), channel_id=1, source_target_pairs={{0,1},{2,3},{1,0},{3,2},{4,5},{6,7},{5,4},{7,6},{8,9},{10,11},{9,8... | collective-permute-start | bytes 172040 | tf_op jit(solution)/shard_map/ppermute | solution.py:496
  42.0 2.1 %collective-permute-start.5 = (f32[112,128]{1,0:T(8,128)S(1)}, f32[112,128]{1,0:T(8,128)S(1)}, u32[]{:S(2)}, u32[]{:S(2)}) collective-permute-start(f32[112,128]{1,0:T(8,128)S(1)} %get-tuple-element.32.after), channel_id=1, source_target_pairs={{1,2},{2,1},{5,6},{6,5},{9,10},{10,9},{13,14},{14,13},{17,18},{18,... | collective-permute-start | bytes 172040 | tf_op jit(solution)/shard_map/ppermute | solution.py:496
  44.1 0.8 collective-permute-done.4.cols_a
  45.0 1.9 %collective-permute-done.5.cols_b = f32[112,128]{1,0:T(8,128)S(1)} collective-permute-done((f32[112,128]{1,0:T(8,128)S(1)}, f32[112,128]{1,0:T(8,128)S(1)}, u32[]{:S(2)}, u32[]{:S(2)}) %collective-permute-start.5) | collective-permute-done | bytes 57376 | tf_op jit(solution)/shard_map/ppermute | solution.py:496
  46.9 0.6 shard_map.61
  47.5 7.2 %collective-permute-start.6 = (f32[448,128]{1,0:T(8,128)S(1)}, f32[448,128]{1,0:T(8,128)S(1)}, u32[]{:S(2)}, u32[]{:S(2)}) collective-permute-start(f32[448,128]{1,0:T(8,128)S(1)} %get-tuple-element.33), channel_id=1, source_target_pairs={{0,4},{8,12},{16,20},{24,28},{4,0},{12,8},{20,16},{28,24},{1,5},{9... | collective-permute-start | bytes 688136 | tf_op jit(solution)/shard_map/ppermute | solution.py:496
  54.7 3.0 %collective-permute-start.7 = (f32[448,128]{1,0:T(8,128)S(1)}, f32[448,128]{1,0:T(8,128)S(1)}, u32[]{:S(2)}, u32[]{:S(2)}) collective-permute-start(f32[448,128]{1,0:T(8,128)S(1)} %get-tuple-element.34), channel_id=1, source_target_pairs={{4,8},{12,16},{20,24},{8,4},{16,12},{24,20},{5,9},{13,17},{21,25},... | collective-permute-start | bytes 688136 | tf_op jit(solution)/shard_map/ppermute | solution.py:496
  57.7 1.8 %shard_map.62.push = f32[8,2,2,48,128]{4,3,2,1,0:T(8,128)S(1)} custom-call(s32[5]{0:T(128)S(1)} %copy-done.2, f32[112,128]{1,0:T(8,128)S(1)} %get-tuple-element.32.after, s32[1,64]{1,0:T(1,128)S(1)} %bitcast.8, s32[1,64]{1,0:T(1,128)S(1)} %bitcast.10, s32[16,64]{1,0:T(8,128)S(1)} %copy-done.3), custom_call_target="tpu_custom_call" | custom-call | tf_op jit(solution)/shard_map/pallas_call | solution.py:485
  59.6 2.5 %collective-permute-done.7.rows_b = f32[448,128]{1,0:T(8,128)S(1)} collective-permute-done((f32[448,128]{1,0:T(8,128)S(1)}, f32[448,128]{1,0:T(8,128)S(1)}, u32[]{:S(2)}, u32[]{:S(2)}) %collective-permute-start.7) | collective-permute-done | bytes 229408 | tf_op jit(solution)/shard_map/ppermute | solution.py:496
  62.0 0.8 shard_map.63
  62.9 1.3 %collective-permute-start.8 = (f32[6,16,128]{2,1,0:T(8,128)S(1)}, f32[6,16,128]{2,1,0:T(8,128)S(1)}, u32[]{:S(2)}, u32[]{:S(2)}) collective-permute-start(f32[6,16,128]{2,1,0:T(8,128)S(1)} %get-tuple-element.35), channel_id=1, source_target_pairs={{0,480},{32,448},{64,416},{96,384},{128,352},{160,320},{192,288},{... | collective-permute-start | bytes 147464 | tf_op jit(solution)/shard_map/ppermute | solution.py:551
  64.2 10.6 %collective-permute-done.8.state = f32[6,16,128]{2,1,0:T(8,128)S(1)} collective-permute-done((f32[6,16,128]{2,1,0:T(8,128)S(1)}, f32[6,16,128]{2,1,0:T(8,128)S(1)}, u32[]{:S(2)}, u32[]{:S(2)}) %collective-permute-start.8) | collective-permute-done | bytes 49184 | tf_op jit(solution)/shard_map/ppermute | solution.py:551
  74.7 4.0 %collective-permute-start.10 = (f32[6,16,128]{2,1,0:T(8,128)S(1)}, f32[6,16,128]{2,1,0:T(8,128)S(1)}, u32[]{:S(2)}, u32[]{:S(2)}) collective-permute-start(f32[6,16,128]{2,1,0:T(8,128)S(1)} %collective-permute-done.8.state), channel_id=1, source_target_pairs={{260,264},{268,272},{276,280},{264,260},{272,268},{280,276},{292,2... | collective-permute-start | bytes 147464 | tf_op jit(solution)/shard_map/ppermute | solution.py:501
  78.7 1.9 %collective-permute-start.9 = (f32[6,16,128]{2,1,0:T(8,128)S(1)}, f32[6,16,128]{2,1,0:T(8,128)S(1)}, u32[]{:S(2)}, u32[]{:S(2)}) collective-permute-start(f32[6,16,128]{2,1,0:T(8,128)S(1)} %collective-permute-done.8.state), channel_id=1, source_target_pairs={{256,260},{264,268},{272,276},{280,284},{260,256},{268,264},{276,2... | collective-permute-start | bytes 147464 | tf_op jit(solution)/shard_map/ppermute | solution.py:501
  80.7 1.1 %collective-permute-done.9.state_a = f32[6,16,128]{2,1,0:T(8,128)S(1)} collective-permute-done((f32[6,16,128]{2,1,0:T(8,128)S(1)}, f32[6,16,128]{2,1,0:T(8,128)S(1)}, u32[]{:S(2)}, u32[]{:S(2)}) %collective-permute-start.9) | collective-permute-done | bytes 49184 | tf_op jit(solution)/shard_map/ppermute | solution.py:501
  81.9 4.0 %shard_map.64 = f32[3,64,512]{2,1,0:T(8,128)} custom-call(s32[5]{0:T(128)S(1)} %copy-done.2, f32[6,16,128]{2,1,0:T(8,128)S(1)} %collective-permute-done.8.state, f32[6,16,128]{2,1,0:T(8,128)S(1)} %collective-permute-done.9.state_a, f32[6,16,128]{2,1,0:T(8,128)S(1)} %collective-permute-done.10.state_b, f32[24,2,48,128]{3,2,1,0:T(8,128)S(1)} %get-tuple-element.36.extra, ...), custom_call_target="tpu_custom_call" | custom-call | tf_op jit(solution)/shard_map/pallas_call | solution.py:485
  (14 shorter events, 0.1 us)
Async XLA Ops:
  0.0 18.0 %copy-start.3 = (s32[16,64]{1,0:T(8,128)S(1)}, s32[16,64]{1,0:T(8,128)}, u32[]{:S(2)}) copy-start(s32[16,64]{1,0:T(8,128)} %yaw_in.3) | copy-start | bytes 12292
  0.0 18.0 %copy-start.5 = (s32[64]{0:T(128)S(1)}, s32[64]{0:T(128)}, u32[]{:S(2)}) copy-start(s32[64]{0:T(128)} %param.8) | copy-start | bytes 772
  0.0 18.0 %copy-start.4 = (s32[64]{0:T(128)S(1)}, s32[64]{0:T(128)}, u32[]{:S(2)}) copy-start(s32[64]{0:T(128)} %param.7) | copy-start | bytes 772
  0.7 10.7 %copy-start.2 = (s32[5]{0:T(128)S(1)}, s32[5]{0:T(128)}, u32[]{:S(2)}) copy-start(s32[5]{0:T(128)} %stack.15.at) | copy-start | bytes 64
  3.0 8.2 %collective-permute-start = (f32[4,8,512]{2,1,0:T(8,128)}, f32[4,8,512]{2,1,0:T(8,128)S(1)}, u32[]{:S(2)}, u32[]{:S(2)}) collective-permute-start(f32[4,8,512]{2,1,0:T(8,128)} %get-tuple-element.24), channel_id=1, source_target_pairs={{0,4},{8,12},{16,20},{24,28},{4,0},{12,8},{20,16},{28,24},{1,5},{9... | collective-permute-start | bytes 196616 | tf_op jit(solution)/shard_map/ppermute | solution.py:496
  5.6 5.8 %collective-permute-start.1 = (f32[4,8,512]{2,1,0:T(8,128)}, f32[4,8,512]{2,1,0:T(8,128)S(1)}, u32[]{:S(2)}, u32[]{:S(2)}) collective-permute-start(f32[4,8,512]{2,1,0:T(8,128)} %get-tuple-element.23.after), channel_id=1, source_target_pairs={{4,8},{12,16},{20,24},{8,4},{16,12},{24,20},{5,9},{13,17},{21,25},... | collective-permute-start | bytes 196616 | tf_op jit(solution)/shard_map/ppermute | solution.py:496
  11.4 1.0 %copy-start = (f32[4,4,64,128]{3,2,1,0:T(8,128)S(1)}, f32[4,4,64,128]{3,2,1,0:T(8,128)}, u32[]{:S(2)}) copy-start(f32[4,4,64,128]{3,2,1,0:T(8,128)} %shard_map.56.own) | copy-start | bytes 1572868
  13.1 6.1 %collective-permute-start.2 = (f32[80,128]{1,0:T(8,128)S(1)}, f32[80,128]{1,0:T(8,128)S(1)}, u32[]{:S(2)}, u32[]{:S(2)}) collective-permute-start(f32[80,128]{1,0:T(8,128)S(1)} %get-tuple-element.25), channel_id=1, source_target_pairs={{0,1},{2,3},{1,0},{3,2},{4,5},{6,7},{5,4},{7,6},{8,9},{10,11},{9,8... | collective-permute-start | bytes 122888 | tf_op jit(solution)/shard_map/ppermute | solution.py:496
  16.1 4.7 %collective-permute-start.3 = (f32[80,128]{1,0:T(8,128)S(1)}, f32[80,128]{1,0:T(8,128)S(1)}, u32[]{:S(2)}, u32[]{:S(2)}) collective-permute-start(f32[80,128]{1,0:T(8,128)S(1)} %get-tuple-element.26.after), channel_id=1, source_target_pairs={{1,2},{2,1},{5,6},{6,5},{9,10},{10,9},{13,14},{14,13},{17,18},{18,... | collective-permute-start | bytes 122888 | tf_op jit(solution)/shard_map/ppermute | solution.py:496
  20.8 1.0 %copy-start.1 = (f32[4,4,64,128]{3,2,1,0:T(8,128)S(1)}, f32[4,4,64,128]{3,2,1,0:T(8,128)}, u32[]{:S(2)}) copy-start(f32[4,4,64,128]{3,2,1,0:T(8,128)} %shard_map.56.own) | copy-start | bytes 1572868
  40.0 4.9 %collective-permute-start.4 = (f32[112,128]{1,0:T(8,128)S(1)}, f32[112,128]{1,0:T(8,128)S(1)}, u32[]{:S(2)}, u32[]{:S(2)}) collective-permute-start(f32[112,128]{1,0:T(8,128)S(1)} %get-tuple-element.31), channel_id=1, source_target_pairs={{0,1},{2,3},{1,0},{3,2},{4,5},{6,7},{5,4},{7,6},{8,9},{10,11},{9,8... | collective-permute-start | bytes 172040 | tf_op jit(solution)/shard_map/ppermute | solution.py:496
  42.0 4.9 %collective-permute-start.5 = (f32[112,128]{1,0:T(8,128)S(1)}, f32[112,128]{1,0:T(8,128)S(1)}, u32[]{:S(2)}, u32[]{:S(2)}) collective-permute-start(f32[112,128]{1,0:T(8,128)S(1)} %get-tuple-element.32.after), channel_id=1, source_target_pairs={{1,2},{2,1},{5,6},{6,5},{9,10},{10,9},{13,14},{14,13},{17,18},{18,... | collective-permute-start | bytes 172040 | tf_op jit(solution)/shard_map/ppermute | solution.py:496
  47.5 12.1 %collective-permute-start.6 = (f32[448,128]{1,0:T(8,128)S(1)}, f32[448,128]{1,0:T(8,128)S(1)}, u32[]{:S(2)}, u32[]{:S(2)}) collective-permute-start(f32[448,128]{1,0:T(8,128)S(1)} %get-tuple-element.33), channel_id=1, source_target_pairs={{0,4},{8,12},{16,20},{24,28},{4,0},{12,8},{20,16},{28,24},{1,5},{9... | collective-permute-start | bytes 688136 | tf_op jit(solution)/shard_map/ppermute | solution.py:496
  54.7 7.3 %collective-permute-start.7 = (f32[448,128]{1,0:T(8,128)S(1)}, f32[448,128]{1,0:T(8,128)S(1)}, u32[]{:S(2)}, u32[]{:S(2)}) collective-permute-start(f32[448,128]{1,0:T(8,128)S(1)} %get-tuple-element.34), channel_id=1, source_target_pairs={{4,8},{12,16},{20,24},{8,4},{16,12},{24,20},{5,9},{13,17},{21,25},... | collective-permute-start | bytes 688136 | tf_op jit(solution)/shard_map/ppermute | solution.py:496
  62.9 11.9 %collective-permute-start.8 = (f32[6,16,128]{2,1,0:T(8,128)S(1)}, f32[6,16,128]{2,1,0:T(8,128)S(1)}, u32[]{:S(2)}, u32[]{:S(2)}) collective-permute-start(f32[6,16,128]{2,1,0:T(8,128)S(1)} %get-tuple-element.35), channel_id=1, source_target_pairs={{0,480},{32,448},{64,416},{96,384},{128,352},{160,320},{192,288},{... | collective-permute-start | bytes 147464 | tf_op jit(solution)/shard_map/ppermute | solution.py:551
  74.7 6.0 %collective-permute-start.10 = (f32[6,16,128]{2,1,0:T(8,128)S(1)}, f32[6,16,128]{2,1,0:T(8,128)S(1)}, u32[]{:S(2)}, u32[]{:S(2)}) collective-permute-start(f32[6,16,128]{2,1,0:T(8,128)S(1)} %collective-permute-done.8.state), channel_id=1, source_target_pairs={{260,264},{268,272},{276,280},{264,260},{272,268},{280,276},{292,2... | collective-permute-start | bytes 147464 | tf_op jit(solution)/shard_map/ppermute | solution.py:501
  78.7 3.1 %collective-permute-start.9 = (f32[6,16,128]{2,1,0:T(8,128)S(1)}, f32[6,16,128]{2,1,0:T(8,128)S(1)}, u32[]{:S(2)}, u32[]{:S(2)}) collective-permute-start(f32[6,16,128]{2,1,0:T(8,128)S(1)} %collective-permute-done.8.state), channel_id=1, source_target_pairs={{256,260},{264,268},{272,276},{280,284},{260,256},{268,264},{276,2... | collective-permute-start | bytes 147464 | tf_op jit(solution)/shard_map/ppermute | solution.py:501

commit v4 on v3

--- a/solution.py
+++ b/solution.py
@@ -149,21 +149,18 @@
         copy.wait()
 
 
-def edge_kernel(at, start, visc, send_a, send_b, sems):
+def open_kernel(at, start, visc, send_a, send_b, own, sems):
     last = pl.multiple_of(56 * (1 - lax.rem(at[1], 2)), 8)
     first = pl.multiple_of(56 * lax.rem(at[1], 2), 8)
-    fetch([
-        (start.at[:, pl.ds(last, 8), :], send_a.at[0:3]),
-        (visc.at[pl.ds(last, 8), :], send_a.at[3]),
-        (start.at[:, pl.ds(first, 8), :], send_b.at[0:3]),
-        (visc.at[pl.ds(first, 8), :], send_b.at[3]),
-    ], sems)
-
-
-def load_kernel(at, after, start, visc, out, sems):
     fetch(
-        [(start.at[:, :, 128 * c : 128 * c + 128], out.at[0:3, c]) for c in range(4)]
-        + [(visc.at[:, 128 * c : 128 * c + 128], out.at[3, c]) for c in range(4)],
+        [
+            (start.at[:, pl.ds(last, 8), :], send_a.at[0:3]),
+            (visc.at[pl.ds(last, 8), :], send_a.at[3]),
+            (start.at[:, pl.ds(first, 8), :], send_b.at[0:3]),
+            (visc.at[pl.ds(first, 8), :], send_b.at[3]),
+        ]
+        + [(start.at[:, :, 128 * c : 128 * c + 128], own.at[0:3, c]) for c in range(4)]
+        + [(visc.at[:, 128 * c : 128 * c + 128], own.at[3, c]) for c in range(4)],
         sems,
     )
 
@@ -206,7 +203,7 @@
 LAST_DIMS = (((1,), (1,)), ((), ()))
 
 
-def push_kernel(at, after, tx_in, ty_in, yaw_in, fine_push, own_push, tx_ref, ty_ref, yaw_ref, sems):
+def push_kernel(at, tx_in, ty_in, yaw_in, fine_push, own_push, tx_ref, ty_ref, yaw_ref, sems):
     fetch([(tx_in, tx_ref), (ty_in, ty_ref), (yaw_in, yaw_ref)], sems)
     tx, ty = tx_ref[...], ty_ref[...]
     mine = sublanes((CUTS, 64)) == at[0]
@@ -228,7 +225,7 @@
         own_push[1, c] = push[40:80]
 
 
-def chain_push_kernel(at, after, tx_in, ty_in, yaw_in, push, tx_ref, ty_ref, yaw_ref, sems):
+def chain_push_kernel(at, tx_in, ty_in, yaw_in, push, tx_ref, ty_ref, yaw_ref, sems):
     fetch([(tx_in, tx_ref), (ty_in, ty_ref), (yaw_in, yaw_ref)], sems)
     tx, ty = tx_ref[...], ty_ref[...]
     row = at[1] * CROWS - 16 + sublanes((EXT, 64))
@@ -432,9 +429,13 @@
             for c in range(2):
                 one[f, c, 8:56, :] = extra[f, c]
         chain(1, one, two, coef, push, extra, kept, at)
-        for f in range(3):
-            for c in range(2):
-                state[2 * f + c] = one[f, c, 24:40, :]
+        lane = lanes((CROWS, 128))
+        sides = jnp.zeros((CROWS, 128), F32)
+        for f in range(3):
+            state[16 * f : 16 * f + 16, :] = one[f, 0, 24:40, :]
+            sides = jnp.where(lane // 32 == f, rolled(one[f, 1, 24:40, :], 16 + 32 * f), sides)
+        state[48:64, :] = sides
+        for f in range(3):
             moved[16 * f : 16 * f + 16, :] = kept[jnp.maximum(at[0], 1), f, 24:40, :]
 
 
@@ -447,12 +448,13 @@
 
     @pl.when(at[0] >= HALF)
     def _():
-        for f in range(3):
-            for c in range(2):
-                a, b = state_a[2 * f + c], state_b[2 * f + c]
-                one[f, c, 8:24, :] = jnp.where(even_x, b, a)
-                one[f, c, 24:40, :] = state[2 * f + c]
-                one[f, c, 40:56, :] = jnp.where(even_x, a, b)
+        lane = lanes((CROWS, 128))
+        a, b = state_a[...], state_b[...]
+        for row, block in ((8, jnp.where(even_x, b, a)), (24, state[...]), (40, jnp.where(even_x, a, b))):
+            for f in range(3):
+                one[f, 0, row : row + 16, :] = block[16 * f : 16 * f + 16]
+                side = rolled(block[48:64], -(16 + 32 * f))
+                one[f, 1, row : row + 16, :] = jnp.where((lane < 16) | (lane >= 112), side, 0.0)
         chain(0, one, two, coef, push, extra, kept, at)
         for f in range(3):
             moved[16 * f : 16 * f + 16, :] = kept[at[0] - HALF, f, 24:40, :]
@@ -473,10 +475,10 @@
 
 SMEM = pl.BlockSpec(memory_space=pltpu.SMEM)
 VMEM = pl.BlockSpec(memory_space=pltpu.VMEM)
-ANY = pl.BlockSpec(memory_space=pl.ANY)
-
-
-def call(kernel, args, outs, scratch=(), far=0, sems=0, grant=48):
+HBM = pl.BlockSpec(memory_space=pltpu.HBM)
+
+
+def call(kernel, args, outs, scratch=(), far=0, sems=0):
     shapes = [jax.ShapeDtypeStruct(s, F32) for s in outs]
     near = len(args) - 1 - far
     memory = [s if not isinstance(s, tuple) else pltpu.VMEM(s, F32) for s in scratch]
@@ -485,10 +487,10 @@
     return pl.pallas_call(
         kernel,
         out_shape=shapes,
-        in_specs=[SMEM] + [VMEM] * near + [ANY] * far,
+        in_specs=[SMEM] + [VMEM] * near + [HBM] * far,
         out_specs=[VMEM] * len(shapes),
         scratch_shapes=memory,
-        compiler_params=pltpu.CompilerParams(vmem_limit_bytes=grant * 1024 * 1024) if grant else None,
+        compiler_params=pltpu.CompilerParams(vmem_limit_bytes=48 * 1024 * 1024),
     )(*args)
 
 
@@ -516,15 +518,15 @@
     turbine_scratch = [pltpu.VMEM((1, 64), jnp.int32), pltpu.VMEM((1, 64), jnp.int32), pltpu.VMEM((CUTS, 64), jnp.int32)]
 
     edge = (4, 8, COLS)
-    send_a, send_b = call(edge_kernel, (at, start, viscosity), [edge, edge], far=2, sems=4, grant=0)
+    send_a, send_b, own = call(
+        open_kernel, (at, start, viscosity), [edge, edge, (4, 4, ROWS, 128)], far=2, sems=12)
     rows_a = swap(send_a, "sx", x_a)
     rows_b = swap(send_b, "sx", x_b)
-    (own,) = call(load_kernel, (at, send_b, start, viscosity), [(4, 4, ROWS, 128)], far=3, sems=8, grant=0)
     send_a, send_b = call(side_kernel, (at, own, rows_a, rows_b), [(80, 128)] * 2)
     cols_a = swap(send_a, "sy", y_a)
     cols_b = swap(send_b, "sy", y_b)
     push, own_push = call(
-        push_kernel, (at, send_b) + turbines, [(2, 5, 96, 128), (2, 2, 40, 128)], turbine_scratch, far=4, sems=3)
+        push_kernel, (at,) + turbines, [(2, 5, 96, 128), (2, 2, 40, 128)], turbine_scratch, far=3, sems=3)
     fine, guess, sent, coarse_nu = call(
         fine_kernel,
         (at, own, rows_a, rows_b, cols_a, cols_b, push, own_push),
@@ -537,7 +539,7 @@
     cols_a = swap(send_a, "sy", y_a)
     cols_b = swap(send_b, "sy", y_b)
     (chain_push,) = call(
-        chain_push_kernel, (at, send_b) + turbines, [(HALF, 2, 2, EXT, 128)], turbine_scratch, far=4, sems=3)
+        chain_push_kernel, (at,) + turbines, [(HALF, 2, 2, EXT, 128)], turbine_scratch, far=3, sems=3)
     send_a, send_b = call(rows_kernel, (at, held, coarse_nu, cols_a, cols_b), [(MESSAGE, 128)] * 2)
     rows_a = swap(send_a, "sx", x_a)
     rows_b = swap(send_b, "sx", x_b)
@@ -545,10 +547,10 @@
     field = (3, 2, 64, 128)
     state, moved, extra, coef = call(
         low_kernel, blocks + (chain_push,),
-        [(6, CROWS, 128), (48, 128), (3 * HALF, 2, EXT, 128), (4, 2, EXT, 128)],
+        [(64, 128), (48, 128), (3 * HALF, 2, EXT, 128), (4, 2, EXT, 128)],
         [field, field, (HALF, 3, 64, 128)],
     )
-    state = lax.ppermute(state, "cuts", [(m, CUTS - 1 - m) for m in range(HALF)])
+    state = lax.ppermute(state, "cuts", [(m, (m + 4 if m >= 4 else m + 12)) for m in range(HALF)])
     state_a = swap_high(state, count_x, x_a)
     state_b = swap_high(state, count_x, x_b)
     (out,) = call(

time: 86.5 us -> 82.6 us (0.955)
  the two profiles are of different devices: /device:TPU:371 before, /device:TPU:305 now
where the time goes in v4:
time: 82.6 us; the launch traced here: 82.2 us
  starting transfers between devices  31.4 us (38%)
  waiting for transfers between devices  17.5 us (21%)
  blocking collectives  17.2 us (21%)
  Pallas kernels  13.8 us (17%)
  local copies, waits for them, and re-layouts  2 us (2%)
    ppermute x8, starting transfers between devices, swap(): lax.ppermute(x, axis, [(a, b) for a, b in pairs] + [(b, a) for a, b in pa...  23.2 us
    all_to_all x1, blocking collectives, on_device(): held = lax.all_to_all(sent, 'cuts', 0, 0, axis_index_groups=halves)  17.2 us
    pallas_call x9, Pallas kernels, call(): pl.pallas_call(kernel, out_shape=shapes, in_specs=[SMEM] + [VMEM] * near...  13.8 us
    ppermute x8, waiting for transfers between devices, swap(): lax.ppermute(x, axis, [(a, b) for a, b in pairs] + [(b, a) for a, b in pa...  8.98 us
    ppermute x1, waiting for transfers between devices, on_device(): lax.ppermute(state, 'cuts', [(m, m + 4 if m >= 4 else m + 12) for m in ra...  7.35 us
    ppermute x2, starting transfers between devices, swap_high(): lax.ppermute(x, ('cuts', 'sx'), [(n * count + a, n * count + b) for n in...  6.93 us
    unnamed x10, local copies, waits for them, and re-layouts  1.91 us
  transfers between devices with their start and end apart: 11, of which 7 were waited for; matrix products, arithmetic and copies ran while one was open for 0% of the time, Pallas kernels for 4%

profile of v4, /device:TPU:305, one launch (start us, length us, event | category | flops | bytes accessed | tf_op | source)
XLA Modules:
  0.0 82.2 jit_solution(182421427280930108)
XLA Ops:
  0.0 0.1 stack.15.at
  0.1 1.0 %copy-done = f32[1,3,64,512]{3,2,1,0:T(8,128)S(1)} copy-done((f32[1,3,64,512]{3,2,1,0:T(8,128)S(1)}, f32[1,3,64,512]{3,2,1,0:T(8,128)}, u32[]{:S(2)}) %copy-start) | copy-done | bytes 393240
  1.1 0.9 %copy-done.1 = f32[64,512]{1,0:T(8,128)S(1)} copy-done((f32[64,512]{1,0:T(8,128)S(1)}, f32[64,512]{1,0:T(8,128)}, u32[]{:S(2)}) %copy-start.1) | copy-done | bytes 131096
  2.0 0.8 %shard_map.55 = (f32[4,8,512]{2,1,0:T(8,128)S(1)}, f32[4,8,512]{2,1,0:T(8,128)S(1)}, f32[4,4,64,128]{3,2,1,0:T(8,128)S(1)}) custom-call(s32[5]{0:T(128)S(1)} %stack.15.at, f32[3,64,512]{2,1,0:T(8,128)S(1)} %bitcast.7, f32[64,512]{1,0:T(8,128)S(1)} %copy-done.1), custom_call_target="tpu_custom_call" | custom-call | tf_op jit(solution)/shard_map/pallas_call | solution.py:487
  2.9 2.6 %collective-permute-start = (f32[4,8,512]{2,1,0:T(8,128)S(1)}, f32[4,8,512]{2,1,0:T(8,128)S(1)}, u32[]{:S(2)}, u32[]{:S(2)}) collective-permute-start(f32[4,8,512]{2,1,0:T(8,128)S(1)} %get-tuple-element.25), channel_id=1, source_target_pairs={{0,4},{8,12},{16,20},{24,28},{4,0},{12,8},{20,16},{28,24},{1,5},{9... | collective-permute-start | bytes 196616 | tf_op jit(solution)/shard_map/ppermute | solution.py:498
  5.4 3.0 %collective-permute-start.1 = (f32[4,8,512]{2,1,0:T(8,128)S(1)}, f32[4,8,512]{2,1,0:T(8,128)S(1)}, u32[]{:S(2)}, u32[]{:S(2)}) collective-permute-start(f32[4,8,512]{2,1,0:T(8,128)S(1)} %get-tuple-element.26), channel_id=1, source_target_pairs={{4,8},{12,16},{20,24},{8,4},{16,12},{24,20},{5,9},{13,17},{21,25},... | collective-permute-start | bytes 196616 | tf_op jit(solution)/shard_map/ppermute | solution.py:498
  8.5 2.5 %collective-permute-done.1.got_b.rows_b = f32[4,8,512]{2,1,0:T(8,128)S(1)} collective-permute-done((f32[4,8,512]{2,1,0:T(8,128)S(1)}, f32[4,8,512]{2,1,0:T(8,128)S(1)}, u32[]{:S(2)}, u32[]{:S(2)}) %collective-permute-start.1) | collective-permute-done | bytes 65568 | tf_op jit(solution)/shard_map/ppermute | solution.py:498
  11.0 0.7 shard_map.56
  11.7 2.9 %collective-permute-start.2 = (f32[80,128]{1,0:T(8,128)S(1)}, f32[80,128]{1,0:T(8,128)S(1)}, u32[]{:S(2)}, u32[]{:S(2)}) collective-permute-start(f32[80,128]{1,0:T(8,128)S(1)} %get-tuple-element.27), channel_id=1, source_target_pairs={{0,1},{2,3},{1,0},{3,2},{4,5},{6,7},{5,4},{7,6},{8,9},{10,11},{9,8... | collective-permute-start | bytes 122888 | tf_op jit(solution)/shard_map/ppermute | solution.py:498
  14.6 1.9 %collective-permute-start.3 = (f32[80,128]{1,0:T(8,128)S(1)}, f32[80,128]{1,0:T(8,128)S(1)}, u32[]{:S(2)}, u32[]{:S(2)}) collective-permute-start(f32[80,128]{1,0:T(8,128)S(1)} %get-tuple-element.28), channel_id=1, source_target_pairs={{1,2},{2,1},{5,6},{6,5},{9,10},{10,9},{13,14},{14,13},{17,18},{18,... | collective-permute-start | bytes 122888 | tf_op jit(solution)/shard_map/ppermute | solution.py:498
  16.6 1.2 %shard_map.57 = (f32[2,5,96,128]{3,2,1,0:T(8,128)S(1)}, f32[2,2,40,128]{3,2,1,0:T(8,128)S(1)}) custom-call(s32[5]{0:T(128)S(1)} %stack.15.at, s32[1,64]{1,0:T(1,128)S(1)} %bitcast.8, s32[1,64]{1,0:T(1,128)S(1)} %bitcast.10, s32[16,64]{1,0:T(8,128)S(1)} %copy-done.2), custom_call_target="tpu_custom_call" | custom-call | tf_op jit(solution)/shard_map/pallas_call | solution.py:487
  17.8 0.0 collective-permute-done.2.cols_a
  17.8 1.6 %collective-permute-done.3.cols_b = f32[80,128]{1,0:T(8,128)S(1)} collective-permute-done((f32[80,128]{1,0:T(8,128)S(1)}, f32[80,128]{1,0:T(8,128)S(1)}, u32[]{:S(2)}, u32[]{:S(2)}) %collective-permute-start.3) | collective-permute-done | bytes 40992 | tf_op jit(solution)/shard_map/ppermute | solution.py:498
  19.4 3.0 %shard_map.58 = (f32[3,64,512]{2,1,0:T(8,128)S(1)}, f32[48,128]{1,0:T(8,128)S(1)}, f32[8,48,128]{2,1,0:T(8,128)S(1)}, f32[16,128]{1,0:T(8,128)S(1)}) custom-call(s32[5]{0:T(128)S(1)} %stack.15.at, f32[4,4,64,128]{3,2,1,0:T(8,128)S(1)} %get-tuple-element.24.own, f32[4,8,512]{2,1,0:T(8,128)S(1)} %collective-permute-done.got_a.rows_a, ...), custom_call_target="tpu_custom_call" | custom-call | tf_op jit(solution)/shard_map/pallas_call | solution.py:487
  22.4 17.2 %all_to_all.5.held = f32[8,48,128]{2,1,0:T(8,128)S(1)} all-to-all(f32[8,48,128]{2,1,0:T(8,128)S(1)} %get-tuple-element.31), channel_id=1, replica_groups={{0,32,64,96,128,160,192,224},{256,288,320,352,384,416,448,480},{1,33,65..., dimensions={0} | all-to-all | bytes 393216 | tf_op jit(solution)/shard_map/all_to_all | solution.py:537
  39.6 0.7 shard_map.59
  40.3 1.9 %collective-permute-start.4 = (f32[112,128]{1,0:T(8,128)S(1)}, f32[112,128]{1,0:T(8,128)S(1)}, u32[]{:S(2)}, u32[]{:S(2)}) collective-permute-start(f32[112,128]{1,0:T(8,128)S(1)} %get-tuple-element.33), channel_id=1, source_target_pairs={{0,1},{2,3},{1,0},{3,2},{4,5},{6,7},{5,4},{7,6},{8,9},{10,11},{9,8... | collective-permute-start | bytes 172040 | tf_op jit(solution)/shard_map/ppermute | solution.py:498
  42.2 1.9 %collective-permute-start.5 = (f32[112,128]{1,0:T(8,128)S(1)}, f32[112,128]{1,0:T(8,128)S(1)}, u32[]{:S(2)}, u32[]{:S(2)}) collective-permute-start(f32[112,128]{1,0:T(8,128)S(1)} %get-tuple-element.34), channel_id=1, source_target_pairs={{1,2},{2,1},{5,6},{6,5},{9,10},{10,9},{13,14},{14,13},{17,18},{18,... | collective-permute-start | bytes 172040 | tf_op jit(solution)/shard_map/ppermute | solution.py:498
  44.2 1.1 %collective-permute-done.4.cols_a = f32[112,128]{1,0:T(8,128)S(1)} collective-permute-done((f32[112,128]{1,0:T(8,128)S(1)}, f32[112,128]{1,0:T(8,128)S(1)}, u32[]{:S(2)}, u32[]{:S(2)}) %collective-permute-start.4) | collective-permute-done | bytes 57376 | tf_op jit(solution)/shard_map/ppermute | solution.py:498
  45.2 1.9 %collective-permute-done.5.cols_b = f32[112,128]{1,0:T(8,128)S(1)} collective-permute-done((f32[112,128]{1,0:T(8,128)S(1)}, f32[112,128]{1,0:T(8,128)S(1)}, u32[]{:S(2)}, u32[]{:S(2)}) %collective-permute-start.5) | collective-permute-done | bytes 57376 | tf_op jit(solution)/shard_map/ppermute | solution.py:498
  47.2 0.6 shard_map.60
  47.7 1.9 %collective-permute-start.6 = (f32[448,128]{1,0:T(8,128)S(1)}, f32[448,128]{1,0:T(8,128)S(1)}, u32[]{:S(2)}, u32[]{:S(2)}) collective-permute-start(f32[448,128]{1,0:T(8,128)S(1)} %get-tuple-element.35), channel_id=1, source_target_pairs={{0,4},{8,12},{16,20},{24,28},{4,0},{12,8},{20,16},{28,24},{1,5},{9... | collective-permute-start | bytes 688136 | tf_op jit(solution)/shard_map/ppermute | solution.py:498
  49.7 7.0 %collective-permute-start.7 = (f32[448,128]{1,0:T(8,128)S(1)}, f32[448,128]{1,0:T(8,128)S(1)}, u32[]{:S(2)}, u32[]{:S(2)}) collective-permute-start(f32[448,128]{1,0:T(8,128)S(1)} %get-tuple-element.36), channel_id=1, source_target_pairs={{4,8},{12,16},{20,24},{8,4},{16,12},{24,20},{5,9},{13,17},{21,25},... | collective-permute-start | bytes 688136 | tf_op jit(solution)/shard_map/ppermute | solution.py:498
  56.7 1.8 %shard_map.61.push = f32[8,2,2,48,128]{4,3,2,1,0:T(8,128)S(1)} custom-call(s32[5]{0:T(128)S(1)} %stack.15.at, s32[1,64]{1,0:T(1,128)S(1)} %bitcast.9, s32[1,64]{1,0:T(1,128)S(1)} %bitcast.11, s32[16,64]{1,0:T(8,128)S(1)} %copy-done.2), custom_call_target="tpu_custom_call" | custom-call | tf_op jit(solution)/shard_map/pallas_call | solution.py:487
  58.6 1.8 %collective-permute-done.7.rows_b = f32[448,128]{1,0:T(8,128)S(1)} collective-permute-done((f32[448,128]{1,0:T(8,128)S(1)}, f32[448,128]{1,0:T(8,128)S(1)}, u32[]{:S(2)}, u32[]{:S(2)}) %collective-permute-start.7) | collective-permute-done | bytes 229408 | tf_op jit(solution)/shard_map/ppermute | solution.py:498
  60.4 0.8 %shard_map.62 = (f32[64,128]{1,0:T(8,128)S(1)}, f32[48,128]{1,0:T(8,128)S(1)}, f32[24,2,48,128]{3,2,1,0:T(8,128)S(1)}, f32[4,2,48,128]{3,2,1,0:T(8,128)S(1)}) custom-call(s32[5]{0:T(128)S(1)} %stack.15.at, f32[8,48,128]{2,1,0:T(8,128)S(1)} %all_to_all.5.held, f32[16,128]{1,0:T(8,128)S(1)} %get-tuple-element.32.nu, ...), custom_call_target="tpu_custom_call" | custom-call | tf_op jit(solution)/shard_map/pallas_call | solution.py:487
  61.2 1.3 %collective-permute-start.8 = (f32[64,128]{1,0:T(8,128)S(1)}, f32[64,128]{1,0:T(8,128)S(1)}, u32[]{:S(2)}, u32[]{:S(2)}) collective-permute-start(f32[64,128]{1,0:T(8,128)S(1)} %get-tuple-element.37), channel_id=1, source_target_pairs={{0,384},{32,416},{64,448},{96,480},{128,256},{160,288},{192,320},{... | collective-permute-start | bytes 98312 | tf_op jit(solution)/shard_map/ppermute | solution.py:553
  62.5 7.4 %collective-permute-done.8.state = f32[64,128]{1,0:T(8,128)S(1)} collective-permute-done((f32[64,128]{1,0:T(8,128)S(1)}, f32[64,128]{1,0:T(8,128)S(1)}, u32[]{:S(2)}, u32[]{:S(2)}) %collective-permute-start.8) | collective-permute-done | bytes 32800 | tf_op jit(solution)/shard_map/ppermute | solution.py:553
  69.9 5.0 %collective-permute-start.10 = (f32[64,128]{1,0:T(8,128)S(1)}, f32[64,128]{1,0:T(8,128)S(1)}, u32[]{:S(2)}, u32[]{:S(2)}) collective-permute-start(f32[64,128]{1,0:T(8,128)S(1)} %collective-permute-done.8.state), channel_id=1, source_target_pairs={{260,264},{268,272},{276,280},{264,260},{272,268},{280,276},{292,2... | collective-permute-start | bytes 98312 | tf_op jit(solution)/shard_map/ppermute | solution.py:503
  74.9 1.9 %collective-permute-start.9 = (f32[64,128]{1,0:T(8,128)S(1)}, f32[64,128]{1,0:T(8,128)S(1)}, u32[]{:S(2)}, u32[]{:S(2)}) collective-permute-start(f32[64,128]{1,0:T(8,128)S(1)} %collective-permute-done.8.state), channel_id=1, source_target_pairs={{256,260},{264,268},{272,276},{280,284},{260,256},{268,264},{276,2... | collective-permute-start | bytes 98312 | tf_op jit(solution)/shard_map/ppermute | solution.py:503
  76.9 1.2 %collective-permute-done.9.state_a = f32[64,128]{1,0:T(8,128)S(1)} collective-permute-done((f32[64,128]{1,0:T(8,128)S(1)}, f32[64,128]{1,0:T(8,128)S(1)}, u32[]{:S(2)}, u32[]{:S(2)}) %collective-permute-start.9) | collective-permute-done | bytes 32800 | tf_op jit(solution)/shard_map/ppermute | solution.py:503
  78.0 4.2 %shard_map.63 = f32[3,64,512]{2,1,0:T(8,128)} custom-call(s32[5]{0:T(128)S(1)} %stack.15.at, f32[64,128]{1,0:T(8,128)S(1)} %collective-permute-done.8.state, f32[64,128]{1,0:T(8,128)S(1)} %collective-permute-done.9.state_a, f32[64,128]{1,0:T(8,128)S(1)} %collective-permute-done.10.state_b, f32[24,2,48,128]{3,2,1,0:T(8,128)S(1)} %get-tuple-element.38.extra, ...), custom_call_target="tpu_custom_call" | custom-call | tf_op jit(solution)/shard_map/pallas_call | solution.py:487
  (11 shorter events, 0.0 us)
Async XLA Ops:
  0.0 16.6 %copy-start.2 = (s32[16,64]{1,0:T(8,128)S(1)}, s32[16,64]{1,0:T(8,128)}, u32[]{:S(2)}) copy-start(s32[16,64]{1,0:T(8,128)} %yaw_in.3) | copy-start | bytes 12292
  0.0 16.6 %copy-start.4 = (s32[64]{0:T(128)S(1)}, s32[64]{0:T(128)}, u32[]{:S(2)}) copy-start(s32[64]{0:T(128)} %param.8) | copy-start | bytes 772
  0.0 16.6 %copy-start.3 = (s32[64]{0:T(128)S(1)}, s32[64]{0:T(128)}, u32[]{:S(2)}) copy-start(s32[64]{0:T(128)} %param.7) | copy-start | bytes 772
  0.1 1.0 %copy-start = (f32[1,3,64,512]{3,2,1,0:T(8,128)S(1)}, f32[1,3,64,512]{3,2,1,0:T(8,128)}, u32[]{:S(2)}) copy-start(f32[1,3,64,512]{3,2,1,0:T(8,128)} %param.5) | copy-start | bytes 1179652
  1.1 0.9 %copy-start.1 = (f32[64,512]{1,0:T(8,128)S(1)}, f32[64,512]{1,0:T(8,128)}, u32[]{:S(2)}) copy-start(f32[64,512]{1,0:T(8,128)} %visc.1) | copy-start | bytes 393220
  2.9 5.6 %collective-permute-start = (f32[4,8,512]{2,1,0:T(8,128)S(1)}, f32[4,8,512]{2,1,0:T(8,128)S(1)}, u32[]{:S(2)}, u32[]{:S(2)}) collective-permute-start(f32[4,8,512]{2,1,0:T(8,128)S(1)} %get-tuple-element.25), channel_id=1, source_target_pairs={{0,4},{8,12},{16,20},{24,28},{4,0},{12,8},{20,16},{28,24},{1,5},{9... | collective-permute-start | bytes 196616 | tf_op jit(solution)/shard_map/ppermute | solution.py:498
  5.4 5.6 %collective-permute-start.1 = (f32[4,8,512]{2,1,0:T(8,128)S(1)}, f32[4,8,512]{2,1,0:T(8,128)S(1)}, u32[]{:S(2)}, u32[]{:S(2)}) collective-permute-start(f32[4,8,512]{2,1,0:T(8,128)S(1)} %get-tuple-element.26), channel_id=1, source_target_pairs={{4,8},{12,16},{20,24},{8,4},{16,12},{24,20},{5,9},{13,17},{21,25},... | collective-permute-start | bytes 196616 | tf_op jit(solution)/shard_map/ppermute | solution.py:498
  11.7 6.1 %collective-permute-start.2 = (f32[80,128]{1,0:T(8,128)S(1)}, f32[80,128]{1,0:T(8,128)S(1)}, u32[]{:S(2)}, u32[]{:S(2)}) collective-permute-start(f32[80,128]{1,0:T(8,128)S(1)} %get-tuple-element.27), channel_id=1, source_target_pairs={{0,1},{2,3},{1,0},{3,2},{4,5},{6,7},{5,4},{7,6},{8,9},{10,11},{9,8... | collective-permute-start | bytes 122888 | tf_op jit(solution)/shard_map/ppermute | solution.py:498
  14.6 4.7 %collective-permute-start.3 = (f32[80,128]{1,0:T(8,128)S(1)}, f32[80,128]{1,0:T(8,128)S(1)}, u32[]{:S(2)}, u32[]{:S(2)}) collective-permute-start(f32[80,128]{1,0:T(8,128)S(1)} %get-tuple-element.28), channel_id=1, source_target_pairs={{1,2},{2,1},{5,6},{6,5},{9,10},{10,9},{13,14},{14,13},{17,18},{18,... | collective-permute-start | bytes 122888 | tf_op jit(solution)/shard_map/ppermute | solution.py:498
  40.3 4.9 %collective-permute-start.4 = (f32[112,128]{1,0:T(8,128)S(1)}, f32[112,128]{1,0:T(8,128)S(1)}, u32[]{:S(2)}, u32[]{:S(2)}) collective-permute-start(f32[112,128]{1,0:T(8,128)S(1)} %get-tuple-element.33), channel_id=1, source_target_pairs={{0,1},{2,3},{1,0},{3,2},{4,5},{6,7},{5,4},{7,6},{8,9},{10,11},{9,8... | collective-permute-start | bytes 172040 | tf_op jit(solution)/shard_map/ppermute | solution.py:498
  42.2 4.9 %collective-permute-start.5 = (f32[112,128]{1,0:T(8,128)S(1)}, f32[112,128]{1,0:T(8,128)S(1)}, u32[]{:S(2)}, u32[]{:S(2)}) collective-permute-start(f32[112,128]{1,0:T(8,128)S(1)} %get-tuple-element.34), channel_id=1, source_target_pairs={{1,2},{2,1},{5,6},{6,5},{9,10},{10,9},{13,14},{14,13},{17,18},{18,... | collective-permute-start | bytes 172040 | tf_op jit(solution)/shard_map/ppermute | solution.py:498
  47.7 10.8 %collective-permute-start.6 = (f32[448,128]{1,0:T(8,128)S(1)}, f32[448,128]{1,0:T(8,128)S(1)}, u32[]{:S(2)}, u32[]{:S(2)}) collective-permute-start(f32[448,128]{1,0:T(8,128)S(1)} %get-tuple-element.35), channel_id=1, source_target_pairs={{0,4},{8,12},{16,20},{24,28},{4,0},{12,8},{20,16},{28,24},{1,5},{9... | collective-permute-start | bytes 688136 | tf_op jit(solution)/shard_map/ppermute | solution.py:498
  49.7 10.7 %collective-permute-start.7 = (f32[448,128]{1,0:T(8,128)S(1)}, f32[448,128]{1,0:T(8,128)S(1)}, u32[]{:S(2)}, u32[]{:S(2)}) collective-permute-start(f32[448,128]{1,0:T(8,128)S(1)} %get-tuple-element.36), channel_id=1, source_target_pairs={{4,8},{12,16},{20,24},{8,4},{16,12},{24,20},{5,9},{13,17},{21,25},... | collective-permute-start | bytes 688136 | tf_op jit(solution)/shard_map/ppermute | solution.py:498
  61.2 8.7 %collective-permute-start.8 = (f32[64,128]{1,0:T(8,128)S(1)}, f32[64,128]{1,0:T(8,128)S(1)}, u32[]{:S(2)}, u32[]{:S(2)}) collective-permute-start(f32[64,128]{1,0:T(8,128)S(1)} %get-tuple-element.37), channel_id=1, source_target_pairs={{0,384},{32,416},{64,448},{96,480},{128,256},{160,288},{192,320},{... | collective-permute-start | bytes 98312 | tf_op jit(solution)/shard_map/ppermute | solution.py:553
  69.9 6.9 %collective-permute-start.10 = (f32[64,128]{1,0:T(8,128)S(1)}, f32[64,128]{1,0:T(8,128)S(1)}, u32[]{:S(2)}, u32[]{:S(2)}) collective-permute-start(f32[64,128]{1,0:T(8,128)S(1)} %collective-permute-done.8.state), channel_id=1, source_target_pairs={{260,264},{268,272},{276,280},{264,260},{272,268},{280,276},{292,2... | collective-permute-start | bytes 98312 | tf_op jit(solution)/shard_map/ppermute | solution.py:503
  74.9 3.1 %collective-permute-start.9 = (f32[64,128]{1,0:T(8,128)S(1)}, f32[64,128]{1,0:T(8,128)S(1)}, u32[]{:S(2)}, u32[]{:S(2)}) collective-permute-start(f32[64,128]{1,0:T(8,128)S(1)} %collective-permute-done.8.state), channel_id=1, source_target_pairs={{256,260},{264,268},{272,276},{280,284},{260,256},{268,264},{276,2... | collective-permute-start | bytes 98312 | tf_op jit(solution)/shard_map/ppermute | solution.py:503

commit v5 on v4

--- a/solution.py
+++ b/solution.py
@@ -149,20 +149,19 @@
         copy.wait()
 
 
-def open_kernel(at, start, visc, send_a, send_b, own, sems):
-    last = pl.multiple_of(56 * (1 - lax.rem(at[1], 2)), 8)
-    first = pl.multiple_of(56 * lax.rem(at[1], 2), 8)
+def load_kernel(at, start, visc, own, sems):
     fetch(
-        [
-            (start.at[:, pl.ds(last, 8), :], send_a.at[0:3]),
-            (visc.at[pl.ds(last, 8), :], send_a.at[3]),
-            (start.at[:, pl.ds(first, 8), :], send_b.at[0:3]),
-            (visc.at[pl.ds(first, 8), :], send_b.at[3]),
-        ]
-        + [(start.at[:, :, 128 * c : 128 * c + 128], own.at[0:3, c]) for c in range(4)]
+        [(start.at[:, :, 128 * c : 128 * c + 128], own.at[0:3, c]) for c in range(4)]
         + [(visc.at[:, 128 * c : 128 * c + 128], own.at[3, c]) for c in range(4)],
         sems,
     )
+
+
+def edge_rows(start, visc, first):
+    return jnp.concatenate([
+        lax.dynamic_slice(start, (0, first, 0), (3, 8, COLS)),
+        lax.dynamic_slice(visc, (first, 0), (8, COLS))[None],
+    ])
 
 
 def side_kernel(at, own, got_a, got_b, send_a, send_b):
@@ -517,11 +516,10 @@
     turbines = (turbine_x[None, :], turbine_y[None, :], yaw_index)
     turbine_scratch = [pltpu.VMEM((1, 64), jnp.int32), pltpu.VMEM((1, 64), jnp.int32), pltpu.VMEM((CUTS, 64), jnp.int32)]
 
-    edge = (4, 8, COLS)
-    send_a, send_b, own = call(
-        open_kernel, (at, start, viscosity), [edge, edge, (4, 4, ROWS, 128)], far=2, sems=12)
-    rows_a = swap(send_a, "sx", x_a)
-    rows_b = swap(send_b, "sx", x_b)
+    odd = at[1] % 2
+    rows_b = swap(edge_rows(start, viscosity, 56 * odd), "sx", x_b)
+    rows_a = swap(edge_rows(start, viscosity, 56 * (1 - odd)), "sx", x_a)
+    (own,) = call(load_kernel, (at, start, viscosity), [(4, 4, ROWS, 128)], far=2, sems=8)
     send_a, send_b = call(side_kernel, (at, own, rows_a, rows_b), [(80, 128)] * 2)
     cols_a = swap(send_a, "sy", y_a)
     cols_b = swap(send_b, "sy", y_b)

time: 82.6 us -> 82 us (level)
  the two profiles are of different devices: /device:TPU:305 before, /device:TPU:297 now
where the time goes in v5:
time: 82 us; the launch traced here: 81.4 us
  starting transfers between devices  32.5 us (40%)
  blocking collectives  19 us (23%)
  Pallas kernels  13.7 us (17%)
  waiting for transfers between devices  12.5 us (15%)
  local copies, waits for them, and re-layouts  3.58 us (4%)
    ppermute x8, starting transfers between devices, swap(): lax.ppermute(x, axis, [(a, b) for a, b in pairs] + [(b, a) for a, b in pa...  24.2 us
    all_to_all x1, blocking collectives, on_device(): held = lax.all_to_all(sent, 'cuts', 0, 0, axis_index_groups=halves)  19 us
    pallas_call x9, Pallas kernels, call(): pl.pallas_call(kernel, out_shape=shapes, in_specs=[SMEM] + [VMEM] * near...  13.7 us
    ppermute x1, waiting for transfers between devices, on_device(): lax.ppermute(state, 'cuts', [(m, m + 4 if m >= 4 else m + 12) for m in ra...  7.35 us
    ppermute x2, starting transfers between devices, swap_high(): lax.ppermute(x, ('cuts', 'sx'), [(n * count + a, n * count + b) for n in...  6.93 us
    ppermute x8, waiting for transfers between devices, swap(): lax.ppermute(x, axis, [(a, b) for a, b in pairs] + [(b, a) for a, b in pa...  3.94 us
    unnamed x10, local copies, waits for them, and re-layouts  1.91 us
  transfers between devices with their start and end apart: 11, of which 5 were waited for; matrix products, arithmetic and copies ran while one was open for 0% of the time, Pallas kernels for 5%

profile of v5, /device:TPU:297, one launch (start us, length us, event | category | flops | bytes accessed | tf_op | source)
XLA Modules:
  0.0 81.4 jit_solution(1873266464022744397)
XLA Ops:
  0.0 0.7 dynamic-slice_bitcast_fusion.2
  0.8 0.8 %dynamic-slice_bitcast_fusion = (f32[3,8,512]{2,1,0:T(8,128)S(1)}, f32[3,8,512]{2,1,0:T(8,128)S(1)}) fusion(f32[1,3,64,512]{3,2,1,0:T(8,128)} %param.5, s32[]{:T(128)S(6)} %select_n.17, s32[]{:T(128)S(6)} %select_n.16), kind=kLoop, calls=%fused_computation.2 | loop fusion | bytes 196616 | tf_op jit(solution)/shard_map/dynamic_slice | solution.py:162
  1.6 2.6 %collective-permute-start = (f32[4,8,512]{2,1,0:T(8,128)S(1)}, f32[4,8,512]{2,1,0:T(8,128)S(1)}, u32[]{:S(2)}, u32[]{:S(2)}) collective-permute-start(f32[4,8,512]{2,1,0:T(8,128)S(1)} %pad_maximum_fusion), channel_id=1, source_target_pairs={{0,4},{8,12},{16,20},{24,28},{4,0},{12,8},{20,16},{28,24},{1,5},{9... | collective-permute-start | bytes 196616 | tf_op jit(solution)/shard_map/ppermute | solution.py:497
  4.2 3.0 %collective-permute-start.1 = (f32[4,8,512]{2,1,0:T(8,128)S(1)}, f32[4,8,512]{2,1,0:T(8,128)S(1)}, u32[]{:S(2)}, u32[]{:S(2)}) collective-permute-start(f32[4,8,512]{2,1,0:T(8,128)S(1)} %pad_maximum_fusion.1), channel_id=1, source_target_pairs={{4,8},{12,16},{20,24},{8,4},{16,12},{24,20},{5,9},{13,17},{21,25},... | collective-permute-start | bytes 196616 | tf_op jit(solution)/shard_map/ppermute | solution.py:497
  7.3 0.1 stack.15.at
  7.3 1.0 %copy-done = f32[1,3,64,512]{3,2,1,0:T(8,128)S(1)} copy-done((f32[1,3,64,512]{3,2,1,0:T(8,128)S(1)}, f32[1,3,64,512]{3,2,1,0:T(8,128)}, u32[]{:S(2)}) %copy-start) | copy-done | bytes 393240
  8.3 0.9 %copy-done.1 = f32[64,512]{1,0:T(8,128)S(1)} copy-done((f32[64,512]{1,0:T(8,128)S(1)}, f32[64,512]{1,0:T(8,128)}, u32[]{:S(2)}) %copy-start.1) | copy-done | bytes 131096
  9.2 0.7 shard_map.55.own
  10.0 0.0 collective-permute-done.got_a.rows_a
  10.0 0.7 shard_map.56
  10.7 2.1 %collective-permute-start.2 = (f32[80,128]{1,0:T(8,128)S(1)}, f32[80,128]{1,0:T(8,128)S(1)}, u32[]{:S(2)}, u32[]{:S(2)}) collective-permute-start(f32[80,128]{1,0:T(8,128)S(1)} %get-tuple-element.21), channel_id=1, source_target_pairs={{0,1},{2,3},{1,0},{3,2},{4,5},{6,7},{5,4},{7,6},{8,9},{10,11},{9,8... | collective-permute-start | bytes 122888 | tf_op jit(solution)/shard_map/ppermute | solution.py:497
  12.8 4.0 %collective-permute-start.3 = (f32[80,128]{1,0:T(8,128)S(1)}, f32[80,128]{1,0:T(8,128)S(1)}, u32[]{:S(2)}, u32[]{:S(2)}) collective-permute-start(f32[80,128]{1,0:T(8,128)S(1)} %get-tuple-element.22), channel_id=1, source_target_pairs={{1,2},{2,1},{5,6},{6,5},{9,10},{10,9},{13,14},{14,13},{17,18},{18,... | collective-permute-start | bytes 122888 | tf_op jit(solution)/shard_map/ppermute | solution.py:497
  16.8 1.2 %shard_map.57 = (f32[2,5,96,128]{3,2,1,0:T(8,128)S(1)}, f32[2,2,40,128]{3,2,1,0:T(8,128)S(1)}) custom-call(s32[5]{0:T(128)S(1)} %stack.15.at, s32[1,64]{1,0:T(1,128)S(1)} %bitcast.16, s32[1,64]{1,0:T(1,128)S(1)} %bitcast.18, s32[16,64]{1,0:T(8,128)S(1)} %copy-done.2), custom_call_target="tpu_custom_call" | custom-call | tf_op jit(solution)/shard_map/pallas_call | solution.py:486
  18.0 0.2 collective-permute-done.3.cols_b
  18.2 3.0 %shard_map.58 = (f32[3,64,512]{2,1,0:T(8,128)S(1)}, f32[48,128]{1,0:T(8,128)S(1)}, f32[8,48,128]{2,1,0:T(8,128)S(1)}, f32[16,128]{1,0:T(8,128)S(1)}) custom-call(s32[5]{0:T(128)S(1)} %stack.15.at, f32[4,4,64,128]{3,2,1,0:T(8,128)S(1)} %shard_map.55.own, f32[4,8,512]{2,1,0:T(8,128)S(1)} %collective-permute-done.got_a.rows_a, ...), custom_call_target="tpu_custom_call" | custom-call | tf_op jit(solution)/shard_map/pallas_call | solution.py:486
  21.2 19.0 %all_to_all.5.held = f32[8,48,128]{2,1,0:T(8,128)S(1)} all-to-all(f32[8,48,128]{2,1,0:T(8,128)S(1)} %get-tuple-element.25), channel_id=1, replica_groups={{0,32,64,96,128,160,192,224},{256,288,320,352,384,416,448,480},{1,33,65..., dimensions={0} | all-to-all | bytes 393216 | tf_op jit(solution)/shard_map/all_to_all | solution.py:535
  40.2 0.7 shard_map.59
  40.8 1.9 %collective-permute-start.4 = (f32[112,128]{1,0:T(8,128)S(1)}, f32[112,128]{1,0:T(8,128)S(1)}, u32[]{:S(2)}, u32[]{:S(2)}) collective-permute-start(f32[112,128]{1,0:T(8,128)S(1)} %get-tuple-element.27), channel_id=1, source_target_pairs={{0,1},{2,3},{1,0},{3,2},{4,5},{6,7},{5,4},{7,6},{8,9},{10,11},{9,8... | collective-permute-start | bytes 172040 | tf_op jit(solution)/shard_map/ppermute | solution.py:497
  42.8 3.8 %collective-permute-start.5 = (f32[112,128]{1,0:T(8,128)S(1)}, f32[112,128]{1,0:T(8,128)S(1)}, u32[]{:S(2)}, u32[]{:S(2)}) collective-permute-start(f32[112,128]{1,0:T(8,128)S(1)} %get-tuple-element.28), channel_id=1, source_target_pairs={{1,2},{2,1},{5,6},{6,5},{9,10},{10,9},{13,14},{14,13},{17,18},{18,... | collective-permute-start | bytes 172040 | tf_op jit(solution)/shard_map/ppermute | solution.py:497
  46.6 1.9 %collective-permute-done.5.cols_b = f32[112,128]{1,0:T(8,128)S(1)} collective-permute-done((f32[112,128]{1,0:T(8,128)S(1)}, f32[112,128]{1,0:T(8,128)S(1)}, u32[]{:S(2)}, u32[]{:S(2)}) %collective-permute-start.5) | collective-permute-done | bytes 57376 | tf_op jit(solution)/shard_map/ppermute | solution.py:497
  48.5 0.6 shard_map.60
  49.1 2.8 %collective-permute-start.6 = (f32[448,128]{1,0:T(8,128)S(1)}, f32[448,128]{1,0:T(8,128)S(1)}, u32[]{:S(2)}, u32[]{:S(2)}) collective-permute-start(f32[448,128]{1,0:T(8,128)S(1)} %get-tuple-element.29), channel_id=1, source_target_pairs={{0,4},{8,12},{16,20},{24,28},{4,0},{12,8},{20,16},{28,24},{1,5},{9... | collective-permute-start | bytes 688136 | tf_op jit(solution)/shard_map/ppermute | solution.py:497
  51.9 4.0 %collective-permute-start.7 = (f32[448,128]{1,0:T(8,128)S(1)}, f32[448,128]{1,0:T(8,128)S(1)}, u32[]{:S(2)}, u32[]{:S(2)}) collective-permute-start(f32[448,128]{1,0:T(8,128)S(1)} %get-tuple-element.30), channel_id=1, source_target_pairs={{4,8},{12,16},{20,24},{8,4},{16,12},{24,20},{5,9},{13,17},{21,25},... | collective-permute-start | bytes 688136 | tf_op jit(solution)/shard_map/ppermute | solution.py:497
  55.9 1.8 %shard_map.61.push = f32[8,2,2,48,128]{4,3,2,1,0:T(8,128)S(1)} custom-call(s32[5]{0:T(128)S(1)} %stack.15.at, s32[1,64]{1,0:T(1,128)S(1)} %bitcast.17, s32[1,64]{1,0:T(1,128)S(1)} %bitcast.19, s32[16,64]{1,0:T(8,128)S(1)} %copy-done.2), custom_call_target="tpu_custom_call" | custom-call | tf_op jit(solution)/shard_map/pallas_call | solution.py:486
  57.8 1.8 %collective-permute-done.7.rows_b = f32[448,128]{1,0:T(8,128)S(1)} collective-permute-done((f32[448,128]{1,0:T(8,128)S(1)}, f32[448,128]{1,0:T(8,128)S(1)}, u32[]{:S(2)}, u32[]{:S(2)}) %collective-permute-start.7) | collective-permute-done | bytes 229408 | tf_op jit(solution)/shard_map/ppermute | solution.py:497
  59.6 0.8 %shard_map.62 = (f32[64,128]{1,0:T(8,128)S(1)}, f32[48,128]{1,0:T(8,128)S(1)}, f32[24,2,48,128]{3,2,1,0:T(8,128)S(1)}, f32[4,2,48,128]{3,2,1,0:T(8,128)S(1)}) custom-call(s32[5]{0:T(128)S(1)} %stack.15.at, f32[8,48,128]{2,1,0:T(8,128)S(1)} %all_to_all.5.held, f32[16,128]{1,0:T(8,128)S(1)} %get-tuple-element.26.nu, ...), custom_call_target="tpu_custom_call" | custom-call | tf_op jit(solution)/shard_map/pallas_call | solution.py:486
  60.5 1.3 %collective-permute-start.8 = (f32[64,128]{1,0:T(8,128)S(1)}, f32[64,128]{1,0:T(8,128)S(1)}, u32[]{:S(2)}, u32[]{:S(2)}) collective-permute-start(f32[64,128]{1,0:T(8,128)S(1)} %get-tuple-element.31), channel_id=1, source_target_pairs={{0,384},{32,416},{64,448},{96,480},{128,256},{160,288},{192,320},{... | collective-permute-start | bytes 98312 | tf_op jit(solution)/shard_map/ppermute | solution.py:551
  61.8 7.4 %collective-permute-done.8.state = f32[64,128]{1,0:T(8,128)S(1)} collective-permute-done((f32[64,128]{1,0:T(8,128)S(1)}, f32[64,128]{1,0:T(8,128)S(1)}, u32[]{:S(2)}, u32[]{:S(2)}) %collective-permute-start.8) | collective-permute-done | bytes 32800 | tf_op jit(solution)/shard_map/ppermute | solution.py:551
  69.1 5.0 %collective-permute-start.10 = (f32[64,128]{1,0:T(8,128)S(1)}, f32[64,128]{1,0:T(8,128)S(1)}, u32[]{:S(2)}, u32[]{:S(2)}) collective-permute-start(f32[64,128]{1,0:T(8,128)S(1)} %collective-permute-done.8.state), channel_id=1, source_target_pairs={{260,264},{268,272},{276,280},{264,260},{272,268},{280,276},{292,2... | collective-permute-start | bytes 98312 | tf_op jit(solution)/shard_map/ppermute | solution.py:502
  74.1 1.9 %collective-permute-start.9 = (f32[64,128]{1,0:T(8,128)S(1)}, f32[64,128]{1,0:T(8,128)S(1)}, u32[]{:S(2)}, u32[]{:S(2)}) collective-permute-start(f32[64,128]{1,0:T(8,128)S(1)} %collective-permute-done.8.state), channel_id=1, source_target_pairs={{256,260},{264,268},{272,276},{280,284},{260,256},{268,264},{276,2... | collective-permute-start | bytes 98312 | tf_op jit(solution)/shard_map/ppermute | solution.py:502
  76.1 1.2 %collective-permute-done.9.state_a = f32[64,128]{1,0:T(8,128)S(1)} collective-permute-done((f32[64,128]{1,0:T(8,128)S(1)}, f32[64,128]{1,0:T(8,128)S(1)}, u32[]{:S(2)}, u32[]{:S(2)}) %collective-permute-start.9) | collective-permute-done | bytes 32800 | tf_op jit(solution)/shard_map/ppermute | solution.py:502
  77.2 4.2 %shard_map.63 = f32[3,64,512]{2,1,0:T(8,128)} custom-call(s32[5]{0:T(128)S(1)} %stack.15.at, f32[64,128]{1,0:T(8,128)S(1)} %collective-permute-done.8.state, f32[64,128]{1,0:T(8,128)S(1)} %collective-permute-done.9.state_a, f32[64,128]{1,0:T(8,128)S(1)} %collective-permute-done.10.state_b, f32[24,2,48,128]{3,2,1,0:T(8,128)S(1)} %get-tuple-element.32.extra, ...), custom_call_target="tpu_custom_call" | custom-call | tf_op jit(solution)/shard_map/pallas_call | solution.py:486
  (15 shorter events, 0.0 us)
Async XLA Ops:
  0.0 16.8 %copy-start.2 = (s32[16,64]{1,0:T(8,128)S(1)}, s32[16,64]{1,0:T(8,128)}, u32[]{:S(2)}) copy-start(s32[16,64]{1,0:T(8,128)} %yaw_in.3) | copy-start | bytes 12292
  0.0 16.8 %copy-start.4 = (s32[64]{0:T(128)S(1)}, s32[64]{0:T(128)}, u32[]{:S(2)}) copy-start(s32[64]{0:T(128)} %param.8) | copy-start | bytes 772
  0.0 16.8 %copy-start.3 = (s32[64]{0:T(128)S(1)}, s32[64]{0:T(128)}, u32[]{:S(2)}) copy-start(s32[64]{0:T(128)} %param.7) | copy-start | bytes 772
  1.6 8.3 %collective-permute-start = (f32[4,8,512]{2,1,0:T(8,128)S(1)}, f32[4,8,512]{2,1,0:T(8,128)S(1)}, u32[]{:S(2)}, u32[]{:S(2)}) collective-permute-start(f32[4,8,512]{2,1,0:T(8,128)S(1)} %pad_maximum_fusion), channel_id=1, source_target_pairs={{0,4},{8,12},{16,20},{24,28},{4,0},{12,8},{20,16},{28,24},{1,5},{9... | collective-permute-start | bytes 196616 | tf_op jit(solution)/shard_map/ppermute | solution.py:497
  4.2 5.7 %collective-permute-start.1 = (f32[4,8,512]{2,1,0:T(8,128)S(1)}, f32[4,8,512]{2,1,0:T(8,128)S(1)}, u32[]{:S(2)}, u32[]{:S(2)}) collective-permute-start(f32[4,8,512]{2,1,0:T(8,128)S(1)} %pad_maximum_fusion.1), channel_id=1, source_target_pairs={{4,8},{12,16},{20,24},{8,4},{16,12},{24,20},{5,9},{13,17},{21,25},... | collective-permute-start | bytes 196616 | tf_op jit(solution)/shard_map/ppermute | solution.py:497
  7.3 1.0 %copy-start = (f32[1,3,64,512]{3,2,1,0:T(8,128)S(1)}, f32[1,3,64,512]{3,2,1,0:T(8,128)}, u32[]{:S(2)}) copy-start(f32[1,3,64,512]{3,2,1,0:T(8,128)} %param.5) | copy-start | bytes 1179652
  8.3 0.9 %copy-start.1 = (f32[64,512]{1,0:T(8,128)S(1)}, f32[64,512]{1,0:T(8,128)}, u32[]{:S(2)}) copy-start(f32[64,512]{1,0:T(8,128)} %visc.1) | copy-start | bytes 393220
  10.7 7.3 %collective-permute-start.2 = (f32[80,128]{1,0:T(8,128)S(1)}, f32[80,128]{1,0:T(8,128)S(1)}, u32[]{:S(2)}, u32[]{:S(2)}) collective-permute-start(f32[80,128]{1,0:T(8,128)S(1)} %get-tuple-element.21), channel_id=1, source_target_pairs={{0,1},{2,3},{1,0},{3,2},{4,5},{6,7},{5,4},{7,6},{8,9},{10,11},{9,8... | collective-permute-start | bytes 122888 | tf_op jit(solution)/shard_map/ppermute | solution.py:497
  12.8 5.4 %collective-permute-start.3 = (f32[80,128]{1,0:T(8,128)S(1)}, f32[80,128]{1,0:T(8,128)S(1)}, u32[]{:S(2)}, u32[]{:S(2)}) collective-permute-start(f32[80,128]{1,0:T(8,128)S(1)} %get-tuple-element.22), channel_id=1, source_target_pairs={{1,2},{2,1},{5,6},{6,5},{9,10},{10,9},{13,14},{14,13},{17,18},{18,... | collective-permute-start | bytes 122888 | tf_op jit(solution)/shard_map/ppermute | solution.py:497
  40.8 5.7 %collective-permute-start.4 = (f32[112,128]{1,0:T(8,128)S(1)}, f32[112,128]{1,0:T(8,128)S(1)}, u32[]{:S(2)}, u32[]{:S(2)}) collective-permute-start(f32[112,128]{1,0:T(8,128)S(1)} %get-tuple-element.27), channel_id=1, source_target_pairs={{0,1},{2,3},{1,0},{3,2},{4,5},{6,7},{5,4},{7,6},{8,9},{10,11},{9,8... | collective-permute-start | bytes 172040 | tf_op jit(solution)/shard_map/ppermute | solution.py:497
  42.8 5.8 %collective-permute-start.5 = (f32[112,128]{1,0:T(8,128)S(1)}, f32[112,128]{1,0:T(8,128)S(1)}, u32[]{:S(2)}, u32[]{:S(2)}) collective-permute-start(f32[112,128]{1,0:T(8,128)S(1)} %get-tuple-element.28), channel_id=1, source_target_pairs={{1,2},{2,1},{5,6},{6,5},{9,10},{10,9},{13,14},{14,13},{17,18},{18,... | collective-permute-start | bytes 172040 | tf_op jit(solution)/shard_map/ppermute | solution.py:497
  49.1 8.7 %collective-permute-start.6 = (f32[448,128]{1,0:T(8,128)S(1)}, f32[448,128]{1,0:T(8,128)S(1)}, u32[]{:S(2)}, u32[]{:S(2)}) collective-permute-start(f32[448,128]{1,0:T(8,128)S(1)} %get-tuple-element.29), channel_id=1, source_target_pairs={{0,4},{8,12},{16,20},{24,28},{4,0},{12,8},{20,16},{28,24},{1,5},{9... | collective-permute-start | bytes 688136 | tf_op jit(solution)/shard_map/ppermute | solution.py:497
  51.9 7.7 %collective-permute-start.7 = (f32[448,128]{1,0:T(8,128)S(1)}, f32[448,128]{1,0:T(8,128)S(1)}, u32[]{:S(2)}, u32[]{:S(2)}) collective-permute-start(f32[448,128]{1,0:T(8,128)S(1)} %get-tuple-element.30), channel_id=1, source_target_pairs={{4,8},{12,16},{20,24},{8,4},{16,12},{24,20},{5,9},{13,17},{21,25},... | collective-permute-start | bytes 688136 | tf_op jit(solution)/shard_map/ppermute | solution.py:497
  60.5 8.7 %collective-permute-start.8 = (f32[64,128]{1,0:T(8,128)S(1)}, f32[64,128]{1,0:T(8,128)S(1)}, u32[]{:S(2)}, u32[]{:S(2)}) collective-permute-start(f32[64,128]{1,0:T(8,128)S(1)} %get-tuple-element.31), channel_id=1, source_target_pairs={{0,384},{32,416},{64,448},{96,480},{128,256},{160,288},{192,320},{... | collective-permute-start | bytes 98312 | tf_op jit(solution)/shard_map/ppermute | solution.py:551
  69.1 6.9 %collective-permute-start.10 = (f32[64,128]{1,0:T(8,128)S(1)}, f32[64,128]{1,0:T(8,128)S(1)}, u32[]{:S(2)}, u32[]{:S(2)}) collective-permute-start(f32[64,128]{1,0:T(8,128)S(1)} %collective-permute-done.8.state), channel_id=1, source_target_pairs={{260,264},{268,272},{276,280},{264,260},{272,268},{280,276},{292,2... | collective-permute-start | bytes 98312 | tf_op jit(solution)/shard_map/ppermute | solution.py:502
  74.1 3.1 %collective-permute-start.9 = (f32[64,128]{1,0:T(8,128)S(1)}, f32[64,128]{1,0:T(8,128)S(1)}, u32[]{:S(2)}, u32[]{:S(2)}) collective-permute-start(f32[64,128]{1,0:T(8,128)S(1)} %collective-permute-done.8.state), channel_id=1, source_target_pairs={{256,260},{264,268},{272,276},{280,284},{260,256},{268,264},{276,2... | collective-permute-start | bytes 98312 | tf_op jit(solution)/shard_map/ppermute | solution.py:502

commit v6 on v5

--- a/solution.py
+++ b/solution.py
@@ -32,18 +32,20 @@
 WEIGHT_Y = [float(np.float32(math.cos(t) ** 2 * math.sin(t))) for t in ANGLES]
 
 WIDTH = 32
-_ORDER = list(range(21)) + [NU, 21, 22, 23]
+_ORDER = list(range(9)) + [NU, 21, 22] + list(range(9, 21)) + [23]
 GROUPS = [_ORDER[_i : _i + 4] for _i in range(0, len(_ORDER), 4)]
 STRIPS = 16 * len(GROUPS)
-ROW_STRIPS = 16 * 6
 PARTS = [(q, 16) for q in range(0, 9)] + [(q, 8) for q in range(9, 21)] + [(NU, 16)]
 PART_AT = {}
 _at = 0
 for _q, _rows in PARTS:
     PART_AT[_q] = (_at, _rows)
     _at += _rows
-STRIP_AT = _at
-MESSAGE = STRIP_AT + 2 * ROW_STRIPS
+STRIP_AT = {}
+for _g, _rows in ((0, 16), (1, 16), (2, 16), (3, 8), (4, 8), (5, 8)):
+    STRIP_AT[_g] = (_at, _rows)
+    _at += 2 * _rows
+MESSAGE = _at
 
 
 def lanes(shape):
@@ -66,15 +68,10 @@
 
 
 def exact_dot(x, y, dims=(((1,), (0,)), ((), ()))):
-    y = y.astype(BF16)
-    a, b, c = [lax.dot_general(part, y, dims, preferred_element_type=F32) for part in split3(x)]
-    return a + (b + c)
-
-
-def dot_exact(y, x):
-    y = y.astype(BF16)
-    a, b, c = [jnp.dot(y, part, preferred_element_type=F32) for part in split3(x)]
-    return a + (b + c)
+    count = x.shape[0]
+    stacked = jnp.concatenate(split3(x), axis=0)
+    out = lax.dot_general(stacked, y.astype(BF16), dims, preferred_element_type=F32)
+    return out[0:count] + (out[count : 2 * count] + out[2 * count : 3 * count])
 
 
 def advance(src, dst, coef, push, shift, row, count, tiles, wanted, terms, side_mask, post=None):
@@ -346,46 +343,63 @@
 
 def rows_kernel(at, held, nu, cols_a, cols_b, send_a, send_b):
     even = lax.rem(at[1], 2) == 0
-    for q, rows in PARTS:
-        place, _ = PART_AT[q]
-        value = plane_of(held, nu, q)
+
+    def put(place, rows, value):
         if rows == 16:
             send_a[place : place + 16, :] = value
             send_b[place : place + 16, :] = value
         else:
             send_a[place : place + 8, :] = jnp.where(even, value[8:16], value[0:8])
             send_b[place : place + 8, :] = jnp.where(even, value[0:8], value[8:16])
-    for ref in (send_a, send_b):
-        ref[STRIP_AT : STRIP_AT + ROW_STRIPS, :] = cols_a[0:ROW_STRIPS, :]
-        ref[STRIP_AT + ROW_STRIPS : MESSAGE, :] = cols_b[0:ROW_STRIPS, :]
+
+    for q, rows in PARTS:
+        put(PART_AT[q][0], rows, plane_of(held, nu, q))
+    for g, (place, rows) in STRIP_AT.items():
+        put(place, rows, cols_a[16 * g : 16 * g + 16, :])
+        put(place + rows, rows, cols_b[16 * g : 16 * g + 16, :])
 
 
 def assemble(at, held, nu, cols_a, cols_b, rows_a, rows_b, put):
     even_x = lax.rem(at[1], 2) == 0
     even_y = lax.rem(at[2], 2) == 0
+
+    def sides(place, rows):
+        a, b = rows_a[place : place + rows, :], rows_b[place : place + rows, :]
+        return jnp.where(even_x, b, a), jnp.where(even_x, a, b)
+
     for q in range(NU + 1):
         put(q, 0, 16, plane_of(held, nu, q))
         if q in PART_AT:
             place, rows = PART_AT[q]
-            a, b = rows_a[place : place + rows, :], rows_b[place : place + rows, :]
-            put(q, 0, 16 - rows, jnp.where(even_x, b, a))
-            put(q, 0, 32, jnp.where(even_x, a, b))
-    lane = lanes((16, 128))
+            before, after = sides(place, rows)
+            put(q, 0, 16 - rows, before)
+            put(q, 0, 32, after)
     for g, members in enumerate(GROUPS):
         cut = slice(16 * g, 16 * g + 16)
         blocks = [(16, cols_a[cut, :], cols_b[cut, :])]
-        if 16 * g < ROW_STRIPS:
-            cut_a = slice(STRIP_AT + 16 * g, STRIP_AT + 16 * g + 16)
-            cut_b = slice(STRIP_AT + ROW_STRIPS + 16 * g, STRIP_AT + ROW_STRIPS + 16 * g + 16)
-            aa, ab, ba, bb = rows_a[cut_a, :], rows_a[cut_b, :], rows_b[cut_a, :], rows_b[cut_b, :]
-            blocks.append((0, jnp.where(even_x, ba, aa), jnp.where(even_x, bb, ab)))
-            blocks.append((32, jnp.where(even_x, aa, ba), jnp.where(even_x, ab, bb)))
+        if g in STRIP_AT:
+            place, rows = STRIP_AT[g]
+            before_a, after_a = sides(place, rows)
+            before_b, after_b = sides(place + rows, rows)
+            blocks += [(16 - rows, before_a, before_b), (32, after_a, after_b)]
         for first, a, b in blocks:
+            lane = lanes(a.shape)
             after, before = jnp.where(even_y, a, b), jnp.where(even_y, b, a)
             for slot, q in enumerate(members):
                 if first == 16 or q in PART_AT:
                     hi, lo = rolled(after, -slot * WIDTH), rolled(before, 128 - WIDTH - slot * WIDTH)
                     put(q, 1, first, jnp.where(lane < WIDTH, hi, jnp.where(lane >= 128 - WIDTH, lo, 0.0)))
+
+
+def putter(extra, coef):
+    def put(q, c, row, value):
+        rows = pl.ds(row, value.shape[0])
+        if q == NU:
+            coefficients(coef, c, rows, value, COARSE[0])
+        else:
+            extra[q, c, rows, :] = value
+
+    return put
 
 
 def chain(first_k, one, two, coef, push, extra, kept, at):
@@ -413,17 +427,9 @@
 
 
 def low_kernel(at, held, nu, cols_a, cols_b, rows_a, rows_b, push, state, moved, extra, coef, one, two, kept):
-    def put(q, c, row, value):
-        rows = pl.ds(row, value.shape[0])
-        if q == NU:
-            coefficients(coef, c, rows, value, COARSE[0])
-        else:
-            extra[q, c, rows, :] = value
-
-    assemble(at, held, nu, cols_a, cols_b, rows_a, rows_b, put)
-
     @pl.when(at[0] < HALF)
     def _():
+        assemble(at, held, nu, cols_a, cols_b, rows_a, rows_b, putter(extra, coef))
         for f in range(3):
             for c in range(2):
                 one[f, c, 8:56, :] = extra[f, c]
@@ -438,7 +444,13 @@
             moved[16 * f : 16 * f + 16, :] = kept[jnp.maximum(at[0], 1), f, 24:40, :]
 
 
-def high_kernel(at, state, state_a, state_b, extra, coef, push, fine, guess, moved_low, out, one, two, kept, moved):
+def planes_kernel(at, held, nu, cols_a, cols_b, rows_a, rows_b, extra, coef):
+    @pl.when(at[0] >= HALF)
+    def _():
+        assemble(at, held, nu, cols_a, cols_b, rows_a, rows_b, putter(extra, coef))
+
+
+def high_kernel(at, state, state_a, state_b, extra, coef, push, fine, guess, moved_low, out, one, two, kept, moved, spread):
     even_x = lax.rem(at[1], 2) == 0
 
     @pl.when(at[0] < HALF)
@@ -463,13 +475,14 @@
         cut = slice(16 * f, 16 * f + 16)
         parts.append(jnp.where(at[0] == 0, 0.0, (moved[cut, :] - guess[cut, :]) * (1.0 / COARSE_SCALE[f])))
     change = jnp.concatenate(parts, axis=0)
-    i, j = sublanes((3 * ROWS, 48)), lanes((3 * ROWS, 48))
-    repeat_rows = jnp.where(i // 4 == j, 1.0, 0.0)
     i, j = sublanes((128, COLS)), lanes((128, COLS))
-    repeat_cols = jnp.where(i == j // 4, 1.0, 0.0)
-    change = exact_dot(dot_exact(repeat_rows, change), repeat_cols)
+    change = exact_dot(change, jnp.where(i == j // 4, 1.0, 0.0))
     for f in range(3):
-        out[f] = fine[f] + change[ROWS * f : ROWS * f + ROWS, :]
+        for c in range(4):
+            cut = slice(128 * c, 128 * c + 128)
+            for k in range(4):
+                spread[f, c, pl.ds(k, CROWS, stride=4), :] = change[16 * f : 16 * f + 16, cut]
+            out[f, :, cut] = fine[f, :, cut] + spread[f, c]
 
 
 SMEM = pl.BlockSpec(memory_space=pltpu.SMEM)
@@ -542,20 +555,22 @@
     rows_a = swap(send_a, "sx", x_a)
     rows_b = swap(send_b, "sx", x_b)
     blocks = (at, held, coarse_nu, cols_a, cols_b, rows_a, rows_b)
-    field = (3, 2, 64, 128)
-    state, moved, extra, coef = call(
-        low_kernel, blocks + (chain_push,),
-        [(64, 128), (48, 128), (3 * HALF, 2, EXT, 128), (4, 2, EXT, 128)],
-        [field, field, (HALF, 3, 64, 128)],
-    )
-    state = lax.ppermute(state, "cuts", [(m, (m + 4 if m >= 4 else m + 12)) for m in range(HALF)])
-    state_a = swap_high(state, count_x, x_a)
+    field, planes, terms = (3, 2, 64, 128), (3 * HALF, 2, EXT, 128), (4, 2, EXT, 128)
+    state, moved = call(
+        low_kernel, blocks + (chain_push,), [(64, 128), (48, 128)], [planes, terms, field, field, (HALF, 3, 64, 128)])
+    goes = [(m, m + 4 if m >= 4 else m + 12) for m in range(HALF)]
+    state_b, state_a = [
+        lax.ppermute(state, ("cuts", "sx"), [(m * count_x + i, n * count_x + (i ^ flip)) for m, n in goes for i in range(count_x)])
+        for flip in (0, 1)
+    ]
+    state = state_b
     state_b = swap_high(state, count_x, x_b)
+    extra, coef = call(planes_kernel, blocks, [planes, terms])
     (out,) = call(
         high_kernel,
         (at, state, state_a, state_b, extra, coef, chain_push, fine, guess, moved),
         [(3, ROWS, COLS)],
-        [field, field, (HALF, 3, 64, 128), (48, 128)],
+        [field, field, (HALF, 3, 64, 128), (48, 128), (3, 4, ROWS, 128)],
     )
     return out[None]
 

time: 82 us -> 79.9 us (0.974)
  the two profiles are of different devices: /device:TPU:297 before, /device:TPU:307 now
where the time goes in v6:
time: 79.9 us; the launch traced here: 79.3 us
  starting transfers between devices  32.2 us (40%)
  waiting for transfers between devices  15.7 us (20%)
  blocking collectives  14.5 us (18%)
  Pallas kernels  13.1 us (16%)
  local copies, waits for them, and re-layouts  3.58 us (4%)
    ppermute x8, starting transfers between devices, swap(): lax.ppermute(x, axis, [(a, b) for a, b in pairs] + [(b, a) for a, b in pa...  25.7 us
    all_to_all x1, blocking collectives, on_device(): held = lax.all_to_all(sent, 'cuts', 0, 0, axis_index_groups=halves)  14.5 us
    pallas_call x10, Pallas kernels, call(): pl.pallas_call(kernel, out_shape=shapes, in_specs=[SMEM] + [VMEM] * near...  13.1 us
    ppermute x8, waiting for transfers between devices, swap(): lax.ppermute(x, axis, [(a, b) for a, b in pairs] + [(b, a) for a, b in pa...  7.86 us
    ppermute x2, waiting for transfers between devices, on_device(): lax.ppermute(state, ('cuts', 'sx'), [(m * count_x + i, n * count_x + (i ^...  6.75 us
    ppermute x1, starting transfers between devices, swap_high(): lax.ppermute(x, ('cuts', 'sx'), [(n * count + a, n * count + b) for n in...  3.88 us
    ppermute x2, starting transfers between devices, on_device(): lax.ppermute(state, ('cuts', 'sx'), [(m * count_x + i, n * count_x + (i ^...  2.58 us
    unnamed x10, local copies, waits for them, and re-layouts  1.91 us
  transfers between devices with their start and end apart: 11, of which 6 were waited for; matrix products, arithmetic and copies ran while one was open for 0% of the time, Pallas kernels for 5%

profile of v6, /device:TPU:307, one launch (start us, length us, event | category | flops | bytes accessed | tf_op | source)
XLA Modules:
  0.0 79.3 jit_solution(3364239091111014665)
XLA Ops:
  0.0 0.8 %dynamic-slice_bitcast_fusion = (f32[3,8,512]{2,1,0:T(8,128)S(1)}, f32[3,8,512]{2,1,0:T(8,128)S(1)}) fusion(f32[1,3,64,512]{3,2,1,0:T(8,128)} %param.5, s32[]{:T(128)S(6)} %select_n.17, s32[]{:T(128)S(6)} %select_n.16), kind=kLoop, calls=%fused_computation.2 | loop fusion | bytes 196616 | tf_op jit(solution)/shard_map/dynamic_slice | solution.py:159
  0.9 0.7 dynamic-slice_bitcast_fusion.2
  1.6 3.7 %collective-permute-start.1 = (f32[4,8,512]{2,1,0:T(8,128)S(1)}, f32[4,8,512]{2,1,0:T(8,128)S(1)}, u32[]{:S(2)}, u32[]{:S(2)}) collective-permute-start(f32[4,8,512]{2,1,0:T(8,128)S(1)} %pad_maximum_fusion.1), channel_id=1, source_target_pairs={{4,8},{12,16},{20,24},{8,4},{16,12},{24,20},{5,9},{13,17},{21,25},... | collective-permute-start | bytes 196616 | tf_op jit(solution)/shard_map/ppermute | solution.py:510
  5.3 1.9 %collective-permute-start = (f32[4,8,512]{2,1,0:T(8,128)S(1)}, f32[4,8,512]{2,1,0:T(8,128)S(1)}, u32[]{:S(2)}, u32[]{:S(2)}) collective-permute-start(f32[4,8,512]{2,1,0:T(8,128)S(1)} %pad_maximum_fusion), channel_id=1, source_target_pairs={{0,4},{8,12},{16,20},{24,28},{4,0},{12,8},{20,16},{28,24},{1,5},{9... | collective-permute-start | bytes 196616 | tf_op jit(solution)/shard_map/ppermute | solution.py:510
  7.3 1.0 %copy-done = f32[1,3,64,512]{3,2,1,0:T(8,128)S(1)} copy-done((f32[1,3,64,512]{3,2,1,0:T(8,128)S(1)}, f32[1,3,64,512]{3,2,1,0:T(8,128)}, u32[]{:S(2)}) %copy-start) | copy-done | bytes 393240
  8.3 0.9 %copy-done.1 = f32[64,512]{1,0:T(8,128)S(1)} copy-done((f32[64,512]{1,0:T(8,128)S(1)}, f32[64,512]{1,0:T(8,128)}, u32[]{:S(2)}) %copy-start.1) | copy-done | bytes 131096
  9.2 0.7 shard_map.55.own
  10.0 0.7 shard_map.56
  10.7 2.9 %collective-permute-start.2 = (f32[80,128]{1,0:T(8,128)S(1)}, f32[80,128]{1,0:T(8,128)S(1)}, u32[]{:S(2)}, u32[]{:S(2)}) collective-permute-start(f32[80,128]{1,0:T(8,128)S(1)} %get-tuple-element.21), channel_id=1, source_target_pairs={{0,1},{2,3},{1,0},{3,2},{4,5},{6,7},{5,4},{7,6},{8,9},{10,11},{9,8... | collective-permute-start | bytes 122888 | tf_op jit(solution)/shard_map/ppermute | solution.py:510
  13.6 1.9 %collective-permute-start.3 = (f32[80,128]{1,0:T(8,128)S(1)}, f32[80,128]{1,0:T(8,128)S(1)}, u32[]{:S(2)}, u32[]{:S(2)}) collective-permute-start(f32[80,128]{1,0:T(8,128)S(1)} %get-tuple-element.22), channel_id=1, source_target_pairs={{1,2},{2,1},{5,6},{6,5},{9,10},{10,9},{13,14},{14,13},{17,18},{18,... | collective-permute-start | bytes 122888 | tf_op jit(solution)/shard_map/ppermute | solution.py:510
  15.6 1.1 %shard_map.57 = (f32[2,5,96,128]{3,2,1,0:T(8,128)S(1)}, f32[2,2,40,128]{3,2,1,0:T(8,128)S(1)}) custom-call(s32[5]{0:T(128)S(1)} %stack.15.at, s32[1,64]{1,0:T(1,128)S(1)} %bitcast.16, s32[1,64]{1,0:T(1,128)S(1)} %bitcast.18, s32[16,64]{1,0:T(8,128)S(1)} %copy-done.2), custom_call_target="tpu_custom_call" | custom-call | tf_op jit(solution)/shard_map/pallas_call | solution.py:499
  16.7 1.7 %collective-permute-done.3.cols_b = f32[80,128]{1,0:T(8,128)S(1)} collective-permute-done((f32[80,128]{1,0:T(8,128)S(1)}, f32[80,128]{1,0:T(8,128)S(1)}, u32[]{:S(2)}, u32[]{:S(2)}) %collective-permute-start.3) | collective-permute-done | bytes 40992 | tf_op jit(solution)/shard_map/ppermute | solution.py:510
  18.3 3.0 %shard_map.58 = (f32[3,64,512]{2,1,0:T(8,128)S(1)}, f32[48,128]{1,0:T(8,128)S(1)}, f32[8,48,128]{2,1,0:T(8,128)S(1)}, f32[16,128]{1,0:T(8,128)S(1)}) custom-call(s32[5]{0:T(128)S(1)} %stack.15.at, f32[4,4,64,128]{3,2,1,0:T(8,128)S(1)} %shard_map.55.own, f32[4,8,512]{2,1,0:T(8,128)S(1)} %collective-permute-done.got_a.rows_a, ...), custom_call_target="tpu_custom_call" | custom-call | tf_op jit(solution)/shard_map/pallas_call | solution.py:499
  21.3 14.5 %all_to_all.5.held = f32[8,48,128]{2,1,0:T(8,128)S(1)} all-to-all(f32[8,48,128]{2,1,0:T(8,128)S(1)} %get-tuple-element.25), channel_id=1, replica_groups={{0,32,64,96,128,160,192,224},{256,288,320,352,384,416,448,480},{1,33,65..., dimensions={0} | all-to-all | bytes 393216 | tf_op jit(solution)/shard_map/all_to_all | solution.py:548
  35.8 0.7 shard_map.59
  36.5 1.9 %collective-permute-start.4 = (f32[112,128]{1,0:T(8,128)S(1)}, f32[112,128]{1,0:T(8,128)S(1)}, u32[]{:S(2)}, u32[]{:S(2)}) collective-permute-start(f32[112,128]{1,0:T(8,128)S(1)} %get-tuple-element.27), channel_id=1, source_target_pairs={{0,1},{2,3},{1,0},{3,2},{4,5},{6,7},{5,4},{7,6},{8,9},{10,11},{9,8... | collective-permute-start | bytes 172040 | tf_op jit(solution)/shard_map/ppermute | solution.py:510
  38.5 1.9 %collective-permute-start.5 = (f32[112,128]{1,0:T(8,128)S(1)}, f32[112,128]{1,0:T(8,128)S(1)}, u32[]{:S(2)}, u32[]{:S(2)}) collective-permute-start(f32[112,128]{1,0:T(8,128)S(1)} %get-tuple-element.28), channel_id=1, source_target_pairs={{1,2},{2,1},{5,6},{6,5},{9,10},{10,9},{13,14},{14,13},{17,18},{18,... | collective-permute-start | bytes 172040 | tf_op jit(solution)/shard_map/ppermute | solution.py:510
  40.4 1.1 %collective-permute-done.4.cols_a = f32[112,128]{1,0:T(8,128)S(1)} collective-permute-done((f32[112,128]{1,0:T(8,128)S(1)}, f32[112,128]{1,0:T(8,128)S(1)}, u32[]{:S(2)}, u32[]{:S(2)}) %collective-permute-start.4) | collective-permute-done | bytes 57376 | tf_op jit(solution)/shard_map/ppermute | solution.py:510
  41.5 1.9 %collective-permute-done.5.cols_b = f32[112,128]{1,0:T(8,128)S(1)} collective-permute-done((f32[112,128]{1,0:T(8,128)S(1)}, f32[112,128]{1,0:T(8,128)S(1)}, u32[]{:S(2)}, u32[]{:S(2)}) %collective-permute-start.5) | collective-permute-done | bytes 57376 | tf_op jit(solution)/shard_map/ppermute | solution.py:510
  43.4 0.6 shard_map.60
  44.0 8.7 %collective-permute-start.6 = (f32[400,128]{1,0:T(8,128)S(1)}, f32[400,128]{1,0:T(8,128)S(1)}, u32[]{:S(2)}, u32[]{:S(2)}) collective-permute-start(f32[400,128]{1,0:T(8,128)S(1)} %get-tuple-element.29), channel_id=1, source_target_pairs={{0,4},{8,12},{16,20},{24,28},{4,0},{12,8},{20,16},{28,24},{1,5},{9... | collective-permute-start | bytes 614408 | tf_op jit(solution)/shard_map/ppermute | solution.py:510
  52.7 2.7 %collective-permute-start.7 = (f32[400,128]{1,0:T(8,128)S(1)}, f32[400,128]{1,0:T(8,128)S(1)}, u32[]{:S(2)}, u32[]{:S(2)}) collective-permute-start(f32[400,128]{1,0:T(8,128)S(1)} %get-tuple-element.30), channel_id=1, source_target_pairs={{4,8},{12,16},{20,24},{8,4},{16,12},{24,20},{5,9},{13,17},{21,25},... | collective-permute-start | bytes 614408 | tf_op jit(solution)/shard_map/ppermute | solution.py:510
  55.4 1.2 %shard_map.61.push = f32[8,2,2,48,128]{4,3,2,1,0:T(8,128)S(1)} custom-call(s32[5]{0:T(128)S(1)} %stack.15.at, s32[1,64]{1,0:T(1,128)S(1)} %bitcast.17, s32[1,64]{1,0:T(1,128)S(1)} %bitcast.19, s32[16,64]{1,0:T(8,128)S(1)} %copy-done.2), custom_call_target="tpu_custom_call" | custom-call | tf_op jit(solution)/shard_map/pallas_call | solution.py:499
  56.6 3.2 %collective-permute-done.7.rows_b = f32[400,128]{1,0:T(8,128)S(1)} collective-permute-done((f32[400,128]{1,0:T(8,128)S(1)}, f32[400,128]{1,0:T(8,128)S(1)}, u32[]{:S(2)}, u32[]{:S(2)}) %collective-permute-start.7) | collective-permute-done | bytes 204832 | tf_op jit(solution)/shard_map/ppermute | solution.py:510
  59.8 0.5 shard_map.62
  60.3 1.3 %collective-permute-start.8 = (f32[64,128]{1,0:T(8,128)S(1)}, f32[64,128]{1,0:T(8,128)S(1)}, u32[]{:S(2)}, u32[]{:S(2)}) collective-permute-start(f32[64,128]{1,0:T(8,128)S(1)} %get-tuple-element.31), channel_id=1, source_target_pairs={{0,384},{4,388},{8,392},{12,396},{16,400},{20,404},{24,408},{28,41... | collective-permute-start | bytes 98312 | tf_op jit(solution)/shard_map/ppermute | solution.py:563
  61.6 1.3 %collective-permute-start.9 = (f32[64,128]{1,0:T(8,128)S(1)}, f32[64,128]{1,0:T(8,128)S(1)}, u32[]{:S(2)}, u32[]{:S(2)}) collective-permute-start(f32[64,128]{1,0:T(8,128)S(1)} %get-tuple-element.31), channel_id=1, source_target_pairs={{0,388},{4,384},{8,396},{12,392},{16,404},{20,400},{24,412},{28,40... | collective-permute-start | bytes 98312 | tf_op jit(solution)/shard_map/ppermute | solution.py:563
  62.9 6.7 %collective-permute-done.8.state = f32[64,128]{1,0:T(8,128)S(1)} collective-permute-done((f32[64,128]{1,0:T(8,128)S(1)}, f32[64,128]{1,0:T(8,128)S(1)}, u32[]{:S(2)}, u32[]{:S(2)}) %collective-permute-start.8) | collective-permute-done | bytes 32800 | tf_op jit(solution)/shard_map/ppermute | solution.py:563
  69.7 3.9 %collective-permute-start.10 = (f32[64,128]{1,0:T(8,128)S(1)}, f32[64,128]{1,0:T(8,128)S(1)}, u32[]{:S(2)}, u32[]{:S(2)}) collective-permute-start(f32[64,128]{1,0:T(8,128)S(1)} %collective-permute-done.8.state), channel_id=1, source_target_pairs={{260,264},{268,272},{276,280},{264,260},{272,268},{280,276},{292,2... | collective-permute-start | bytes 98312 | tf_op jit(solution)/shard_map/ppermute | solution.py:515
  73.5 0.8 %shard_map.63 = (f32[24,2,48,128]{3,2,1,0:T(8,128)S(1)}, f32[4,2,48,128]{3,2,1,0:T(8,128)S(1)}) custom-call(s32[5]{0:T(128)S(1)} %stack.15.at, f32[8,48,128]{2,1,0:T(8,128)S(1)} %all_to_all.5.held, f32[16,128]{1,0:T(8,128)S(1)} %get-tuple-element.26.nu, f32[112,128]{1,0:T(8,128)S(1)} %collective-permute-done.4.cols_a, ...), custom_call_target="tpu_custom_call" | custom-call | tf_op jit(solution)/shard_map/pallas_call | solution.py:499
  74.4 1.1 %collective-permute-done.10.state_b = f32[64,128]{1,0:T(8,128)S(1)} collective-permute-done((f32[64,128]{1,0:T(8,128)S(1)}, f32[64,128]{1,0:T(8,128)S(1)}, u32[]{:S(2)}, u32[]{:S(2)}) %collective-permute-start.10) | collective-permute-done | bytes 32800 | tf_op jit(solution)/shard_map/ppermute | solution.py:515
  75.4 3.9 %shard_map.64 = f32[3,64,512]{2,1,0:T(8,128)} custom-call(s32[5]{0:T(128)S(1)} %stack.15.at, f32[64,128]{1,0:T(8,128)S(1)} %collective-permute-done.8.state, f32[64,128]{1,0:T(8,128)S(1)} %collective-permute-done.9.state_a, f32[64,128]{1,0:T(8,128)S(1)} %collective-permute-done.10.state_b, f32[24,2,48,128]{3,2,1,0:T(8,128)S(1)} %get-tuple-element.32.extra, ...), custom_call_target="tpu_custom_call" | custom-call | tf_op jit(solution)/shard_map/pallas_call | solution.py:499
  (16 shorter events, 0.1 us)
Async XLA Ops:
  0.0 15.5 %copy-start.3 = (s32[64]{0:T(128)S(1)}, s32[64]{0:T(128)}, u32[]{:S(2)}) copy-start(s32[64]{0:T(128)} %param.7) | copy-start | bytes 772
  0.0 15.5 %copy-start.4 = (s32[64]{0:T(128)S(1)}, s32[64]{0:T(128)}, u32[]{:S(2)}) copy-start(s32[64]{0:T(128)} %param.8) | copy-start | bytes 772
  0.0 15.5 %copy-start.2 = (s32[16,64]{1,0:T(8,128)S(1)}, s32[16,64]{1,0:T(8,128)}, u32[]{:S(2)}) copy-start(s32[16,64]{1,0:T(8,128)} %yaw_in.3) | copy-start | bytes 12292
  1.6 8.3 %collective-permute-start.1 = (f32[4,8,512]{2,1,0:T(8,128)S(1)}, f32[4,8,512]{2,1,0:T(8,128)S(1)}, u32[]{:S(2)}, u32[]{:S(2)}) collective-permute-start(f32[4,8,512]{2,1,0:T(8,128)S(1)} %pad_maximum_fusion.1), channel_id=1, source_target_pairs={{4,8},{12,16},{20,24},{8,4},{16,12},{24,20},{5,9},{13,17},{21,25},... | collective-permute-start | bytes 196616 | tf_op jit(solution)/shard_map/ppermute | solution.py:510
  5.3 4.6 %collective-permute-start = (f32[4,8,512]{2,1,0:T(8,128)S(1)}, f32[4,8,512]{2,1,0:T(8,128)S(1)}, u32[]{:S(2)}, u32[]{:S(2)}) collective-permute-start(f32[4,8,512]{2,1,0:T(8,128)S(1)} %pad_maximum_fusion), channel_id=1, source_target_pairs={{0,4},{8,12},{16,20},{24,28},{4,0},{12,8},{20,16},{28,24},{1,5},{9... | collective-permute-start | bytes 196616 | tf_op jit(solution)/shard_map/ppermute | solution.py:510
  7.3 1.0 %copy-start = (f32[1,3,64,512]{3,2,1,0:T(8,128)S(1)}, f32[1,3,64,512]{3,2,1,0:T(8,128)}, u32[]{:S(2)}) copy-start(f32[1,3,64,512]{3,2,1,0:T(8,128)} %param.5) | copy-start | bytes 1179652
  8.3 0.9 %copy-start.1 = (f32[64,512]{1,0:T(8,128)S(1)}, f32[64,512]{1,0:T(8,128)}, u32[]{:S(2)}) copy-start(f32[64,512]{1,0:T(8,128)} %visc.1) | copy-start | bytes 393220
  10.7 6.0 %collective-permute-start.2 = (f32[80,128]{1,0:T(8,128)S(1)}, f32[80,128]{1,0:T(8,128)S(1)}, u32[]{:S(2)}, u32[]{:S(2)}) collective-permute-start(f32[80,128]{1,0:T(8,128)S(1)} %get-tuple-element.21), channel_id=1, source_target_pairs={{0,1},{2,3},{1,0},{3,2},{4,5},{6,7},{5,4},{7,6},{8,9},{10,11},{9,8... | collective-permute-start | bytes 122888 | tf_op jit(solution)/shard_map/ppermute | solution.py:510
  13.6 4.7 %collective-permute-start.3 = (f32[80,128]{1,0:T(8,128)S(1)}, f32[80,128]{1,0:T(8,128)S(1)}, u32[]{:S(2)}, u32[]{:S(2)}) collective-permute-start(f32[80,128]{1,0:T(8,128)S(1)} %get-tuple-element.22), channel_id=1, source_target_pairs={{1,2},{2,1},{5,6},{6,5},{9,10},{10,9},{13,14},{14,13},{17,18},{18,... | collective-permute-start | bytes 122888 | tf_op jit(solution)/shard_map/ppermute | solution.py:510
  36.5 4.9 %collective-permute-start.4 = (f32[112,128]{1,0:T(8,128)S(1)}, f32[112,128]{1,0:T(8,128)S(1)}, u32[]{:S(2)}, u32[]{:S(2)}) collective-permute-start(f32[112,128]{1,0:T(8,128)S(1)} %get-tuple-element.27), channel_id=1, source_target_pairs={{0,1},{2,3},{1,0},{3,2},{4,5},{6,7},{5,4},{7,6},{8,9},{10,11},{9,8... | collective-permute-start | bytes 172040 | tf_op jit(solution)/shard_map/ppermute | solution.py:510
  38.5 4.9 %collective-permute-start.5 = (f32[112,128]{1,0:T(8,128)S(1)}, f32[112,128]{1,0:T(8,128)S(1)}, u32[]{:S(2)}, u32[]{:S(2)}) collective-permute-start(f32[112,128]{1,0:T(8,128)S(1)} %get-tuple-element.28), channel_id=1, source_target_pairs={{1,2},{2,1},{5,6},{6,5},{9,10},{10,9},{13,14},{14,13},{17,18},{18,... | collective-permute-start | bytes 172040 | tf_op jit(solution)/shard_map/ppermute | solution.py:510
  44.0 12.6 %collective-permute-start.6 = (f32[400,128]{1,0:T(8,128)S(1)}, f32[400,128]{1,0:T(8,128)S(1)}, u32[]{:S(2)}, u32[]{:S(2)}) collective-permute-start(f32[400,128]{1,0:T(8,128)S(1)} %get-tuple-element.29), channel_id=1, source_target_pairs={{0,4},{8,12},{16,20},{24,28},{4,0},{12,8},{20,16},{28,24},{1,5},{9... | collective-permute-start | bytes 614408 | tf_op jit(solution)/shard_map/ppermute | solution.py:510
  52.7 7.1 %collective-permute-start.7 = (f32[400,128]{1,0:T(8,128)S(1)}, f32[400,128]{1,0:T(8,128)S(1)}, u32[]{:S(2)}, u32[]{:S(2)}) collective-permute-start(f32[400,128]{1,0:T(8,128)S(1)} %get-tuple-element.30), channel_id=1, source_target_pairs={{4,8},{12,16},{20,24},{8,4},{16,12},{24,20},{5,9},{13,17},{21,25},... | collective-permute-start | bytes 614408 | tf_op jit(solution)/shard_map/ppermute | solution.py:510
  60.3 9.3 %collective-permute-start.8 = (f32[64,128]{1,0:T(8,128)S(1)}, f32[64,128]{1,0:T(8,128)S(1)}, u32[]{:S(2)}, u32[]{:S(2)}) collective-permute-start(f32[64,128]{1,0:T(8,128)S(1)} %get-tuple-element.31), channel_id=1, source_target_pairs={{0,384},{4,388},{8,392},{12,396},{16,400},{20,404},{24,408},{28,41... | collective-permute-start | bytes 98312 | tf_op jit(solution)/shard_map/ppermute | solution.py:563
  61.6 12.7 %collective-permute-start.9 = (f32[64,128]{1,0:T(8,128)S(1)}, f32[64,128]{1,0:T(8,128)S(1)}, u32[]{:S(2)}, u32[]{:S(2)}) collective-permute-start(f32[64,128]{1,0:T(8,128)S(1)} %get-tuple-element.31), channel_id=1, source_target_pairs={{0,388},{4,384},{8,396},{12,392},{16,404},{20,400},{24,412},{28,40... | collective-permute-start | bytes 98312 | tf_op jit(solution)/shard_map/ppermute | solution.py:563
  69.7 5.8 %collective-permute-start.10 = (f32[64,128]{1,0:T(8,128)S(1)}, f32[64,128]{1,0:T(8,128)S(1)}, u32[]{:S(2)}, u32[]{:S(2)}) collective-permute-start(f32[64,128]{1,0:T(8,128)S(1)} %collective-permute-done.8.state), channel_id=1, source_target_pairs={{260,264},{268,272},{276,280},{264,260},{272,268},{280,276},{292,2... | collective-permute-start | bytes 98312 | tf_op jit(solution)/shard_map/ppermute | solution.py:515

commit v7 on v6

--- a/solution.py
+++ b/solution.py
@@ -146,14 +146,6 @@
         copy.wait()
 
 
-def load_kernel(at, start, visc, own, sems):
-    fetch(
-        [(start.at[:, :, 128 * c : 128 * c + 128], own.at[0:3, c]) for c in range(4)]
-        + [(visc.at[:, 128 * c : 128 * c + 128], own.at[3, c]) for c in range(4)],
-        sems,
-    )
-
-
 def edge_rows(start, visc, first):
     return jnp.concatenate([
         lax.dynamic_slice(start, (0, first, 0), (3, 8, COLS)),
@@ -170,7 +162,7 @@
         right = jnp.zeros((count, 128), F32)
         for f in range(4):
             if r0 == 8:
-                a, b = own[f, 0], own[f, 3]
+                a, b = own[f, :, 0:128], own[f, :, COLS - 128 : COLS]
             else:
                 from_a = jnp.logical_xor(even_x, r0 == 0)
                 a = jnp.where(from_a, got_a[f, :, 0:128], got_b[f, :, 0:128])
@@ -249,7 +241,7 @@
             if c < 4:
                 cut = slice(128 * c, 128 * c + 128)
                 a, b = rows_a[f, :, cut], rows_b[f, :, cut]
-                pieces = [(8, 8, jnp.where(even_x, b, a)), (16, 64, own[f, c]), (80, 8, jnp.where(even_x, a, b))]
+                pieces = [(8, 8, jnp.where(even_x, b, a)), (16, 64, own[f, :, cut]), (80, 8, jnp.where(even_x, a, b))]
             else:
                 after, before = rolled(after_all, -8 * f), rolled(before_all, 120 - 8 * f)
                 pieces = [(8, 80, jnp.where(lane < 8, after, jnp.where(lane >= 120, before, 0.0)))]
@@ -426,7 +418,7 @@
                 clear_rows(dst, 2, 8 + 15, 8 + 32, outside)
 
 
-def low_kernel(at, held, nu, cols_a, cols_b, rows_a, rows_b, push, state, moved, extra, coef, one, two, kept):
+def low_kernel(at, held, nu, cols_a, cols_b, rows_b, rows_a, push, state, moved, extra, coef, one, two, kept):
     @pl.when(at[0] < HALF)
     def _():
         assemble(at, held, nu, cols_a, cols_b, rows_a, rows_b, putter(extra, coef))
@@ -444,7 +436,7 @@
             moved[16 * f : 16 * f + 16, :] = kept[jnp.maximum(at[0], 1), f, 24:40, :]
 
 
-def planes_kernel(at, held, nu, cols_a, cols_b, rows_a, rows_b, extra, coef):
+def planes_kernel(at, held, nu, cols_a, cols_b, rows_b, rows_a, extra, coef):
     @pl.when(at[0] >= HALF)
     def _():
         assemble(at, held, nu, cols_a, cols_b, rows_a, rows_b, putter(extra, coef))
@@ -532,7 +524,7 @@
     odd = at[1] % 2
     rows_b = swap(edge_rows(start, viscosity, 56 * odd), "sx", x_b)
     rows_a = swap(edge_rows(start, viscosity, 56 * (1 - odd)), "sx", x_a)
-    (own,) = call(load_kernel, (at, start, viscosity), [(4, 4, ROWS, 128)], far=2, sems=8)
+    own = jnp.concatenate([start, viscosity[None]])
     send_a, send_b = call(side_kernel, (at, own, rows_a, rows_b), [(80, 128)] * 2)
     cols_a = swap(send_a, "sy", y_a)
     cols_b = swap(send_b, "sy", y_b)
@@ -554,7 +546,7 @@
     send_a, send_b = call(rows_kernel, (at, held, coarse_nu, cols_a, cols_b), [(MESSAGE, 128)] * 2)
     rows_a = swap(send_a, "sx", x_a)
     rows_b = swap(send_b, "sx", x_b)
-    blocks = (at, held, coarse_nu, cols_a, cols_b, rows_a, rows_b)
+    blocks = (at, held, coarse_nu, cols_a, cols_b, rows_b, rows_a)
     field, planes, terms = (3, 2, 64, 128), (3 * HALF, 2, EXT, 128), (4, 2, EXT, 128)
     state, moved = call(
         low_kernel, blocks + (chain_push,), [(64, 128), (48, 128)], [planes, terms, field, field, (HALF, 3, 64, 128)])

time: 79.9 us -> 77.6 us (0.971)
  the two profiles are of different devices: /device:TPU:307 before, /device:TPU:401 now
where the time goes in v7:
time: 77.6 us; the launch traced here: 77 us
  starting transfers between devices  35.6 us (46%)
  blocking collectives  14.2 us (18%)
  Pallas kernels  12.4 us (16%)
  waiting for transfers between devices  11.8 us (15%)
  local copies, waits for them, and re-layouts  1.68 us (2%)
  other arithmetic  1.12 us (1%)
    ppermute x8, starting transfers between devices, swap(): lax.ppermute(x, axis, [(a, b) for a, b in pairs] + [(b, a) for a, b in pa...  24 us
    all_to_all x1, blocking collectives, on_device(): held = lax.all_to_all(sent, 'cuts', 0, 0, axis_index_groups=halves)  14.2 us
    pallas_call x9, Pallas kernels, call(): pl.pallas_call(kernel, out_shape=shapes, in_specs=[SMEM] + [VMEM] * near...  12.4 us
    ppermute x1, starting transfers between devices, swap_high(): lax.ppermute(x, ('cuts', 'sx'), [(n * count + a, n * count + b) for n in...  9.05 us
    ppermute x2, waiting for transfers between devices, on_device(): lax.ppermute(state, ('cuts', 'sx'), [(m * count_x + i, n * count_x + (i ^...  5.99 us
    ppermute x8, waiting for transfers between devices, swap(): lax.ppermute(x, axis, [(a, b) for a, b in pairs] + [(b, a) for a, b in pa...  5 us
    ppermute x2, starting transfers between devices, on_device(): lax.ppermute(state, ('cuts', 'sx'), [(m * count_x + i, n * count_x + (i ^...  2.58 us
  transfers between devices with their start and end apart: 11, of which 6 were waited for; matrix products, arithmetic and copies ran while one was open for 2% of the time, Pallas kernels for 4%

profile of v7, /device:TPU:401, one launch (start us, length us, event | category | flops | bytes accessed | tf_op | source)
XLA Modules:
  0.0 77.0 jit_solution(8669900482997613650)
XLA Ops:
  0.0 0.8 %dynamic-slice_bitcast_fusion = (f32[3,8,512]{2,1,0:T(8,128)S(1)}, f32[3,8,512]{2,1,0:T(8,128)S(1)}) fusion(f32[1,3,64,512]{3,2,1,0:T(8,128)} %param.5, s32[]{:T(128)S(6)} %select_n.17, s32[]{:T(128)S(6)} %select_n.16), kind=kLoop, calls=%fused_computation.3 | loop fusion | bytes 196616 | tf_op jit(solution)/shard_map/dynamic_slice | solution.py:151
  0.9 0.7 dynamic-slice_bitcast_fusion.2
  1.6 3.7 %collective-permute-start.1 = (f32[4,8,512]{2,1,0:T(8,128)S(1)}, f32[4,8,512]{2,1,0:T(8,128)S(1)}, u32[]{:S(2)}, u32[]{:S(2)}) collective-permute-start(f32[4,8,512]{2,1,0:T(8,128)S(1)} %pad_maximum_fusion.2), channel_id=1, source_target_pairs={{4,8},{12,16},{20,24},{8,4},{16,12},{24,20},{5,9},{13,17},{21,25},... | collective-permute-start | bytes 196616 | tf_op jit(solution)/shard_map/ppermute | solution.py:502
  5.3 1.9 %collective-permute-start = (f32[4,8,512]{2,1,0:T(8,128)S(1)}, f32[4,8,512]{2,1,0:T(8,128)S(1)}, u32[]{:S(2)}, u32[]{:S(2)}) collective-permute-start(f32[4,8,512]{2,1,0:T(8,128)S(1)} %pad_maximum_fusion.1), channel_id=1, source_target_pairs={{0,4},{8,12},{16,20},{24,28},{4,0},{12,8},{20,16},{28,24},{1,5},{9... | collective-permute-start | bytes 196616 | tf_op jit(solution)/shard_map/ppermute | solution.py:502
  7.3 0.1 stack.15.at
  7.3 1.1 %pad_maximum_fusion.own = f32[4,64,512]{2,1,0:T(8,128)S(1)} fusion(f32[1,64,512]{2,1,0:T(8,128)} %bitcast.21, f32[3,64,512]{2,1,0:T(8,128)} %bitcast.20), kind=kLoop, calls=%fused_computation | loop fusion | flops 131072 | bytes 1048576 | tf_op jit(solution)/shard_map/concatenate | solution.py:527
  8.5 0.0 collective-permute-done.got_a.rows_a
  8.5 0.7 shard_map.55
  9.2 2.9 %collective-permute-start.2 = (f32[80,128]{1,0:T(8,128)S(1)}, f32[80,128]{1,0:T(8,128)S(1)}, u32[]{:S(2)}, u32[]{:S(2)}) collective-permute-start(f32[80,128]{1,0:T(8,128)S(1)} %get-tuple-element.21), channel_id=1, source_target_pairs={{0,1},{2,3},{1,0},{3,2},{4,5},{6,7},{5,4},{7,6},{8,9},{10,11},{9,8... | collective-permute-start | bytes 122888 | tf_op jit(solution)/shard_map/ppermute | solution.py:502
  12.1 1.9 %collective-permute-start.3 = (f32[80,128]{1,0:T(8,128)S(1)}, f32[80,128]{1,0:T(8,128)S(1)}, u32[]{:S(2)}, u32[]{:S(2)}) collective-permute-start(f32[80,128]{1,0:T(8,128)S(1)} %get-tuple-element.22), channel_id=1, source_target_pairs={{1,2},{2,1},{5,6},{6,5},{9,10},{10,9},{13,14},{14,13},{17,18},{18,... | collective-permute-start | bytes 122888 | tf_op jit(solution)/shard_map/ppermute | solution.py:502
  14.0 1.1 %shard_map.56 = (f32[2,5,96,128]{3,2,1,0:T(8,128)S(1)}, f32[2,2,40,128]{3,2,1,0:T(8,128)S(1)}) custom-call(s32[5]{0:T(128)S(1)} %stack.15.at, s32[1,64]{1,0:T(1,128)S(1)} %bitcast.16, s32[1,64]{1,0:T(1,128)S(1)} %bitcast.18, s32[16,64]{1,0:T(8,128)S(1)} %copy-done), custom_call_target="tpu_custom_call" | custom-call | tf_op jit(solution)/shard_map/pallas_call | solution.py:491
  15.2 1.7 %collective-permute-done.3.cols_b = f32[80,128]{1,0:T(8,128)S(1)} collective-permute-done((f32[80,128]{1,0:T(8,128)S(1)}, f32[80,128]{1,0:T(8,128)S(1)}, u32[]{:S(2)}, u32[]{:S(2)}) %collective-permute-start.3) | collective-permute-done | bytes 40992 | tf_op jit(solution)/shard_map/ppermute | solution.py:502
  16.8 3.0 %shard_map.57 = (f32[3,64,512]{2,1,0:T(8,128)S(1)}, f32[48,128]{1,0:T(8,128)S(1)}, f32[8,48,128]{2,1,0:T(8,128)S(1)}, f32[16,128]{1,0:T(8,128)S(1)}) custom-call(s32[5]{0:T(128)S(1)} %stack.15.at, f32[4,64,512]{2,1,0:T(8,128)S(1)} %pad_maximum_fusion.own, f32[4,8,512]{2,1,0:T(8,128)S(1)} %collective-permute-done.got_a.rows_a, ...), custom_call_target="tpu_custom_call" | custom-call | tf_op jit(solution)/shard_map/pallas_call | solution.py:491
  19.8 14.2 %all_to_all.5.held = f32[8,48,128]{2,1,0:T(8,128)S(1)} all-to-all(f32[8,48,128]{2,1,0:T(8,128)S(1)} %get-tuple-element.25), channel_id=1, replica_groups={{0,32,64,96,128,160,192,224},{256,288,320,352,384,416,448,480},{1,33,65..., dimensions={0} | all-to-all | bytes 393216 | tf_op jit(solution)/shard_map/all_to_all | solution.py:540
  34.0 0.7 shard_map.58
  34.7 1.9 %collective-permute-start.4 = (f32[112,128]{1,0:T(8,128)S(1)}, f32[112,128]{1,0:T(8,128)S(1)}, u32[]{:S(2)}, u32[]{:S(2)}) collective-permute-start(f32[112,128]{1,0:T(8,128)S(1)} %get-tuple-element.27), channel_id=1, source_target_pairs={{0,1},{2,3},{1,0},{3,2},{4,5},{6,7},{5,4},{7,6},{8,9},{10,11},{9,8... | collective-permute-start | bytes 172040 | tf_op jit(solution)/shard_map/ppermute | solution.py:502
  36.6 1.9 %collective-permute-start.5 = (f32[112,128]{1,0:T(8,128)S(1)}, f32[112,128]{1,0:T(8,128)S(1)}, u32[]{:S(2)}, u32[]{:S(2)}) collective-permute-start(f32[112,128]{1,0:T(8,128)S(1)} %get-tuple-element.28), channel_id=1, source_target_pairs={{1,2},{2,1},{5,6},{6,5},{9,10},{10,9},{13,14},{14,13},{17,18},{18,... | collective-permute-start | bytes 172040 | tf_op jit(solution)/shard_map/ppermute | solution.py:502
  38.6 1.0 %collective-permute-done.4.cols_a = f32[112,128]{1,0:T(8,128)S(1)} collective-permute-done((f32[112,128]{1,0:T(8,128)S(1)}, f32[112,128]{1,0:T(8,128)S(1)}, u32[]{:S(2)}, u32[]{:S(2)}) %collective-permute-start.4) | collective-permute-done | bytes 57376 | tf_op jit(solution)/shard_map/ppermute | solution.py:502
  39.6 1.9 %collective-permute-done.5.cols_b = f32[112,128]{1,0:T(8,128)S(1)} collective-permute-done((f32[112,128]{1,0:T(8,128)S(1)}, f32[112,128]{1,0:T(8,128)S(1)}, u32[]{:S(2)}, u32[]{:S(2)}) %collective-permute-start.5) | collective-permute-done | bytes 57376 | tf_op jit(solution)/shard_map/ppermute | solution.py:502
  41.5 0.6 shard_map.59
  42.1 7.8 %collective-permute-start.6 = (f32[400,128]{1,0:T(8,128)S(1)}, f32[400,128]{1,0:T(8,128)S(1)}, u32[]{:S(2)}, u32[]{:S(2)}) collective-permute-start(f32[400,128]{1,0:T(8,128)S(1)} %get-tuple-element.29), channel_id=1, source_target_pairs={{4,8},{12,16},{20,24},{8,4},{16,12},{24,20},{5,9},{13,17},{21,25},... | collective-permute-start | bytes 614408 | tf_op jit(solution)/shard_map/ppermute | solution.py:502
  49.9 1.9 %collective-permute-start.7 = (f32[400,128]{1,0:T(8,128)S(1)}, f32[400,128]{1,0:T(8,128)S(1)}, u32[]{:S(2)}, u32[]{:S(2)}) collective-permute-start(f32[400,128]{1,0:T(8,128)S(1)} %get-tuple-element.30), channel_id=1, source_target_pairs={{0,4},{8,12},{16,20},{24,28},{4,0},{12,8},{20,16},{28,24},{1,5},{9... | collective-permute-start | bytes 614408 | tf_op jit(solution)/shard_map/ppermute | solution.py:502
  51.8 1.2 %shard_map.60.push = f32[8,2,2,48,128]{4,3,2,1,0:T(8,128)S(1)} custom-call(s32[5]{0:T(128)S(1)} %stack.15.at, s32[1,64]{1,0:T(1,128)S(1)} %bitcast.17, s32[1,64]{1,0:T(1,128)S(1)} %bitcast.19, s32[16,64]{1,0:T(8,128)S(1)} %copy-done), custom_call_target="tpu_custom_call" | custom-call | tf_op jit(solution)/shard_map/pallas_call | solution.py:491
  53.0 0.3 collective-permute-done.6.rows_b
  53.3 0.5 shard_map.61
  53.9 1.3 %collective-permute-start.8 = (f32[64,128]{1,0:T(8,128)S(1)}, f32[64,128]{1,0:T(8,128)S(1)}, u32[]{:S(2)}, u32[]{:S(2)}) collective-permute-start(f32[64,128]{1,0:T(8,128)S(1)} %get-tuple-element.31), channel_id=1, source_target_pairs={{0,384},{4,388},{8,392},{12,396},{16,400},{20,404},{24,408},{28,41... | collective-permute-start | bytes 98312 | tf_op jit(solution)/shard_map/ppermute | solution.py:555
  55.2 1.3 %collective-permute-start.9 = (f32[64,128]{1,0:T(8,128)S(1)}, f32[64,128]{1,0:T(8,128)S(1)}, u32[]{:S(2)}, u32[]{:S(2)}) collective-permute-start(f32[64,128]{1,0:T(8,128)S(1)} %get-tuple-element.31), channel_id=1, source_target_pairs={{0,388},{4,384},{8,396},{12,392},{16,404},{20,400},{24,412},{28,40... | collective-permute-start | bytes 98312 | tf_op jit(solution)/shard_map/ppermute | solution.py:555
  56.5 6.0 %collective-permute-done.8.state = f32[64,128]{1,0:T(8,128)S(1)} collective-permute-done((f32[64,128]{1,0:T(8,128)S(1)}, f32[64,128]{1,0:T(8,128)S(1)}, u32[]{:S(2)}, u32[]{:S(2)}) %collective-permute-start.8) | collective-permute-done | bytes 32800 | tf_op jit(solution)/shard_map/ppermute | solution.py:555
  62.5 9.1 %collective-permute-start.10 = (f32[64,128]{1,0:T(8,128)S(1)}, f32[64,128]{1,0:T(8,128)S(1)}, u32[]{:S(2)}, u32[]{:S(2)}) collective-permute-start(f32[64,128]{1,0:T(8,128)S(1)} %collective-permute-done.8.state), channel_id=1, source_target_pairs={{260,264},{268,272},{276,280},{264,260},{272,268},{280,276},{292,2... | collective-permute-start | bytes 98312 | tf_op jit(solution)/shard_map/ppermute | solution.py:507
  71.5 0.8 %shard_map.62 = (f32[24,2,48,128]{3,2,1,0:T(8,128)S(1)}, f32[4,2,48,128]{3,2,1,0:T(8,128)S(1)}) custom-call(s32[5]{0:T(128)S(1)} %stack.15.at, f32[8,48,128]{2,1,0:T(8,128)S(1)} %all_to_all.5.held, f32[16,128]{1,0:T(8,128)S(1)} %get-tuple-element.26.nu, f32[112,128]{1,0:T(8,128)S(1)} %collective-permute-done.4.cols_a, ...), custom_call_target="tpu_custom_call" | custom-call | tf_op jit(solution)/shard_map/pallas_call | solution.py:491
  72.4 0.8 collective-permute-done.10.state_b
  73.1 3.9 %shard_map.63 = f32[3,64,512]{2,1,0:T(8,128)} custom-call(s32[5]{0:T(128)S(1)} %stack.15.at, f32[64,128]{1,0:T(8,128)S(1)} %collective-permute-done.8.state, f32[64,128]{1,0:T(8,128)S(1)} %collective-permute-done.9.state_a, f32[64,128]{1,0:T(8,128)S(1)} %collective-permute-done.10.state_b, f32[24,2,48,128]{3,2,1,0:T(8,128)S(1)} %get-tuple-element.32.extra, ...), custom_call_target="tpu_custom_call" | custom-call | tf_op jit(solution)/shard_map/pallas_call | solution.py:491
  (12 shorter events, 0.0 us)
Async XLA Ops:
  0.0 14.0 %copy-start.2 = (s32[64]{0:T(128)S(1)}, s32[64]{0:T(128)}, u32[]{:S(2)}) copy-start(s32[64]{0:T(128)} %param.8) | copy-start | bytes 772
  0.0 14.0 %copy-start.1 = (s32[64]{0:T(128)S(1)}, s32[64]{0:T(128)}, u32[]{:S(2)}) copy-start(s32[64]{0:T(128)} %param.7) | copy-start | bytes 772
  0.0 14.0 %copy-start = (s32[16,64]{1,0:T(8,128)S(1)}, s32[16,64]{1,0:T(8,128)}, u32[]{:S(2)}) copy-start(s32[16,64]{1,0:T(8,128)} %yaw_in.3) | copy-start | bytes 12292
  1.6 6.8 %collective-permute-start.1 = (f32[4,8,512]{2,1,0:T(8,128)S(1)}, f32[4,8,512]{2,1,0:T(8,128)S(1)}, u32[]{:S(2)}, u32[]{:S(2)}) collective-permute-start(f32[4,8,512]{2,1,0:T(8,128)S(1)} %pad_maximum_fusion.2), channel_id=1, source_target_pairs={{4,8},{12,16},{20,24},{8,4},{16,12},{24,20},{5,9},{13,17},{21,25},... | collective-permute-start | bytes 196616 | tf_op jit(solution)/shard_map/ppermute | solution.py:502
  5.3 3.1 %collective-permute-start = (f32[4,8,512]{2,1,0:T(8,128)S(1)}, f32[4,8,512]{2,1,0:T(8,128)S(1)}, u32[]{:S(2)}, u32[]{:S(2)}) collective-permute-start(f32[4,8,512]{2,1,0:T(8,128)S(1)} %pad_maximum_fusion.1), channel_id=1, source_target_pairs={{0,4},{8,12},{16,20},{24,28},{4,0},{12,8},{20,16},{28,24},{1,5},{9... | collective-permute-start | bytes 196616 | tf_op jit(solution)/shard_map/ppermute | solution.py:502
  9.2 6.0 %collective-permute-start.2 = (f32[80,128]{1,0:T(8,128)S(1)}, f32[80,128]{1,0:T(8,128)S(1)}, u32[]{:S(2)}, u32[]{:S(2)}) collective-permute-start(f32[80,128]{1,0:T(8,128)S(1)} %get-tuple-element.21), channel_id=1, source_target_pairs={{0,1},{2,3},{1,0},{3,2},{4,5},{6,7},{5,4},{7,6},{8,9},{10,11},{9,8... | collective-permute-start | bytes 122888 | tf_op jit(solution)/shard_map/ppermute | solution.py:502
  12.1 4.7 %collective-permute-start.3 = (f32[80,128]{1,0:T(8,128)S(1)}, f32[80,128]{1,0:T(8,128)S(1)}, u32[]{:S(2)}, u32[]{:S(2)}) collective-permute-start(f32[80,128]{1,0:T(8,128)S(1)} %get-tuple-element.22), channel_id=1, source_target_pairs={{1,2},{2,1},{5,6},{6,5},{9,10},{10,9},{13,14},{14,13},{17,18},{18,... | collective-permute-start | bytes 122888 | tf_op jit(solution)/shard_map/ppermute | solution.py:502
  34.7 4.9 %collective-permute-start.4 = (f32[112,128]{1,0:T(8,128)S(1)}, f32[112,128]{1,0:T(8,128)S(1)}, u32[]{:S(2)}, u32[]{:S(2)}) collective-permute-start(f32[112,128]{1,0:T(8,128)S(1)} %get-tuple-element.27), channel_id=1, source_target_pairs={{0,1},{2,3},{1,0},{3,2},{4,5},{6,7},{5,4},{7,6},{8,9},{10,11},{9,8... | collective-permute-start | bytes 172040 | tf_op jit(solution)/shard_map/ppermute | solution.py:502
  36.6 4.9 %collective-permute-start.5 = (f32[112,128]{1,0:T(8,128)S(1)}, f32[112,128]{1,0:T(8,128)S(1)}, u32[]{:S(2)}, u32[]{:S(2)}) collective-permute-start(f32[112,128]{1,0:T(8,128)S(1)} %get-tuple-element.28), channel_id=1, source_target_pairs={{1,2},{2,1},{5,6},{6,5},{9,10},{10,9},{13,14},{14,13},{17,18},{18,... | collective-permute-start | bytes 172040 | tf_op jit(solution)/shard_map/ppermute | solution.py:502
  42.1 11.2 %collective-permute-start.6 = (f32[400,128]{1,0:T(8,128)S(1)}, f32[400,128]{1,0:T(8,128)S(1)}, u32[]{:S(2)}, u32[]{:S(2)}) collective-permute-start(f32[400,128]{1,0:T(8,128)S(1)} %get-tuple-element.29), channel_id=1, source_target_pairs={{4,8},{12,16},{20,24},{8,4},{16,12},{24,20},{5,9},{13,17},{21,25},... | collective-permute-start | bytes 614408 | tf_op jit(solution)/shard_map/ppermute | solution.py:502
  49.9 3.4 %collective-permute-start.7 = (f32[400,128]{1,0:T(8,128)S(1)}, f32[400,128]{1,0:T(8,128)S(1)}, u32[]{:S(2)}, u32[]{:S(2)}) collective-permute-start(f32[400,128]{1,0:T(8,128)S(1)} %get-tuple-element.30), channel_id=1, source_target_pairs={{0,4},{8,12},{16,20},{24,28},{4,0},{12,8},{20,16},{28,24},{1,5},{9... | collective-permute-start | bytes 614408 | tf_op jit(solution)/shard_map/ppermute | solution.py:502
  53.9 8.6 %collective-permute-start.8 = (f32[64,128]{1,0:T(8,128)S(1)}, f32[64,128]{1,0:T(8,128)S(1)}, u32[]{:S(2)}, u32[]{:S(2)}) collective-permute-start(f32[64,128]{1,0:T(8,128)S(1)} %get-tuple-element.31), channel_id=1, source_target_pairs={{0,384},{4,388},{8,392},{12,396},{16,400},{20,404},{24,408},{28,41... | collective-permute-start | bytes 98312 | tf_op jit(solution)/shard_map/ppermute | solution.py:555
  55.2 17.2 %collective-permute-start.9 = (f32[64,128]{1,0:T(8,128)S(1)}, f32[64,128]{1,0:T(8,128)S(1)}, u32[]{:S(2)}, u32[]{:S(2)}) collective-permute-start(f32[64,128]{1,0:T(8,128)S(1)} %get-tuple-element.31), channel_id=1, source_target_pairs={{0,388},{4,384},{8,396},{12,392},{16,404},{20,400},{24,412},{28,40... | collective-permute-start | bytes 98312 | tf_op jit(solution)/shard_map/ppermute | solution.py:555
  62.5 10.6 %collective-permute-start.10 = (f32[64,128]{1,0:T(8,128)S(1)}, f32[64,128]{1,0:T(8,128)S(1)}, u32[]{:S(2)}, u32[]{:S(2)}) collective-permute-start(f32[64,128]{1,0:T(8,128)S(1)} %collective-permute-done.8.state), channel_id=1, source_target_pairs={{260,264},{268,272},{276,280},{264,260},{272,268},{280,276},{292,2... | collective-permute-start | bytes 98312 | tf_op jit(solution)/shard_map/ppermute | solution.py:507

commit v8 on v7

--- a/solution.py
+++ b/solution.py
@@ -74,7 +74,8 @@
     return out[0:count] + (out[count : 2 * count] + out[2 * count : 3 * count])
 
 
-def advance(src, dst, coef, push, shift, row, count, tiles, wanted, terms, side_mask, post=None):
+def advance(src, dst, coef, push, shift, row, count, tiles, wanted, terms, edge, post=None):
+    (row_before, row_after), (factor_before, factor_after), side_mask = edge
     _, lift, gain = terms
     lane = lanes((count, 128))
     low, high = lane == 0, lane == 127
@@ -101,24 +102,24 @@
         new = [new_u, new_v, new_p]
         if c == tiles - 1:
             new = [f * side_mask for f in new]
+        line = sublanes((count, 128))
+        if row <= row_before < row + count:
+            inside = jnp.where(line == row_before - row, factor_before, 1.0)
+            new = [f * inside for f in new]
+        if row <= row_after < row + count:
+            inside = jnp.where(line == row_after - row, factor_after, 1.0)
+            new = [f * inside for f in new]
         for f in range(3):
             if post is not None:
                 new[f] = post(f, c, here, new[f])
             dst[f, c, here, :] = new[f]
 
 
-def clear_rows(ref, tiles, before, after, outside):
-    for row, factor in ((before, outside[0]), (after, outside[1])):
-        for f in range(3):
-            for c in range(tiles):
-                ref[f, c, pl.ds(row, 1), :] = ref[f, c, pl.ds(row, 1), :] * factor
-
-
 def edges(at):
     lane = lanes((8, 128))
     outside = [jnp.where(at[1] > 0, 1.0, 0.0), jnp.where(at[1] < at[3] - 1, 1.0, 0.0)]
     side = jnp.where(lane < 64, jnp.where(at[2] < at[4] - 1, 1.0, 0.0), jnp.where(at[2] > 0, 1.0, 0.0))
-    return outside, side
+    return tuple(outside), side
 
 
 def coefficients(coef, c, rows, nu, carry):
@@ -153,7 +154,7 @@
     ])
 
 
-def side_kernel(at, own, got_a, got_b, send_a, send_b):
+def side_kernel(at, own, got_b, got_a, send_a, send_b):
     even_x = lax.rem(at[1], 2) == 0
     even_y = lax.rem(at[2], 2) == 0
     for r0, count in ((0, 8), (8, 64), (72, 8)):
@@ -233,6 +234,7 @@
     even_x = lax.rem(at[1], 2) == 0
     even_y = lax.rem(at[2], 2) == 0
     outside, side_mask = edges(at)
+    fine_edge, rough_edge = ((15, 80), outside, side_mask), ((9, 26), outside, side_mask)
     after_all = jnp.where(even_y, cols_a[...], cols_b[...])
     before_all = jnp.where(even_y, cols_b[...], cols_a[...])
     lane = lanes((80, 128))
@@ -280,10 +282,9 @@
         return own_push[d, c, r, :]
 
     for k in range(3):
-        advance(rough, rough_two, rough_coef, coarse_push, 0, 9 + 8 * k, 8, 2, (0, 1), COARSE, side_mask)
-    clear_rows(rough_two, 2, 9, 26, outside)
+        advance(rough, rough_two, rough_coef, coarse_push, 0, 9 + 8 * k, 8, 2, (0, 1), COARSE, rough_edge)
     for k in range(2):
-        advance(rough_two, rough, rough_coef, coarse_push, 0, 10 + 8 * k, 8, 2, (0,), COARSE, side_mask)
+        advance(rough_two, rough, rough_coef, coarse_push, 0, 10 + 8 * k, 8, 2, (0,), COARSE, rough_edge)
     for f in range(3):
         guess[16 * f : 16 * f + 16, :] = rough[f, 0, 10:26, :]
 
@@ -297,9 +298,7 @@
         (two, one, 16, 8, range(4)),
     ):
         for k in range(count):
-            advance(src, dst, coef, fine_push, 0, first + 8 * k, 8, 5, wanted, FINE, side_mask)
-        if count == 9:
-            clear_rows(dst, 5, 15, 80, outside)
+            advance(src, dst, coef, fine_push, 0, first + 8 * k, 8, 5, wanted, FINE, fine_edge)
     for f in range(3):
         for c in range(4):
             fine[f, :, 128 * c : 128 * c + 128] = one[f, c, 16:80, :] * (1.0 / FINE_SCALE[f])
@@ -395,7 +394,7 @@
 
 
 def chain(first_k, one, two, coef, push, extra, kept, at):
-    outside, side_mask = edges(at)
+    edge = ((8 + 15, 8 + 32),) + edges(at)
 
     for k in range(first_k, HALF):
         def pushed(d, c, r, k=k):
@@ -413,9 +412,7 @@
             src, dst = (one, two) if half == 0 else (two, one)
             post = keep_and_add if half else None
             for i in range(count):
-                advance(src, dst, coef, pushed, 8, first + 8 * i, 8, 2, (0, 1), COARSE, side_mask, post=post)
-            if halo:
-                clear_rows(dst, 2, 8 + 15, 8 + 32, outside)
+                advance(src, dst, coef, pushed, 8, first + 8 * i, 8, 2, (0, 1), COARSE, edge, post=post)
 
 
 def low_kernel(at, held, nu, cols_a, cols_b, rows_b, rows_a, push, state, moved, extra, coef, one, two, kept):
@@ -442,7 +439,7 @@
         assemble(at, held, nu, cols_a, cols_b, rows_a, rows_b, putter(extra, coef))
 
 
-def high_kernel(at, state, state_a, state_b, extra, coef, push, fine, guess, moved_low, out, one, two, kept, moved, spread):
+def high_kernel(at, state, state_a, state_b, extra, coef, push, fine, guess, moved_low, out, one, two, kept, moved, spread, result, sems):
     even_x = lax.rem(at[1], 2) == 0
 
     @pl.when(at[0] < HALF)
@@ -469,30 +466,42 @@
     change = jnp.concatenate(parts, axis=0)
     i, j = sublanes((128, COLS)), lanes((128, COLS))
     change = exact_dot(change, jnp.where(i == j // 4, 1.0, 0.0))
+    copies = []
     for f in range(3):
         for c in range(4):
             cut = slice(128 * c, 128 * c + 128)
             for k in range(4):
                 spread[f, c, pl.ds(k, CROWS, stride=4), :] = change[16 * f : 16 * f + 16, cut]
-            out[f, :, cut] = fine[f, :, cut] + spread[f, c]
-
-
-SMEM = pl.BlockSpec(memory_space=pltpu.SMEM)
+            result[f, :, cut] = fine[f, :, cut] + spread[f, c]
+        copies.append(pltpu.make_async_copy(result.at[f], out.at[f], sems.at[f]))
+        copies[f].start()
+    for copy in copies:
+        copy.wait()
+
+
+def place():
+    return (*[lax.axis_index(a) for a in ("cuts", "sx", "sy")], lax.axis_size("sx"), lax.axis_size("sy"))
+
+
 VMEM = pl.BlockSpec(memory_space=pltpu.VMEM)
 HBM = pl.BlockSpec(memory_space=pltpu.HBM)
 
 
-def call(kernel, args, outs, scratch=(), far=0, sems=0):
+def call(kernel, args, outs, scratch=(), far=0, sems=0, away=False):
     shapes = [jax.ShapeDtypeStruct(s, F32) for s in outs]
-    near = len(args) - 1 - far
+    near = len(args) - far
     memory = [s if not isinstance(s, tuple) else pltpu.VMEM(s, F32) for s in scratch]
     if sems:
         memory.append(pltpu.SemaphoreType.DMA((sems,)))
+
+    def placed(*refs):
+        kernel(place(), *refs)
+
     return pl.pallas_call(
-        kernel,
+        placed,
         out_shape=shapes,
-        in_specs=[SMEM] + [VMEM] * near + [HBM] * far,
-        out_specs=[VMEM] * len(shapes),
+        in_specs=[VMEM] * near + [HBM] * far,
+        out_specs=[HBM if away else VMEM] * len(shapes),
         scratch_shapes=memory,
         compiler_params=pltpu.CompilerParams(vmem_limit_bytes=48 * 1024 * 1024),
     )(*args)
@@ -502,17 +511,14 @@
     return lax.ppermute(x, axis, [(a, b) for a, b in pairs] + [(b, a) for a, b in pairs])
 
 
-def swap_high(x, count, pairs):
+def swap_half(x, count, pairs, cuts):
     both = [(a, b) for a, b in pairs] + [(b, a) for a, b in pairs]
-    return lax.ppermute(x, ("cuts", "sx"), [(n * count + a, n * count + b) for n in range(HALF, CUTS) for a, b in both])
+    return lax.ppermute(x, ("cuts", "sx"), [(n * count + a, n * count + b) for n in cuts for a, b in both])
 
 
 def on_device(starts, viscosity, turbine_x, turbine_y, yaw_index):
     count_x, count_y = lax.axis_size("sx"), lax.axis_size("sy")
-    at = jnp.stack([
-        lax.axis_index("cuts"), lax.axis_index("sx"), lax.axis_index("sy"),
-        jnp.int32(count_x), jnp.int32(count_y),
-    ]).astype(jnp.int32)
+    at = place()
     start = starts[0]
     x_a = [(i, i + 1) for i in range(0, count_x - 1, 2)]
     x_b = [(i, i + 1) for i in range(1, count_x - 1, 2)]
@@ -525,44 +531,46 @@
     rows_b = swap(edge_rows(start, viscosity, 56 * odd), "sx", x_b)
     rows_a = swap(edge_rows(start, viscosity, 56 * (1 - odd)), "sx", x_a)
     own = jnp.concatenate([start, viscosity[None]])
-    send_a, send_b = call(side_kernel, (at, own, rows_a, rows_b), [(80, 128)] * 2)
+    send_a, send_b = call(side_kernel, (own, rows_b, rows_a), [(80, 128)] * 2)
     cols_a = swap(send_a, "sy", y_a)
     cols_b = swap(send_b, "sy", y_b)
     push, own_push = call(
-        push_kernel, (at,) + turbines, [(2, 5, 96, 128), (2, 2, 40, 128)], turbine_scratch, far=3, sems=3)
+        push_kernel, turbines, [(2, 5, 96, 128), (2, 2, 40, 128)], turbine_scratch, far=3, sems=3)
     fine, guess, sent, coarse_nu = call(
         fine_kernel,
-        (at, own, rows_a, rows_b, cols_a, cols_b, push, own_push),
+        (own, rows_a, rows_b, cols_a, cols_b, push, own_push),
         [(3, ROWS, COLS), (48, 128), (HALF, 48, 128), (CROWS, 128)],
         [(3, 5, 96, 128), (3, 5, 96, 128), (4, 5, 96, 128), (3, 2, 40, 128), (3, 2, 40, 128), (4, 2, 40, 128)],
     )
     halves = [list(range(HALF)), list(range(HALF, CUTS))]
     held = lax.all_to_all(sent, "cuts", 0, 0, axis_index_groups=halves)
-    send_a, send_b = call(cols_kernel, (at, held, coarse_nu), [(STRIPS, 128)] * 2)
+    send_a, send_b = call(cols_kernel, (held, coarse_nu), [(STRIPS, 128)] * 2)
     cols_a = swap(send_a, "sy", y_a)
     cols_b = swap(send_b, "sy", y_b)
     (chain_push,) = call(
-        chain_push_kernel, (at,) + turbines, [(HALF, 2, 2, EXT, 128)], turbine_scratch, far=3, sems=3)
-    send_a, send_b = call(rows_kernel, (at, held, coarse_nu, cols_a, cols_b), [(MESSAGE, 128)] * 2)
+        chain_push_kernel, turbines, [(HALF, 2, 2, EXT, 128)], turbine_scratch, far=3, sems=3)
+    send_a, send_b = call(rows_kernel, (held, coarse_nu, cols_a, cols_b), [(MESSAGE, 128)] * 2)
+    low, high = range(HALF), range(HALF, CUTS)
     rows_a = swap(send_a, "sx", x_a)
     rows_b = swap(send_b, "sx", x_b)
-    blocks = (at, held, coarse_nu, cols_a, cols_b, rows_b, rows_a)
+    blocks = (held, coarse_nu, cols_a, cols_b, rows_b, rows_a)
     field, planes, terms = (3, 2, 64, 128), (3 * HALF, 2, EXT, 128), (4, 2, EXT, 128)
     state, moved = call(
         low_kernel, blocks + (chain_push,), [(64, 128), (48, 128)], [planes, terms, field, field, (HALF, 3, 64, 128)])
-    goes = [(m, m + 4 if m >= 4 else m + 12) for m in range(HALF)]
+    goes = [(m, m + 4 if m >= 4 else m + 12) for m in low]
     state_b, state_a = [
         lax.ppermute(state, ("cuts", "sx"), [(m * count_x + i, n * count_x + (i ^ flip)) for m, n in goes for i in range(count_x)])
         for flip in (0, 1)
     ]
+    extra, coef = call(planes_kernel, (held, coarse_nu, cols_a, cols_b, rows_b, rows_a), [planes, terms])
     state = state_b
-    state_b = swap_high(state, count_x, x_b)
-    extra, coef = call(planes_kernel, blocks, [planes, terms])
+    state_b = swap_half(state, count_x, x_b, high)
     (out,) = call(
         high_kernel,
-        (at, state, state_a, state_b, extra, coef, chain_push, fine, guess, moved),
+        (state, state_a, state_b, extra, coef, chain_push, fine, guess, moved),
         [(3, ROWS, COLS)],
-        [field, field, (HALF, 3, 64, 128), (48, 128), (3, 4, ROWS, 128)],
+        [field, field, (HALF, 3, 64, 128), (48, 128), (3, 4, ROWS, 128), (3, ROWS, COLS)],
+        sems=3, away=True,
     )
     return out[None]
 

time: 77.6 us -> 74.1 us (0.955)
  Pallas kernels: 12.4 us -> 7.18 us
  waiting for transfers between devices: 11.8 us -> 13.3 us
    pallas_call x9, Pallas kernels: 12.4 us -> 7.18 us  [call(): pl.pallas_call(placed, out_shape=shapes, in_specs=[VMEM] * near + [HBM] *...]
    ppermute x8, waiting for transfers between devices: 5 us -> 6.07 us  [swap(): lax.ppermute(x, axis, [(a, b) for a, b in pairs] + [(b, a) for a, b in pa...]
  transfers between devices with their start and end apart: 11 -> 11, of which waited for: 6 -> 7; matrix products, arithmetic and copies ran while one was open for 2% -> 2% of each run, Pallas kernels for 4% -> 2%
where the time goes in v8:
time: 74.1 us; the launch traced here: 73.6 us
  starting transfers between devices  36 us (49%)
  blocking collectives  14.1 us (19%)
  waiting for transfers between devices  13.3 us (18%)
  Pallas kernels  7.18 us (10%)
  local copies, waits for them, and re-layouts  1.59 us (2%)
  other arithmetic  1.12 us (2%)
    ppermute x8, starting transfers between devices, swap(): lax.ppermute(x, axis, [(a, b) for a, b in pairs] + [(b, a) for a, b in pa...  24.2 us
    all_to_all x1, blocking collectives, on_device(): held = lax.all_to_all(sent, 'cuts', 0, 0, axis_index_groups=halves)  14.1 us
    ppermute x1, starting transfers between devices, swap_half(): lax.ppermute(x, ('cuts', 'sx'), [(n * count + a, n * count + b) for n in...  9.22 us
    pallas_call x9, Pallas kernels, call(): pl.pallas_call(placed, out_shape=shapes, in_specs=[VMEM] * near + [HBM] *...  7.18 us
    ppermute x8, waiting for transfers between devices, swap(): lax.ppermute(x, axis, [(a, b) for a, b in pairs] + [(b, a) for a, b in pa...  6.07 us
    ppermute x2, waiting for transfers between devices, on_device(): lax.ppermute(state, ('cuts', 'sx'), [(m * count_x + i, n * count_x + (i ^...  5.97 us
    ppermute x2, starting transfers between devices, on_device(): lax.ppermute(state, ('cuts', 'sx'), [(m * count_x + i, n * count_x + (i ^...  2.57 us
  transfers between devices with their start and end apart: 11, of which 7 were waited for; matrix products, arithmetic and copies ran while one was open for 2% of the time, Pallas kernels for 2%

profile of v8, /device:TPU:401, one launch (start us, length us, event | category | flops | bytes accessed | tf_op | source)
XLA Modules:
  0.0 73.6 jit_solution(11879407640888005533)
XLA Ops:
  0.0 0.8 %dynamic-slice_bitcast_fusion = (f32[3,8,512]{2,1,0:T(8,128)S(1)}, f32[3,8,512]{2,1,0:T(8,128)S(1)}) fusion(f32[1,3,64,512]{3,2,1,0:T(8,128)} %param.5, s32[]{:T(128)S(6)} %select_n.17, s32[]{:T(128)S(6)} %select_n.16), kind=kLoop, calls=%fused_computation.3 | loop fusion | bytes 196616 | tf_op jit(solution)/shard_map/dynamic_slice | solution.py:152
  0.9 0.7 %dynamic-slice_bitcast_fusion.2 = (f32[1,8,512]{2,1,0:T(8,128)S(1)}, f32[1,8,512]{2,1,0:T(8,128)S(1)}) fusion(f32[64,512]{1,0:T(8,128)} %param.6, s32[]{:T(128)S(6)} %select_n.17, s32[]{:T(128)S(6)} %select_n.16), kind=kLoop, calls=%fused_computation.5 | loop fusion | bytes 65544 | tf_op jit(solution)/shard_map/broadcast_in_dim | solution.py:153
  1.6 3.7 %collective-permute-start.1 = (f32[4,8,512]{2,1,0:T(8,128)S(1)}, f32[4,8,512]{2,1,0:T(8,128)S(1)}, u32[]{:S(2)}, u32[]{:S(2)}) collective-permute-start(f32[4,8,512]{2,1,0:T(8,128)S(1)} %pad_maximum_fusion.2), channel_id=1, source_target_pairs={{4,8},{12,16},{20,24},{8,4},{16,12},{24,20},{5,9},{13,17},{21,25},... | collective-permute-start | bytes 196616 | tf_op jit(solution)/shard_map/ppermute | solution.py:511
  5.3 1.9 %collective-permute-start = (f32[4,8,512]{2,1,0:T(8,128)S(1)}, f32[4,8,512]{2,1,0:T(8,128)S(1)}, u32[]{:S(2)}, u32[]{:S(2)}) collective-permute-start(f32[4,8,512]{2,1,0:T(8,128)S(1)} %pad_maximum_fusion.1), channel_id=1, source_target_pairs={{0,4},{8,12},{16,20},{24,28},{4,0},{12,8},{20,16},{28,24},{1,5},{9... | collective-permute-start | bytes 196616 | tf_op jit(solution)/shard_map/ppermute | solution.py:511
  7.3 1.1 %pad_maximum_fusion.refs_0_ = f32[4,64,512]{2,1,0:T(8,128)S(1)} fusion(f32[1,64,512]{2,1,0:T(8,128)} %bitcast.18, f32[3,64,512]{2,1,0:T(8,128)} %bitcast.17), kind=kLoop, calls=%fused_computation | loop fusion | flops 131072 | bytes 1048576 | tf_op jit(solution)/shard_map/concatenate | solution.py:533
  8.4 0.0 collective-permute-done.1.refs_1_.refs_2_
  8.4 0.1 collective-permute-done.refs_2_.refs_1_
  8.5 0.1 shard_map.55
  8.6 2.9 %collective-permute-start.2 = (f32[80,128]{1,0:T(8,128)S(1)}, f32[80,128]{1,0:T(8,128)S(1)}, u32[]{:S(2)}, u32[]{:S(2)}) collective-permute-start(f32[80,128]{1,0:T(8,128)S(1)} %get-tuple-element.21), channel_id=1, source_target_pairs={{0,1},{2,3},{1,0},{3,2},{4,5},{6,7},{5,4},{7,6},{8,9},{10,11},{9,8... | collective-permute-start | bytes 122888 | tf_op jit(solution)/shard_map/ppermute | solution.py:511
  11.5 1.9 %collective-permute-start.3 = (f32[80,128]{1,0:T(8,128)S(1)}, f32[80,128]{1,0:T(8,128)S(1)}, u32[]{:S(2)}, u32[]{:S(2)}) collective-permute-start(f32[80,128]{1,0:T(8,128)S(1)} %get-tuple-element.22), channel_id=1, source_target_pairs={{1,2},{2,1},{5,6},{6,5},{9,10},{10,9},{13,14},{14,13},{17,18},{18,... | collective-permute-start | bytes 122888 | tf_op jit(solution)/shard_map/ppermute | solution.py:511
  13.5 0.5 shard_map.56
  14.0 0.0 collective-permute-done.2.refs_3_
  14.1 2.2 %collective-permute-done.3.refs_4_ = f32[80,128]{1,0:T(8,128)S(1)} collective-permute-done((f32[80,128]{1,0:T(8,128)S(1)}, f32[80,128]{1,0:T(8,128)S(1)}, u32[]{:S(2)}, u32[]{:S(2)}) %collective-permute-start.3) | collective-permute-done | bytes 40992 | tf_op jit(solution)/shard_map/ppermute | solution.py:511
  16.3 2.3 %shard_map.57 = (f32[3,64,512]{2,1,0:T(8,128)S(1)}, f32[48,128]{1,0:T(8,128)S(1)}, f32[8,48,128]{2,1,0:T(8,128)S(1)}, f32[16,128]{1,0:T(8,128)S(1)}) custom-call(f32[4,64,512]{2,1,0:T(8,128)S(1)} %pad_maximum_fusion.refs_0_, f32[4,8,512]{2,1,0:T(8,128)S(1)} %collective-permute-done.refs_2_.refs_1_, f32[4,8,512]{2,1,0:T(8,128)S(1)} %collective-permute-done.1.refs_1_.refs_2_, ...), custom_call_target="tpu_custom_call" | custom-call | tf_op jit(solution)/shard_map/pallas_call | solution.py:500
  18.6 14.1 %all_to_all.5.refs_0_ = f32[8,48,128]{2,1,0:T(8,128)S(1)} all-to-all(f32[8,48,128]{2,1,0:T(8,128)S(1)} %get-tuple-element.25), channel_id=1, replica_groups={{0,32,64,96,128,160,192,224},{256,288,320,352,384,416,448,480},{1,33,65..., dimensions={0} | all-to-all | bytes 393216 | tf_op jit(solution)/shard_map/all_to_all | solution.py:546
  32.7 0.1 shard_map.58
  32.9 1.9 %collective-permute-start.4 = (f32[112,128]{1,0:T(8,128)S(1)}, f32[112,128]{1,0:T(8,128)S(1)}, u32[]{:S(2)}, u32[]{:S(2)}) collective-permute-start(f32[112,128]{1,0:T(8,128)S(1)} %get-tuple-element.27), channel_id=1, source_target_pairs={{0,1},{2,3},{1,0},{3,2},{4,5},{6,7},{5,4},{7,6},{8,9},{10,11},{9,8... | collective-permute-start | bytes 172040 | tf_op jit(solution)/shard_map/ppermute | solution.py:511
  34.8 2.0 %collective-permute-start.5 = (f32[112,128]{1,0:T(8,128)S(1)}, f32[112,128]{1,0:T(8,128)S(1)}, u32[]{:S(2)}, u32[]{:S(2)}) collective-permute-start(f32[112,128]{1,0:T(8,128)S(1)} %get-tuple-element.28), channel_id=1, source_target_pairs={{1,2},{2,1},{5,6},{6,5},{9,10},{10,9},{13,14},{14,13},{17,18},{18,... | collective-permute-start | bytes 172040 | tf_op jit(solution)/shard_map/ppermute | solution.py:511
  36.9 0.9 %collective-permute-done.4.refs_2_ = f32[112,128]{1,0:T(8,128)S(1)} collective-permute-done((f32[112,128]{1,0:T(8,128)S(1)}, f32[112,128]{1,0:T(8,128)S(1)}, u32[]{:S(2)}, u32[]{:S(2)}) %collective-permute-start.4) | collective-permute-done | bytes 57376 | tf_op jit(solution)/shard_map/ppermute | solution.py:511
  37.8 1.9 %collective-permute-done.5.refs_3_ = f32[112,128]{1,0:T(8,128)S(1)} collective-permute-done((f32[112,128]{1,0:T(8,128)S(1)}, f32[112,128]{1,0:T(8,128)S(1)}, u32[]{:S(2)}, u32[]{:S(2)}) %collective-permute-start.5) | collective-permute-done | bytes 57376 | tf_op jit(solution)/shard_map/ppermute | solution.py:511
  39.8 7.9 %collective-permute-start.6 = (f32[400,128]{1,0:T(8,128)S(1)}, f32[400,128]{1,0:T(8,128)S(1)}, u32[]{:S(2)}, u32[]{:S(2)}) collective-permute-start(f32[400,128]{1,0:T(8,128)S(1)} %get-tuple-element.29), channel_id=1, source_target_pairs={{4,8},{12,16},{20,24},{8,4},{16,12},{24,20},{5,9},{13,17},{21,25},... | collective-permute-start | bytes 614408 | tf_op jit(solution)/shard_map/ppermute | solution.py:511
  47.6 1.9 %collective-permute-start.7 = (f32[400,128]{1,0:T(8,128)S(1)}, f32[400,128]{1,0:T(8,128)S(1)}, u32[]{:S(2)}, u32[]{:S(2)}) collective-permute-start(f32[400,128]{1,0:T(8,128)S(1)} %get-tuple-element.30), channel_id=1, source_target_pairs={{0,4},{8,12},{16,20},{24,28},{4,0},{12,8},{20,16},{28,24},{1,5},{9... | collective-permute-start | bytes 614408 | tf_op jit(solution)/shard_map/ppermute | solution.py:511
  49.6 0.6 shard_map.60.refs_6_.refs_5_
  50.2 0.9 %collective-permute-done.6.refs_4_ = f32[400,128]{1,0:T(8,128)S(1)} collective-permute-done((f32[400,128]{1,0:T(8,128)S(1)}, f32[400,128]{1,0:T(8,128)S(1)}, u32[]{:S(2)}, u32[]{:S(2)}) %collective-permute-start.6) | collective-permute-done | bytes 204832 | tf_op jit(solution)/shard_map/ppermute | solution.py:511
  51.1 0.0 collective-permute-done.7.refs_5_
  51.1 1.3 %collective-permute-start.8 = (f32[64,128]{1,0:T(8,128)S(1)}, f32[64,128]{1,0:T(8,128)S(1)}, u32[]{:S(2)}, u32[]{:S(2)}) collective-permute-start(f32[64,128]{1,0:T(8,128)S(1)} %get-tuple-element.31), channel_id=1, source_target_pairs={{0,384},{4,388},{8,392},{12,396},{16,400},{20,404},{24,408},{28,41... | collective-permute-start | bytes 98312 | tf_op jit(solution)/shard_map/ppermute | solution.py:562
  52.4 1.3 %collective-permute-start.9 = (f32[64,128]{1,0:T(8,128)S(1)}, f32[64,128]{1,0:T(8,128)S(1)}, u32[]{:S(2)}, u32[]{:S(2)}) collective-permute-start(f32[64,128]{1,0:T(8,128)S(1)} %get-tuple-element.31), channel_id=1, source_target_pairs={{0,388},{4,384},{8,396},{12,392},{16,404},{20,400},{24,412},{28,40... | collective-permute-start | bytes 98312 | tf_op jit(solution)/shard_map/ppermute | solution.py:562
  53.7 6.0 %collective-permute-done.8.refs_0_ = f32[64,128]{1,0:T(8,128)S(1)} collective-permute-done((f32[64,128]{1,0:T(8,128)S(1)}, f32[64,128]{1,0:T(8,128)S(1)}, u32[]{:S(2)}, u32[]{:S(2)}) %collective-permute-start.8) | collective-permute-done | bytes 32800 | tf_op jit(solution)/shard_map/ppermute | solution.py:562
  59.6 9.2 %collective-permute-start.10 = (f32[64,128]{1,0:T(8,128)S(1)}, f32[64,128]{1,0:T(8,128)S(1)}, u32[]{:S(2)}, u32[]{:S(2)}) collective-permute-start(f32[64,128]{1,0:T(8,128)S(1)} %collective-permute-done.8.refs_0_), channel_id=1, source_target_pairs={{260,264},{268,272},{276,280},{264,260},{272,268},{280,276},{292,2... | collective-permute-start | bytes 98312 | tf_op jit(solution)/shard_map/ppermute | solution.py:516
  68.9 0.3 shard_map.62
  69.1 1.3 %collective-permute-done.10.refs_2_ = f32[64,128]{1,0:T(8,128)S(1)} collective-permute-done((f32[64,128]{1,0:T(8,128)S(1)}, f32[64,128]{1,0:T(8,128)S(1)}, u32[]{:S(2)}, u32[]{:S(2)}) %collective-permute-start.10) | collective-permute-done | bytes 32800 | tf_op jit(solution)/shard_map/ppermute | solution.py:516
  70.4 3.1 %shard_map.63 = f32[3,64,512]{2,1,0:T(8,128)} custom-call(f32[64,128]{1,0:T(8,128)S(1)} %collective-permute-done.8.refs_0_, f32[64,128]{1,0:T(8,128)S(1)} %collective-permute-done.9.refs_1_, f32[64,128]{1,0:T(8,128)S(1)} %collective-permute-done.10.refs_2_, f32[24,2,48,128]{3,2,1,0:T(8,128)S(1)} %get-tuple-element.32.refs_3_, ...), custom_call_target="tpu_custom_call" | custom-call | tf_op jit(solution)/shard_map/pallas_call | solution.py:500
  (11 shorter events, 0.1 us)
Async XLA Ops:
  0.0 13.5 %copy-start.1 = (s32[64]{0:T(128)S(1)}, s32[64]{0:T(128)}, u32[]{:S(2)}) copy-start(s32[64]{0:T(128)} %param.7) | copy-start | bytes 772
  0.0 13.5 %copy-start.2 = (s32[64]{0:T(128)S(1)}, s32[64]{0:T(128)}, u32[]{:S(2)}) copy-start(s32[64]{0:T(128)} %param.8) | copy-start | bytes 772
  0.0 13.5 %copy-start = (s32[16,64]{1,0:T(8,128)S(1)}, s32[16,64]{1,0:T(8,128)}, u32[]{:S(2)}) copy-start(s32[16,64]{1,0:T(8,128)} %refs_2_.3) | copy-start | bytes 12292
  1.6 6.7 %collective-permute-start.1 = (f32[4,8,512]{2,1,0:T(8,128)S(1)}, f32[4,8,512]{2,1,0:T(8,128)S(1)}, u32[]{:S(2)}, u32[]{:S(2)}) collective-permute-start(f32[4,8,512]{2,1,0:T(8,128)S(1)} %pad_maximum_fusion.2), channel_id=1, source_target_pairs={{4,8},{12,16},{20,24},{8,4},{16,12},{24,20},{5,9},{13,17},{21,25},... | collective-permute-start | bytes 196616 | tf_op jit(solution)/shard_map/ppermute | solution.py:511
  5.3 3.1 %collective-permute-start = (f32[4,8,512]{2,1,0:T(8,128)S(1)}, f32[4,8,512]{2,1,0:T(8,128)S(1)}, u32[]{:S(2)}, u32[]{:S(2)}) collective-permute-start(f32[4,8,512]{2,1,0:T(8,128)S(1)} %pad_maximum_fusion.1), channel_id=1, source_target_pairs={{0,4},{8,12},{16,20},{24,28},{4,0},{12,8},{20,16},{28,24},{1,5},{9... | collective-permute-start | bytes 196616 | tf_op jit(solution)/shard_map/ppermute | solution.py:511
  8.6 5.4 %collective-permute-start.2 = (f32[80,128]{1,0:T(8,128)S(1)}, f32[80,128]{1,0:T(8,128)S(1)}, u32[]{:S(2)}, u32[]{:S(2)}) collective-permute-start(f32[80,128]{1,0:T(8,128)S(1)} %get-tuple-element.21), channel_id=1, source_target_pairs={{0,1},{2,3},{1,0},{3,2},{4,5},{6,7},{5,4},{7,6},{8,9},{10,11},{9,8... | collective-permute-start | bytes 122888 | tf_op jit(solution)/shard_map/ppermute | solution.py:511
  11.5 4.7 %collective-permute-start.3 = (f32[80,128]{1,0:T(8,128)S(1)}, f32[80,128]{1,0:T(8,128)S(1)}, u32[]{:S(2)}, u32[]{:S(2)}) collective-permute-start(f32[80,128]{1,0:T(8,128)S(1)} %get-tuple-element.22), channel_id=1, source_target_pairs={{1,2},{2,1},{5,6},{6,5},{9,10},{10,9},{13,14},{14,13},{17,18},{18,... | collective-permute-start | bytes 122888 | tf_op jit(solution)/shard_map/ppermute | solution.py:511
  32.9 4.9 %collective-permute-start.4 = (f32[112,128]{1,0:T(8,128)S(1)}, f32[112,128]{1,0:T(8,128)S(1)}, u32[]{:S(2)}, u32[]{:S(2)}) collective-permute-start(f32[112,128]{1,0:T(8,128)S(1)} %get-tuple-element.27), channel_id=1, source_target_pairs={{0,1},{2,3},{1,0},{3,2},{4,5},{6,7},{5,4},{7,6},{8,9},{10,11},{9,8... | collective-permute-start | bytes 172040 | tf_op jit(solution)/shard_map/ppermute | solution.py:511
  34.8 4.9 %collective-permute-start.5 = (f32[112,128]{1,0:T(8,128)S(1)}, f32[112,128]{1,0:T(8,128)S(1)}, u32[]{:S(2)}, u32[]{:S(2)}) collective-permute-start(f32[112,128]{1,0:T(8,128)S(1)} %get-tuple-element.28), channel_id=1, source_target_pairs={{1,2},{2,1},{5,6},{6,5},{9,10},{10,9},{13,14},{14,13},{17,18},{18,... | collective-permute-start | bytes 172040 | tf_op jit(solution)/shard_map/ppermute | solution.py:511
  39.8 11.3 %collective-permute-start.6 = (f32[400,128]{1,0:T(8,128)S(1)}, f32[400,128]{1,0:T(8,128)S(1)}, u32[]{:S(2)}, u32[]{:S(2)}) collective-permute-start(f32[400,128]{1,0:T(8,128)S(1)} %get-tuple-element.29), channel_id=1, source_target_pairs={{4,8},{12,16},{20,24},{8,4},{16,12},{24,20},{5,9},{13,17},{21,25},... | collective-permute-start | bytes 614408 | tf_op jit(solution)/shard_map/ppermute | solution.py:511
  47.6 3.4 %collective-permute-start.7 = (f32[400,128]{1,0:T(8,128)S(1)}, f32[400,128]{1,0:T(8,128)S(1)}, u32[]{:S(2)}, u32[]{:S(2)}) collective-permute-start(f32[400,128]{1,0:T(8,128)S(1)} %get-tuple-element.30), channel_id=1, source_target_pairs={{0,4},{8,12},{16,20},{24,28},{4,0},{12,8},{20,16},{28,24},{1,5},{9... | collective-permute-start | bytes 614408 | tf_op jit(solution)/shard_map/ppermute | solution.py:511
  51.1 8.6 %collective-permute-start.8 = (f32[64,128]{1,0:T(8,128)S(1)}, f32[64,128]{1,0:T(8,128)S(1)}, u32[]{:S(2)}, u32[]{:S(2)}) collective-permute-start(f32[64,128]{1,0:T(8,128)S(1)} %get-tuple-element.31), channel_id=1, source_target_pairs={{0,384},{4,388},{8,392},{12,396},{16,400},{20,404},{24,408},{28,41... | collective-permute-start | bytes 98312 | tf_op jit(solution)/shard_map/ppermute | solution.py:562
  52.4 16.8 %collective-permute-start.9 = (f32[64,128]{1,0:T(8,128)S(1)}, f32[64,128]{1,0:T(8,128)S(1)}, u32[]{:S(2)}, u32[]{:S(2)}) collective-permute-start(f32[64,128]{1,0:T(8,128)S(1)} %get-tuple-element.31), channel_id=1, source_target_pairs={{0,388},{4,384},{8,396},{12,392},{16,404},{20,400},{24,412},{28,40... | collective-permute-start | bytes 98312 | tf_op jit(solution)/shard_map/ppermute | solution.py:562
  59.6 10.8 %collective-permute-start.10 = (f32[64,128]{1,0:T(8,128)S(1)}, f32[64,128]{1,0:T(8,128)S(1)}, u32[]{:S(2)}, u32[]{:S(2)}) collective-permute-start(f32[64,128]{1,0:T(8,128)S(1)} %collective-permute-done.8.refs_0_), channel_id=1, source_target_pairs={{260,264},{268,272},{276,280},{264,260},{272,268},{280,276},{292,2... | collective-permute-start | bytes 98312 | tf_op jit(solution)/shard_map/ppermute | solution.py:516

commit v9 on v8

--- a/solution.py
+++ b/solution.py
@@ -147,11 +147,12 @@
         copy.wait()
 
 
-def edge_rows(start, visc, first):
-    return jnp.concatenate([
-        lax.dynamic_slice(start, (0, first, 0), (3, 8, COLS)),
-        lax.dynamic_slice(visc, (first, 0), (8, COLS))[None],
-    ])
+def edge_kernel(at, own, send_b, send_a):
+    even = lax.rem(at[1], 2) == 0
+    for f in range(4):
+        first, last = own[f, 0:8, :], own[f, ROWS - 8 : ROWS, :]
+        send_a[f] = jnp.where(even, last, first)
+        send_b[f] = jnp.where(even, first, last)
 
 
 def side_kernel(at, own, got_b, got_a, send_a, send_b):
@@ -229,7 +230,7 @@
             push[k, 1, c] = value[EXT : 2 * EXT]
 
 
-def fine_kernel(at, own, rows_a, rows_b, cols_a, cols_b, push, own_push, fine, guess, sent, coarse_nu,
+def fine_kernel(at, own, rows_b, rows_a, cols_a, cols_b, push, own_push, fine, guess, sent, coarse_nu,
                 one, two, coef, rough, rough_two, rough_coef):
     even_x = lax.rem(at[1], 2) == 0
     even_y = lax.rem(at[2], 2) == 0
@@ -527,10 +528,10 @@
     turbines = (turbine_x[None, :], turbine_y[None, :], yaw_index)
     turbine_scratch = [pltpu.VMEM((1, 64), jnp.int32), pltpu.VMEM((1, 64), jnp.int32), pltpu.VMEM((CUTS, 64), jnp.int32)]
 
-    odd = at[1] % 2
-    rows_b = swap(edge_rows(start, viscosity, 56 * odd), "sx", x_b)
-    rows_a = swap(edge_rows(start, viscosity, 56 * (1 - odd)), "sx", x_a)
     own = jnp.concatenate([start, viscosity[None]])
+    send_b, send_a = call(edge_kernel, (own,), [(4, 8, COLS)] * 2)
+    rows_b = swap(send_b, "sx", x_b)
+    rows_a = swap(send_a, "sx", x_a)
     send_a, send_b = call(side_kernel, (own, rows_b, rows_a), [(80, 128)] * 2)
     cols_a = swap(send_a, "sy", y_a)
     cols_b = swap(send_b, "sy", y_b)
@@ -538,7 +539,7 @@
         push_kernel, turbines, [(2, 5, 96, 128), (2, 2, 40, 128)], turbine_scratch, far=3, sems=3)
     fine, guess, sent, coarse_nu = call(
         fine_kernel,
-        (own, rows_a, rows_b, cols_a, cols_b, push, own_push),
+        (own, rows_b, rows_a, cols_a, cols_b, push, own_push),
         [(3, ROWS, COLS), (48, 128), (HALF, 48, 128), (CROWS, 128)],
         [(3, 5, 96, 128), (3, 5, 96, 128), (4, 5, 96, 128), (3, 2, 40, 128), (3, 2, 40, 128), (4, 2, 40, 128)],
     )

time: 74.1 us -> 73.5 us (level)
  local copies, waits for them, and re-layouts: 1.59 us -> 0.01 us
  starting transfers between devices: 36 us -> 37.2 us
    ppermute x8, starting transfers between devices: 24.2 us -> 25.4 us  [swap(): lax.ppermute(x, axis, [(a, b) for a, b in pairs] + [(b, a) for a, b in pa...]
    dynamic_slice x1 -> x0, local copies, waits for them, and re-layouts: 0.85 us -> none  [edge_rows(): lax.dynamic_slice(start, (0, first, 0), (3, 8, COLS))]
    pallas_call x9 -> x10, Pallas kernels: 7.18 us -> 7.21 us  [call(): pl.pallas_call(placed, out_shape=shapes, in_specs=[VMEM] * near + [HBM] *...]
  transfers between devices with their start and end apart: 11 -> 11, of which waited for: 7 -> 6; matrix products, arithmetic and copies ran while one was open for 2% -> 0% of each run, Pallas kernels for 2% -> 2%
where the time goes in v9:
time: 73.5 us; the launch traced here: 73.1 us
  starting transfers between devices  37.2 us (51%)
  blocking collectives  14.2 us (19%)
  waiting for transfers between devices  13.1 us (18%)
  Pallas kernels  7.21 us (10%)
  other arithmetic  1.13 us (2%)
    ppermute x8, starting transfers between devices, swap(): lax.ppermute(x, axis, [(a, b) for a, b in pairs] + [(b, a) for a, b in pa...  25.4 us
    all_to_all x1, blocking collectives, on_device(): held = lax.all_to_all(sent, 'cuts', 0, 0, axis_index_groups=halves)  14.2 us
    ppermute x1, starting transfers between devices, swap_half(): lax.ppermute(x, ('cuts', 'sx'), [(n * count + a, n * count + b) for n in...  9.22 us
    pallas_call x10, Pallas kernels, call(): pl.pallas_call(placed, out_shape=shapes, in_specs=[VMEM] * near + [HBM] *...  7.21 us
    ppermute x2, waiting for transfers between devices, on_device(): lax.ppermute(state, ('cuts', 'sx'), [(m * count_x + i, n * count_x + (i ^...  5.97 us
    ppermute x8, waiting for transfers between devices, swap(): lax.ppermute(x, axis, [(a, b) for a, b in pairs] + [(b, a) for a, b in pa...  5.85 us
    ppermute x2, starting transfers between devices, on_device(): lax.ppermute(state, ('cuts', 'sx'), [(m * count_x + i, n * count_x + (i ^...  2.57 us
  transfers between devices with their start and end apart: 11, of which 6 were waited for; matrix products, arithmetic and copies ran while one was open for 0% of the time, Pallas kernels for 2%

profile of v9, /device:TPU:401, one launch (start us, length us, event | category | flops | bytes accessed | tf_op | source)
XLA Modules:
  0.0 73.1 jit_solution(9723198602240147829)
XLA Ops:
  0.0 1.1 %pad_maximum_fusion.refs_0_ = f32[4,64,512]{2,1,0:T(8,128)S(1)} fusion(f32[1,64,512]{2,1,0:T(8,128)} %bitcast.10, f32[3,64,512]{2,1,0:T(8,128)} %bitcast.9), kind=kLoop, calls=%fused_computation | loop fusion | flops 131072 | bytes 1048576 | tf_op jit(solution)/shard_map/concatenate | solution.py:531
  1.2 3.7 %collective-permute-start = (f32[4,8,512]{2,1,0:T(8,128)S(1)}, f32[4,8,512]{2,1,0:T(8,128)S(1)}, u32[]{:S(2)}, u32[]{:S(2)}) collective-permute-start(f32[4,8,512]{2,1,0:T(8,128)S(1)} %get-tuple-element.23), channel_id=1, source_target_pairs={{4,8},{12,16},{20,24},{8,4},{16,12},{24,20},{5,9},{13,17},{21,25},... | collective-permute-start | bytes 196616 | tf_op jit(solution)/shard_map/ppermute | solution.py:512
  4.9 1.9 %collective-permute-start.1 = (f32[4,8,512]{2,1,0:T(8,128)S(1)}, f32[4,8,512]{2,1,0:T(8,128)S(1)}, u32[]{:S(2)}, u32[]{:S(2)}) collective-permute-start(f32[4,8,512]{2,1,0:T(8,128)S(1)} %get-tuple-element.24), channel_id=1, source_target_pairs={{0,4},{8,12},{16,20},{24,28},{4,0},{12,8},{20,16},{28,24},{1,5},{9... | collective-permute-start | bytes 196616 | tf_op jit(solution)/shard_map/ppermute | solution.py:512
  6.8 0.0 collective-permute-done.refs_1_
  6.8 1.2 %collective-permute-done.1.refs_2_ = f32[4,8,512]{2,1,0:T(8,128)S(1)} collective-permute-done((f32[4,8,512]{2,1,0:T(8,128)S(1)}, f32[4,8,512]{2,1,0:T(8,128)S(1)}, u32[]{:S(2)}, u32[]{:S(2)}) %collective-permute-start.1) | collective-permute-done | bytes 65568 | tf_op jit(solution)/shard_map/ppermute | solution.py:512
  8.0 0.1 shard_map.56
  8.2 2.9 %collective-permute-start.2 = (f32[80,128]{1,0:T(8,128)S(1)}, f32[80,128]{1,0:T(8,128)S(1)}, u32[]{:S(2)}, u32[]{:S(2)}) collective-permute-start(f32[80,128]{1,0:T(8,128)S(1)} %get-tuple-element.25), channel_id=1, source_target_pairs={{0,1},{2,3},{1,0},{3,2},{4,5},{6,7},{5,4},{7,6},{8,9},{10,11},{9,8... | collective-permute-start | bytes 122888 | tf_op jit(solution)/shard_map/ppermute | solution.py:512
  11.1 1.9 %collective-permute-start.3 = (f32[80,128]{1,0:T(8,128)S(1)}, f32[80,128]{1,0:T(8,128)S(1)}, u32[]{:S(2)}, u32[]{:S(2)}) collective-permute-start(f32[80,128]{1,0:T(8,128)S(1)} %get-tuple-element.26), channel_id=1, source_target_pairs={{1,2},{2,1},{5,6},{6,5},{9,10},{10,9},{13,14},{14,13},{17,18},{18,... | collective-permute-start | bytes 122888 | tf_op jit(solution)/shard_map/ppermute | solution.py:512
  13.0 0.0 copy-done.1
  13.0 0.5 shard_map.57
  13.6 0.0 collective-permute-done.2.refs_3_
  13.6 2.2 %collective-permute-done.3.refs_4_ = f32[80,128]{1,0:T(8,128)S(1)} collective-permute-done((f32[80,128]{1,0:T(8,128)S(1)}, f32[80,128]{1,0:T(8,128)S(1)}, u32[]{:S(2)}, u32[]{:S(2)}) %collective-permute-start.3) | collective-permute-done | bytes 40992 | tf_op jit(solution)/shard_map/ppermute | solution.py:512
  15.8 2.3 %shard_map.58 = (f32[3,64,512]{2,1,0:T(8,128)S(1)}, f32[48,128]{1,0:T(8,128)S(1)}, f32[8,48,128]{2,1,0:T(8,128)S(1)}, f32[16,128]{1,0:T(8,128)S(1)}) custom-call(f32[4,64,512]{2,1,0:T(8,128)S(1)} %pad_maximum_fusion.refs_0_, f32[4,8,512]{2,1,0:T(8,128)S(1)} %collective-permute-done.refs_1_, f32[4,8,512]{2,1,0:T(8,128)S(1)} %collective-permute-done.1.refs_2_, ...), custom_call_target="tpu_custom_call" | custom-call | tf_op jit(solution)/shard_map/pallas_call | solution.py:501
  18.1 14.2 %all_to_all.5.refs_0_ = f32[8,48,128]{2,1,0:T(8,128)S(1)} all-to-all(f32[8,48,128]{2,1,0:T(8,128)S(1)} %get-tuple-element.29), channel_id=1, replica_groups={{0,32,64,96,128,160,192,224},{256,288,320,352,384,416,448,480},{1,33,65..., dimensions={0} | all-to-all | bytes 393216 | tf_op jit(solution)/shard_map/all_to_all | solution.py:547
  32.4 0.1 shard_map.59
  32.5 1.9 %collective-permute-start.4 = (f32[112,128]{1,0:T(8,128)S(1)}, f32[112,128]{1,0:T(8,128)S(1)}, u32[]{:S(2)}, u32[]{:S(2)}) collective-permute-start(f32[112,128]{1,0:T(8,128)S(1)} %get-tuple-element.31), channel_id=1, source_target_pairs={{0,1},{2,3},{1,0},{3,2},{4,5},{6,7},{5,4},{7,6},{8,9},{10,11},{9,8... | collective-permute-start | bytes 172040 | tf_op jit(solution)/shard_map/ppermute | solution.py:512
  34.5 3.5 %collective-permute-start.5 = (f32[112,128]{1,0:T(8,128)S(1)}, f32[112,128]{1,0:T(8,128)S(1)}, u32[]{:S(2)}, u32[]{:S(2)}) collective-permute-start(f32[112,128]{1,0:T(8,128)S(1)} %get-tuple-element.32), channel_id=1, source_target_pairs={{1,2},{2,1},{5,6},{6,5},{9,10},{10,9},{13,14},{14,13},{17,18},{18,... | collective-permute-start | bytes 172040 | tf_op jit(solution)/shard_map/ppermute | solution.py:512
  38.0 0.0 collective-permute-done.4.refs_2_
  38.0 1.5 %collective-permute-done.5.refs_3_ = f32[112,128]{1,0:T(8,128)S(1)} collective-permute-done((f32[112,128]{1,0:T(8,128)S(1)}, f32[112,128]{1,0:T(8,128)S(1)}, u32[]{:S(2)}, u32[]{:S(2)}) %collective-permute-start.5) | collective-permute-done | bytes 57376 | tf_op jit(solution)/shard_map/ppermute | solution.py:512
  39.6 7.6 %collective-permute-start.6 = (f32[400,128]{1,0:T(8,128)S(1)}, f32[400,128]{1,0:T(8,128)S(1)}, u32[]{:S(2)}, u32[]{:S(2)}) collective-permute-start(f32[400,128]{1,0:T(8,128)S(1)} %get-tuple-element.33), channel_id=1, source_target_pairs={{4,8},{12,16},{20,24},{8,4},{16,12},{24,20},{5,9},{13,17},{21,25},... | collective-permute-start | bytes 614408 | tf_op jit(solution)/shard_map/ppermute | solution.py:512
  47.2 1.9 %collective-permute-start.7 = (f32[400,128]{1,0:T(8,128)S(1)}, f32[400,128]{1,0:T(8,128)S(1)}, u32[]{:S(2)}, u32[]{:S(2)}) collective-permute-start(f32[400,128]{1,0:T(8,128)S(1)} %get-tuple-element.34), channel_id=1, source_target_pairs={{0,4},{8,12},{16,20},{24,28},{4,0},{12,8},{20,16},{28,24},{1,5},{9... | collective-permute-start | bytes 614408 | tf_op jit(solution)/shard_map/ppermute | solution.py:512
  49.1 0.6 shard_map.61.refs_6_.refs_5_
  49.7 0.9 %collective-permute-done.6.refs_4_ = f32[400,128]{1,0:T(8,128)S(1)} collective-permute-done((f32[400,128]{1,0:T(8,128)S(1)}, f32[400,128]{1,0:T(8,128)S(1)}, u32[]{:S(2)}, u32[]{:S(2)}) %collective-permute-start.6) | collective-permute-done | bytes 204832 | tf_op jit(solution)/shard_map/ppermute | solution.py:512
  50.6 0.0 collective-permute-done.7.refs_5_
  50.6 1.3 %collective-permute-start.8 = (f32[64,128]{1,0:T(8,128)S(1)}, f32[64,128]{1,0:T(8,128)S(1)}, u32[]{:S(2)}, u32[]{:S(2)}) collective-permute-start(f32[64,128]{1,0:T(8,128)S(1)} %get-tuple-element.35), channel_id=1, source_target_pairs={{0,384},{4,388},{8,392},{12,396},{16,400},{20,404},{24,408},{28,41... | collective-permute-start | bytes 98312 | tf_op jit(solution)/shard_map/ppermute | solution.py:563
  51.9 1.3 %collective-permute-start.9 = (f32[64,128]{1,0:T(8,128)S(1)}, f32[64,128]{1,0:T(8,128)S(1)}, u32[]{:S(2)}, u32[]{:S(2)}) collective-permute-start(f32[64,128]{1,0:T(8,128)S(1)} %get-tuple-element.35), channel_id=1, source_target_pairs={{0,388},{4,384},{8,396},{12,392},{16,404},{20,400},{24,412},{28,40... | collective-permute-start | bytes 98312 | tf_op jit(solution)/shard_map/ppermute | solution.py:563
  53.2 6.0 %collective-permute-done.8.refs_0_ = f32[64,128]{1,0:T(8,128)S(1)} collective-permute-done((f32[64,128]{1,0:T(8,128)S(1)}, f32[64,128]{1,0:T(8,128)S(1)}, u32[]{:S(2)}, u32[]{:S(2)}) %collective-permute-start.8) | collective-permute-done | bytes 32800 | tf_op jit(solution)/shard_map/ppermute | solution.py:563
  59.2 9.2 %collective-permute-start.10 = (f32[64,128]{1,0:T(8,128)S(1)}, f32[64,128]{1,0:T(8,128)S(1)}, u32[]{:S(2)}, u32[]{:S(2)}) collective-permute-start(f32[64,128]{1,0:T(8,128)S(1)} %collective-permute-done.8.refs_0_), channel_id=1, source_target_pairs={{260,264},{268,272},{276,280},{264,260},{272,268},{280,276},{292,2... | collective-permute-start | bytes 98312 | tf_op jit(solution)/shard_map/ppermute | solution.py:517
  68.4 0.3 shard_map.63
  68.7 0.0 collective-permute-done.9.refs_1_
  68.7 1.3 %collective-permute-done.10.refs_2_ = f32[64,128]{1,0:T(8,128)S(1)} collective-permute-done((f32[64,128]{1,0:T(8,128)S(1)}, f32[64,128]{1,0:T(8,128)S(1)}, u32[]{:S(2)}, u32[]{:S(2)}) %collective-permute-start.10) | collective-permute-done | bytes 32800 | tf_op jit(solution)/shard_map/ppermute | solution.py:517
  70.0 3.1 %shard_map.64 = f32[3,64,512]{2,1,0:T(8,128)} custom-call(f32[64,128]{1,0:T(8,128)S(1)} %collective-permute-done.8.refs_0_, f32[64,128]{1,0:T(8,128)S(1)} %collective-permute-done.9.refs_1_, f32[64,128]{1,0:T(8,128)S(1)} %collective-permute-done.10.refs_2_, f32[24,2,48,128]{3,2,1,0:T(8,128)S(1)} %get-tuple-element.36.refs_3_, ...), custom_call_target="tpu_custom_call" | custom-call | tf_op jit(solution)/shard_map/pallas_call | solution.py:501
  (8 shorter events, 0.1 us)
Async XLA Ops:
  0.0 13.0 %copy-start.1 = (s32[64]{0:T(128)S(1)}, s32[64]{0:T(128)}, u32[]{:S(2)}) copy-start(s32[64]{0:T(128)} %param.7) | copy-start | bytes 772
  0.0 13.0 %copy-start.2 = (s32[64]{0:T(128)S(1)}, s32[64]{0:T(128)}, u32[]{:S(2)}) copy-start(s32[64]{0:T(128)} %param.8) | copy-start | bytes 772
  0.0 13.0 %copy-start = (s32[16,64]{1,0:T(8,128)S(1)}, s32[16,64]{1,0:T(8,128)}, u32[]{:S(2)}) copy-start(s32[16,64]{1,0:T(8,128)} %refs_2_.3) | copy-start | bytes 12292
  1.2 5.6 %collective-permute-start = (f32[4,8,512]{2,1,0:T(8,128)S(1)}, f32[4,8,512]{2,1,0:T(8,128)S(1)}, u32[]{:S(2)}, u32[]{:S(2)}) collective-permute-start(f32[4,8,512]{2,1,0:T(8,128)S(1)} %get-tuple-element.23), channel_id=1, source_target_pairs={{4,8},{12,16},{20,24},{8,4},{16,12},{24,20},{5,9},{13,17},{21,25},... | collective-permute-start | bytes 196616 | tf_op jit(solution)/shard_map/ppermute | solution.py:512
  4.9 3.1 %collective-permute-start.1 = (f32[4,8,512]{2,1,0:T(8,128)S(1)}, f32[4,8,512]{2,1,0:T(8,128)S(1)}, u32[]{:S(2)}, u32[]{:S(2)}) collective-permute-start(f32[4,8,512]{2,1,0:T(8,128)S(1)} %get-tuple-element.24), channel_id=1, source_target_pairs={{0,4},{8,12},{16,20},{24,28},{4,0},{12,8},{20,16},{28,24},{1,5},{9... | collective-permute-start | bytes 196616 | tf_op jit(solution)/shard_map/ppermute | solution.py:512
  8.2 5.4 %collective-permute-start.2 = (f32[80,128]{1,0:T(8,128)S(1)}, f32[80,128]{1,0:T(8,128)S(1)}, u32[]{:S(2)}, u32[]{:S(2)}) collective-permute-start(f32[80,128]{1,0:T(8,128)S(1)} %get-tuple-element.25), channel_id=1, source_target_pairs={{0,1},{2,3},{1,0},{3,2},{4,5},{6,7},{5,4},{7,6},{8,9},{10,11},{9,8... | collective-permute-start | bytes 122888 | tf_op jit(solution)/shard_map/ppermute | solution.py:512
  11.1 4.7 %collective-permute-start.3 = (f32[80,128]{1,0:T(8,128)S(1)}, f32[80,128]{1,0:T(8,128)S(1)}, u32[]{:S(2)}, u32[]{:S(2)}) collective-permute-start(f32[80,128]{1,0:T(8,128)S(1)} %get-tuple-element.26), channel_id=1, source_target_pairs={{1,2},{2,1},{5,6},{6,5},{9,10},{10,9},{13,14},{14,13},{17,18},{18,... | collective-permute-start | bytes 122888 | tf_op jit(solution)/shard_map/ppermute | solution.py:512
  32.5 5.5 %collective-permute-start.4 = (f32[112,128]{1,0:T(8,128)S(1)}, f32[112,128]{1,0:T(8,128)S(1)}, u32[]{:S(2)}, u32[]{:S(2)}) collective-permute-start(f32[112,128]{1,0:T(8,128)S(1)} %get-tuple-element.31), channel_id=1, source_target_pairs={{0,1},{2,3},{1,0},{3,2},{4,5},{6,7},{5,4},{7,6},{8,9},{10,11},{9,8... | collective-permute-start | bytes 172040 | tf_op jit(solution)/shard_map/ppermute | solution.py:512
  34.5 5.1 %collective-permute-start.5 = (f32[112,128]{1,0:T(8,128)S(1)}, f32[112,128]{1,0:T(8,128)S(1)}, u32[]{:S(2)}, u32[]{:S(2)}) collective-permute-start(f32[112,128]{1,0:T(8,128)S(1)} %get-tuple-element.32), channel_id=1, source_target_pairs={{1,2},{2,1},{5,6},{6,5},{9,10},{10,9},{13,14},{14,13},{17,18},{18,... | collective-permute-start | bytes 172040 | tf_op jit(solution)/shard_map/ppermute | solution.py:512
  39.6 11.0 %collective-permute-start.6 = (f32[400,128]{1,0:T(8,128)S(1)}, f32[400,128]{1,0:T(8,128)S(1)}, u32[]{:S(2)}, u32[]{:S(2)}) collective-permute-start(f32[400,128]{1,0:T(8,128)S(1)} %get-tuple-element.33), channel_id=1, source_target_pairs={{4,8},{12,16},{20,24},{8,4},{16,12},{24,20},{5,9},{13,17},{21,25},... | collective-permute-start | bytes 614408 | tf_op jit(solution)/shard_map/ppermute | solution.py:512
  47.2 3.4 %collective-permute-start.7 = (f32[400,128]{1,0:T(8,128)S(1)}, f32[400,128]{1,0:T(8,128)S(1)}, u32[]{:S(2)}, u32[]{:S(2)}) collective-permute-start(f32[400,128]{1,0:T(8,128)S(1)} %get-tuple-element.34), channel_id=1, source_target_pairs={{0,4},{8,12},{16,20},{24,28},{4,0},{12,8},{20,16},{28,24},{1,5},{9... | collective-permute-start | bytes 614408 | tf_op jit(solution)/shard_map/ppermute | solution.py:512
  50.6 8.6 %collective-permute-start.8 = (f32[64,128]{1,0:T(8,128)S(1)}, f32[64,128]{1,0:T(8,128)S(1)}, u32[]{:S(2)}, u32[]{:S(2)}) collective-permute-start(f32[64,128]{1,0:T(8,128)S(1)} %get-tuple-element.35), channel_id=1, source_target_pairs={{0,384},{4,388},{8,392},{12,396},{16,400},{20,404},{24,408},{28,41... | collective-permute-start | bytes 98312 | tf_op jit(solution)/shard_map/ppermute | solution.py:563
  51.9 16.8 %collective-permute-start.9 = (f32[64,128]{1,0:T(8,128)S(1)}, f32[64,128]{1,0:T(8,128)S(1)}, u32[]{:S(2)}, u32[]{:S(2)}) collective-permute-start(f32[64,128]{1,0:T(8,128)S(1)} %get-tuple-element.35), channel_id=1, source_target_pairs={{0,388},{4,384},{8,396},{12,392},{16,404},{20,400},{24,412},{28,40... | collective-permute-start | bytes 98312 | tf_op jit(solution)/shard_map/ppermute | solution.py:563
  59.2 10.8 %collective-permute-start.10 = (f32[64,128]{1,0:T(8,128)S(1)}, f32[64,128]{1,0:T(8,128)S(1)}, u32[]{:S(2)}, u32[]{:S(2)}) collective-permute-start(f32[64,128]{1,0:T(8,128)S(1)} %collective-permute-done.8.refs_0_), channel_id=1, source_target_pairs={{260,264},{268,272},{276,280},{264,260},{272,268},{280,276},{292,2... | collective-permute-start | bytes 98312 | tf_op jit(solution)/shard_map/ppermute | solution.py:517

commit v10 on v9

--- a/solution.py
+++ b/solution.py
@@ -155,7 +155,7 @@
         send_b[f] = jnp.where(even, first, last)
 
 
-def side_kernel(at, own, got_b, got_a, send_a, send_b):
+def side_kernel(at, own, got_b, got_a, send_a, send_b, left_all, right_all):
     even_x = lax.rem(at[1], 2) == 0
     even_y = lax.rem(at[2], 2) == 0
     for r0, count in ((0, 8), (8, 64), (72, 8)):
@@ -172,8 +172,17 @@
             mine = (lane >= 8 * f) & (lane < 8 * f + 8)
             left = jnp.where(mine, rolled(a, 8 * f), left)
             right = jnp.where(mine, rolled(b, 8 * f + 8), right)
-        send_a[r0 : r0 + count, :] = jnp.where(even_y, right, left)
-        send_b[r0 : r0 + count, :] = jnp.where(even_y, left, right)
+        left_all[r0 : r0 + count, :] = left
+        right_all[r0 : r0 + count, :] = right
+    left_all[80:96, :] = jnp.zeros((16, 128), F32)
+    right_all[80:96, :] = jnp.zeros((16, 128), F32)
+    lane = lanes((24, 128))
+    left, right = left_all[0:24, :], right_all[0:24, :]
+    for k in range(1, 4):
+        left = jnp.where(lane // 32 == k, rolled(left_all[24 * k : 24 * k + 24, :], 32 * k), left)
+        right = jnp.where(lane // 32 == k, rolled(right_all[24 * k : 24 * k + 24, :], 32 * k), right)
+    send_a[...] = jnp.where(even_y, right, left)
+    send_b[...] = jnp.where(even_y, left, right)
 
 
 def fine_cols(sy, c, shape):
@@ -238,7 +247,6 @@
     fine_edge, rough_edge = ((15, 80), outside, side_mask), ((9, 26), outside, side_mask)
     after_all = jnp.where(even_y, cols_a[...], cols_b[...])
     before_all = jnp.where(even_y, cols_b[...], cols_a[...])
-    lane = lanes((80, 128))
     for f in range(4):
         for c in range(5):
             if c < 4:
@@ -246,8 +254,14 @@
                 a, b = rows_a[f, :, cut], rows_b[f, :, cut]
                 pieces = [(8, 8, jnp.where(even_x, b, a)), (16, 64, own[f, :, cut]), (80, 8, jnp.where(even_x, a, b))]
             else:
-                after, before = rolled(after_all, -8 * f), rolled(before_all, 120 - 8 * f)
-                pieces = [(8, 80, jnp.where(lane < 8, after, jnp.where(lane >= 120, before, 0.0)))]
+                pieces = []
+                for k in range(4):
+                    count = 24 if k < 3 else 8
+                    after = rolled(after_all[0:count], -32 * k - 8 * f)
+                    before = rolled(before_all[0:count], 120 - 32 * k - 8 * f)
+                    lane = lanes((count, 128))
+                    value = jnp.where(lane < 8, after, jnp.where(lane >= 120, before, 0.0))
+                    pieces.append((8 + 24 * k, count, value))
             for r, count, value in pieces:
                 if f < 3:
                     one[f, c, r : r + count, :] = value * FINE_SCALE[f]
@@ -532,7 +546,7 @@
     send_b, send_a = call(edge_kernel, (own,), [(4, 8, COLS)] * 2)
     rows_b = swap(send_b, "sx", x_b)
     rows_a = swap(send_a, "sx", x_a)
-    send_a, send_b = call(side_kernel, (own, rows_b, rows_a), [(80, 128)] * 2)
+    send_a, send_b = call(side_kernel, (own, rows_b, rows_a), [(24, 128)] * 2, [(96, 128)] * 2)
     cols_a = swap(send_a, "sy", y_a)
     cols_b = swap(send_b, "sy", y_b)
     push, own_push = call(

time: 73.5 us -> 73.3 us (level)
  no operation moved by 1% of the time
where the time goes in v10:
time: 73.3 us; the launch traced here: 72.9 us
  starting transfers between devices  37.2 us (51%)
  blocking collectives  14.2 us (19%)
  waiting for transfers between devices  12.8 us (17%)
  Pallas kernels  7.29 us (10%)
  other arithmetic  1.13 us (2%)
    ppermute x8, starting transfers between devices, swap(): lax.ppermute(x, axis, [(a, b) for a, b in pairs] + [(b, a) for a, b in pa...  25.4 us
    all_to_all x1, blocking collectives, on_device(): held = lax.all_to_all(sent, 'cuts', 0, 0, axis_index_groups=halves)  14.2 us
    ppermute x1, starting transfers between devices, swap_half(): lax.ppermute(x, ('cuts', 'sx'), [(n * count + a, n * count + b) for n in...  9.22 us
    pallas_call x10, Pallas kernels, call(): pl.pallas_call(placed, out_shape=shapes, in_specs=[VMEM] * near + [HBM] *...  7.29 us
    ppermute x2, waiting for transfers between devices, on_device(): lax.ppermute(state, ('cuts', 'sx'), [(m * count_x + i, n * count_x + (i ^...  5.97 us
    ppermute x8, waiting for transfers between devices, swap(): lax.ppermute(x, axis, [(a, b) for a, b in pairs] + [(b, a) for a, b in pa...  5.55 us
    ppermute x2, starting transfers between devices, on_device(): lax.ppermute(state, ('cuts', 'sx'), [(m * count_x + i, n * count_x + (i ^...  2.57 us
  transfers between devices with their start and end apart: 11, of which 6 were waited for; matrix products, arithmetic and copies ran while one was open for 0% of the time, Pallas kernels for 2%

profile of v10, /device:TPU:401, one launch (start us, length us, event | category | flops | bytes accessed | tf_op | source)
XLA Modules:
  0.0 72.9 jit_solution(1584343979499556110)
XLA Ops:
  0.0 1.1 %pad_maximum_fusion.refs_0_ = f32[4,64,512]{2,1,0:T(8,128)S(1)} fusion(f32[1,64,512]{2,1,0:T(8,128)} %bitcast.10, f32[3,64,512]{2,1,0:T(8,128)} %bitcast.9), kind=kLoop, calls=%fused_computation | loop fusion | flops 131072 | bytes 1048576 | tf_op jit(solution)/shard_map/concatenate | solution.py:545
  1.2 3.7 %collective-permute-start = (f32[4,8,512]{2,1,0:T(8,128)S(1)}, f32[4,8,512]{2,1,0:T(8,128)S(1)}, u32[]{:S(2)}, u32[]{:S(2)}) collective-permute-start(f32[4,8,512]{2,1,0:T(8,128)S(1)} %get-tuple-element.23), channel_id=1, source_target_pairs={{4,8},{12,16},{20,24},{8,4},{16,12},{24,20},{5,9},{13,17},{21,25},... | collective-permute-start | bytes 196616 | tf_op jit(solution)/shard_map/ppermute | solution.py:526
  4.9 1.9 %collective-permute-start.1 = (f32[4,8,512]{2,1,0:T(8,128)S(1)}, f32[4,8,512]{2,1,0:T(8,128)S(1)}, u32[]{:S(2)}, u32[]{:S(2)}) collective-permute-start(f32[4,8,512]{2,1,0:T(8,128)S(1)} %get-tuple-element.24), channel_id=1, source_target_pairs={{0,4},{8,12},{16,20},{24,28},{4,0},{12,8},{20,16},{28,24},{1,5},{9... | collective-permute-start | bytes 196616 | tf_op jit(solution)/shard_map/ppermute | solution.py:526
  6.8 0.0 collective-permute-done.refs_1_
  6.8 1.2 %collective-permute-done.1.refs_2_ = f32[4,8,512]{2,1,0:T(8,128)S(1)} collective-permute-done((f32[4,8,512]{2,1,0:T(8,128)S(1)}, f32[4,8,512]{2,1,0:T(8,128)S(1)}, u32[]{:S(2)}, u32[]{:S(2)}) %collective-permute-start.1) | collective-permute-done | bytes 65568 | tf_op jit(solution)/shard_map/ppermute | solution.py:526
  8.0 0.2 shard_map.56
  8.2 2.9 %collective-permute-start.2 = (f32[24,128]{1,0:T(8,128)S(1)}, f32[24,128]{1,0:T(8,128)S(1)}, u32[]{:S(2)}, u32[]{:S(2)}) collective-permute-start(f32[24,128]{1,0:T(8,128)S(1)} %get-tuple-element.25), channel_id=1, source_target_pairs={{0,1},{2,3},{1,0},{3,2},{4,5},{6,7},{5,4},{7,6},{8,9},{10,11},{9,8... | collective-permute-start | bytes 36872 | tf_op jit(solution)/shard_map/ppermute | solution.py:526
  11.1 1.9 %collective-permute-start.3 = (f32[24,128]{1,0:T(8,128)S(1)}, f32[24,128]{1,0:T(8,128)S(1)}, u32[]{:S(2)}, u32[]{:S(2)}) collective-permute-start(f32[24,128]{1,0:T(8,128)S(1)} %get-tuple-element.26), channel_id=1, source_target_pairs={{1,2},{2,1},{5,6},{6,5},{9,10},{10,9},{13,14},{14,13},{17,18},{18,... | collective-permute-start | bytes 36872 | tf_op jit(solution)/shard_map/ppermute | solution.py:526
  13.1 0.0 copy-done.1
  13.1 0.5 shard_map.57
  13.6 0.0 collective-permute-done.2.refs_3_
  13.7 1.9 %collective-permute-done.3.refs_4_ = f32[24,128]{1,0:T(8,128)S(1)} collective-permute-done((f32[24,128]{1,0:T(8,128)S(1)}, f32[24,128]{1,0:T(8,128)S(1)}, u32[]{:S(2)}, u32[]{:S(2)}) %collective-permute-start.3) | collective-permute-done | bytes 12320 | tf_op jit(solution)/shard_map/ppermute | solution.py:526
  15.6 2.3 %shard_map.58 = (f32[3,64,512]{2,1,0:T(8,128)S(1)}, f32[48,128]{1,0:T(8,128)S(1)}, f32[8,48,128]{2,1,0:T(8,128)S(1)}, f32[16,128]{1,0:T(8,128)S(1)}) custom-call(f32[4,64,512]{2,1,0:T(8,128)S(1)} %pad_maximum_fusion.refs_0_, f32[4,8,512]{2,1,0:T(8,128)S(1)} %collective-permute-done.refs_1_, f32[4,8,512]{2,1,0:T(8,128)S(1)} %collective-permute-done.1.refs_2_, ...), custom_call_target="tpu_custom_call" | custom-call | tf_op jit(solution)/shard_map/pallas_call | solution.py:515
  17.9 14.2 %all_to_all.5.refs_0_ = f32[8,48,128]{2,1,0:T(8,128)S(1)} all-to-all(f32[8,48,128]{2,1,0:T(8,128)S(1)} %get-tuple-element.29), channel_id=1, replica_groups={{0,32,64,96,128,160,192,224},{256,288,320,352,384,416,448,480},{1,33,65..., dimensions={0} | all-to-all | bytes 393216 | tf_op jit(solution)/shard_map/all_to_all | solution.py:561
  32.1 0.1 shard_map.59
  32.3 1.9 %collective-permute-start.4 = (f32[112,128]{1,0:T(8,128)S(1)}, f32[112,128]{1,0:T(8,128)S(1)}, u32[]{:S(2)}, u32[]{:S(2)}) collective-permute-start(f32[112,128]{1,0:T(8,128)S(1)} %get-tuple-element.31), channel_id=1, source_target_pairs={{0,1},{2,3},{1,0},{3,2},{4,5},{6,7},{5,4},{7,6},{8,9},{10,11},{9,8... | collective-permute-start | bytes 172040 | tf_op jit(solution)/shard_map/ppermute | solution.py:526
  34.2 3.5 %collective-permute-start.5 = (f32[112,128]{1,0:T(8,128)S(1)}, f32[112,128]{1,0:T(8,128)S(1)}, u32[]{:S(2)}, u32[]{:S(2)}) collective-permute-start(f32[112,128]{1,0:T(8,128)S(1)} %get-tuple-element.32), channel_id=1, source_target_pairs={{1,2},{2,1},{5,6},{6,5},{9,10},{10,9},{13,14},{14,13},{17,18},{18,... | collective-permute-start | bytes 172040 | tf_op jit(solution)/shard_map/ppermute | solution.py:526
  37.8 0.0 collective-permute-done.4.refs_2_
  37.8 1.5 %collective-permute-done.5.refs_3_ = f32[112,128]{1,0:T(8,128)S(1)} collective-permute-done((f32[112,128]{1,0:T(8,128)S(1)}, f32[112,128]{1,0:T(8,128)S(1)}, u32[]{:S(2)}, u32[]{:S(2)}) %collective-permute-start.5) | collective-permute-done | bytes 57376 | tf_op jit(solution)/shard_map/ppermute | solution.py:526
  39.3 7.6 %collective-permute-start.6 = (f32[400,128]{1,0:T(8,128)S(1)}, f32[400,128]{1,0:T(8,128)S(1)}, u32[]{:S(2)}, u32[]{:S(2)}) collective-permute-start(f32[400,128]{1,0:T(8,128)S(1)} %get-tuple-element.33), channel_id=1, source_target_pairs={{4,8},{12,16},{20,24},{8,4},{16,12},{24,20},{5,9},{13,17},{21,25},... | collective-permute-start | bytes 614408 | tf_op jit(solution)/shard_map/ppermute | solution.py:526
  46.9 1.9 %collective-permute-start.7 = (f32[400,128]{1,0:T(8,128)S(1)}, f32[400,128]{1,0:T(8,128)S(1)}, u32[]{:S(2)}, u32[]{:S(2)}) collective-permute-start(f32[400,128]{1,0:T(8,128)S(1)} %get-tuple-element.34), channel_id=1, source_target_pairs={{0,4},{8,12},{16,20},{24,28},{4,0},{12,8},{20,16},{28,24},{1,5},{9... | collective-permute-start | bytes 614408 | tf_op jit(solution)/shard_map/ppermute | solution.py:526
  48.9 0.6 shard_map.61.refs_6_.refs_5_
  49.5 0.9 %collective-permute-done.6.refs_4_ = f32[400,128]{1,0:T(8,128)S(1)} collective-permute-done((f32[400,128]{1,0:T(8,128)S(1)}, f32[400,128]{1,0:T(8,128)S(1)}, u32[]{:S(2)}, u32[]{:S(2)}) %collective-permute-start.6) | collective-permute-done | bytes 204832 | tf_op jit(solution)/shard_map/ppermute | solution.py:526
  50.4 0.0 collective-permute-done.7.refs_5_
  50.4 1.3 %collective-permute-start.8 = (f32[64,128]{1,0:T(8,128)S(1)}, f32[64,128]{1,0:T(8,128)S(1)}, u32[]{:S(2)}, u32[]{:S(2)}) collective-permute-start(f32[64,128]{1,0:T(8,128)S(1)} %get-tuple-element.35), channel_id=1, source_target_pairs={{0,384},{4,388},{8,392},{12,396},{16,400},{20,404},{24,408},{28,41... | collective-permute-start | bytes 98312 | tf_op jit(solution)/shard_map/ppermute | solution.py:577
  51.7 1.3 %collective-permute-start.9 = (f32[64,128]{1,0:T(8,128)S(1)}, f32[64,128]{1,0:T(8,128)S(1)}, u32[]{:S(2)}, u32[]{:S(2)}) collective-permute-start(f32[64,128]{1,0:T(8,128)S(1)} %get-tuple-element.35), channel_id=1, source_target_pairs={{0,388},{4,384},{8,396},{12,392},{16,404},{20,400},{24,412},{28,40... | collective-permute-start | bytes 98312 | tf_op jit(solution)/shard_map/ppermute | solution.py:577
  53.0 6.0 %collective-permute-done.8.refs_0_ = f32[64,128]{1,0:T(8,128)S(1)} collective-permute-done((f32[64,128]{1,0:T(8,128)S(1)}, f32[64,128]{1,0:T(8,128)S(1)}, u32[]{:S(2)}, u32[]{:S(2)}) %collective-permute-start.8) | collective-permute-done | bytes 32800 | tf_op jit(solution)/shard_map/ppermute | solution.py:577
  58.9 9.2 %collective-permute-start.10 = (f32[64,128]{1,0:T(8,128)S(1)}, f32[64,128]{1,0:T(8,128)S(1)}, u32[]{:S(2)}, u32[]{:S(2)}) collective-permute-start(f32[64,128]{1,0:T(8,128)S(1)} %collective-permute-done.8.refs_0_), channel_id=1, source_target_pairs={{260,264},{268,272},{276,280},{264,260},{272,268},{280,276},{292,2... | collective-permute-start | bytes 98312 | tf_op jit(solution)/shard_map/ppermute | solution.py:531
  68.2 0.3 shard_map.63
  68.4 0.0 collective-permute-done.9.refs_1_
  68.4 1.3 %collective-permute-done.10.refs_2_ = f32[64,128]{1,0:T(8,128)S(1)} collective-permute-done((f32[64,128]{1,0:T(8,128)S(1)}, f32[64,128]{1,0:T(8,128)S(1)}, u32[]{:S(2)}, u32[]{:S(2)}) %collective-permute-start.10) | collective-permute-done | bytes 32800 | tf_op jit(solution)/shard_map/ppermute | solution.py:531
  69.7 3.1 %shard_map.64 = f32[3,64,512]{2,1,0:T(8,128)} custom-call(f32[64,128]{1,0:T(8,128)S(1)} %collective-permute-done.8.refs_0_, f32[64,128]{1,0:T(8,128)S(1)} %collective-permute-done.9.refs_1_, f32[64,128]{1,0:T(8,128)S(1)} %collective-permute-done.10.refs_2_, f32[24,2,48,128]{3,2,1,0:T(8,128)S(1)} %get-tuple-element.36.refs_3_, ...), custom_call_target="tpu_custom_call" | custom-call | tf_op jit(solution)/shard_map/pallas_call | solution.py:515
  (8 shorter events, 0.1 us)
Async XLA Ops:
  0.0 13.1 %copy-start.1 = (s32[64]{0:T(128)S(1)}, s32[64]{0:T(128)}, u32[]{:S(2)}) copy-start(s32[64]{0:T(128)} %param.7) | copy-start | bytes 772
  0.0 13.1 %copy-start.2 = (s32[64]{0:T(128)S(1)}, s32[64]{0:T(128)}, u32[]{:S(2)}) copy-start(s32[64]{0:T(128)} %param.8) | copy-start | bytes 772
  0.0 13.1 %copy-start = (s32[16,64]{1,0:T(8,128)S(1)}, s32[16,64]{1,0:T(8,128)}, u32[]{:S(2)}) copy-start(s32[16,64]{1,0:T(8,128)} %refs_2_.3) | copy-start | bytes 12292
  1.2 5.6 %collective-permute-start = (f32[4,8,512]{2,1,0:T(8,128)S(1)}, f32[4,8,512]{2,1,0:T(8,128)S(1)}, u32[]{:S(2)}, u32[]{:S(2)}) collective-permute-start(f32[4,8,512]{2,1,0:T(8,128)S(1)} %get-tuple-element.23), channel_id=1, source_target_pairs={{4,8},{12,16},{20,24},{8,4},{16,12},{24,20},{5,9},{13,17},{21,25},... | collective-permute-start | bytes 196616 | tf_op jit(solution)/shard_map/ppermute | solution.py:526
  4.9 3.1 %collective-permute-start.1 = (f32[4,8,512]{2,1,0:T(8,128)S(1)}, f32[4,8,512]{2,1,0:T(8,128)S(1)}, u32[]{:S(2)}, u32[]{:S(2)}) collective-permute-start(f32[4,8,512]{2,1,0:T(8,128)S(1)} %get-tuple-element.24), channel_id=1, source_target_pairs={{0,4},{8,12},{16,20},{24,28},{4,0},{12,8},{20,16},{28,24},{1,5},{9... | collective-permute-start | bytes 196616 | tf_op jit(solution)/shard_map/ppermute | solution.py:526
  8.2 5.4 %collective-permute-start.2 = (f32[24,128]{1,0:T(8,128)S(1)}, f32[24,128]{1,0:T(8,128)S(1)}, u32[]{:S(2)}, u32[]{:S(2)}) collective-permute-start(f32[24,128]{1,0:T(8,128)S(1)} %get-tuple-element.25), channel_id=1, source_target_pairs={{0,1},{2,3},{1,0},{3,2},{4,5},{6,7},{5,4},{7,6},{8,9},{10,11},{9,8... | collective-permute-start | bytes 36872 | tf_op jit(solution)/shard_map/ppermute | solution.py:526
  11.1 4.4 %collective-permute-start.3 = (f32[24,128]{1,0:T(8,128)S(1)}, f32[24,128]{1,0:T(8,128)S(1)}, u32[]{:S(2)}, u32[]{:S(2)}) collective-permute-start(f32[24,128]{1,0:T(8,128)S(1)} %get-tuple-element.26), channel_id=1, source_target_pairs={{1,2},{2,1},{5,6},{6,5},{9,10},{10,9},{13,14},{14,13},{17,18},{18,... | collective-permute-start | bytes 36872 | tf_op jit(solution)/shard_map/ppermute | solution.py:526
  32.3 5.5 %collective-permute-start.4 = (f32[112,128]{1,0:T(8,128)S(1)}, f32[112,128]{1,0:T(8,128)S(1)}, u32[]{:S(2)}, u32[]{:S(2)}) collective-permute-start(f32[112,128]{1,0:T(8,128)S(1)} %get-tuple-element.31), channel_id=1, source_target_pairs={{0,1},{2,3},{1,0},{3,2},{4,5},{6,7},{5,4},{7,6},{8,9},{10,11},{9,8... | collective-permute-start | bytes 172040 | tf_op jit(solution)/shard_map/ppermute | solution.py:526
  34.2 5.1 %collective-permute-start.5 = (f32[112,128]{1,0:T(8,128)S(1)}, f32[112,128]{1,0:T(8,128)S(1)}, u32[]{:S(2)}, u32[]{:S(2)}) collective-permute-start(f32[112,128]{1,0:T(8,128)S(1)} %get-tuple-element.32), channel_id=1, source_target_pairs={{1,2},{2,1},{5,6},{6,5},{9,10},{10,9},{13,14},{14,13},{17,18},{18,... | collective-permute-start | bytes 172040 | tf_op jit(solution)/shard_map/ppermute | solution.py:526
  39.3 11.0 %collective-permute-start.6 = (f32[400,128]{1,0:T(8,128)S(1)}, f32[400,128]{1,0:T(8,128)S(1)}, u32[]{:S(2)}, u32[]{:S(2)}) collective-permute-start(f32[400,128]{1,0:T(8,128)S(1)} %get-tuple-element.33), channel_id=1, source_target_pairs={{4,8},{12,16},{20,24},{8,4},{16,12},{24,20},{5,9},{13,17},{21,25},... | collective-permute-start | bytes 614408 | tf_op jit(solution)/shard_map/ppermute | solution.py:526
  46.9 3.4 %collective-permute-start.7 = (f32[400,128]{1,0:T(8,128)S(1)}, f32[400,128]{1,0:T(8,128)S(1)}, u32[]{:S(2)}, u32[]{:S(2)}) collective-permute-start(f32[400,128]{1,0:T(8,128)S(1)} %get-tuple-element.34), channel_id=1, source_target_pairs={{0,4},{8,12},{16,20},{24,28},{4,0},{12,8},{20,16},{28,24},{1,5},{9... | collective-permute-start | bytes 614408 | tf_op jit(solution)/shard_map/ppermute | solution.py:526
  50.4 8.6 %collective-permute-start.8 = (f32[64,128]{1,0:T(8,128)S(1)}, f32[64,128]{1,0:T(8,128)S(1)}, u32[]{:S(2)}, u32[]{:S(2)}) collective-permute-start(f32[64,128]{1,0:T(8,128)S(1)} %get-tuple-element.35), channel_id=1, source_target_pairs={{0,384},{4,388},{8,392},{12,396},{16,400},{20,404},{24,408},{28,41... | collective-permute-start | bytes 98312 | tf_op jit(solution)/shard_map/ppermute | solution.py:577
  51.7 16.8 %collective-permute-start.9 = (f32[64,128]{1,0:T(8,128)S(1)}, f32[64,128]{1,0:T(8,128)S(1)}, u32[]{:S(2)}, u32[]{:S(2)}) collective-permute-start(f32[64,128]{1,0:T(8,128)S(1)} %get-tuple-element.35), channel_id=1, source_target_pairs={{0,388},{4,384},{8,396},{12,392},{16,404},{20,400},{24,412},{28,40... | collective-permute-start | bytes 98312 | tf_op jit(solution)/shard_map/ppermute | solution.py:577
  58.9 10.8 %collective-permute-start.10 = (f32[64,128]{1,0:T(8,128)S(1)}, f32[64,128]{1,0:T(8,128)S(1)}, u32[]{:S(2)}, u32[]{:S(2)}) collective-permute-start(f32[64,128]{1,0:T(8,128)S(1)} %collective-permute-done.8.refs_0_), channel_id=1, source_target_pairs={{260,264},{268,272},{276,280},{264,260},{272,268},{280,276},{292,2... | collective-permute-start | bytes 98312 | tf_op jit(solution)/shard_map/ppermute | solution.py:531
